TPU v7x, 256 devices: a whole 4x4x8 slice. The times are simulated.
256 devices in a mesh: dp: 4 (over y), gx: 4 (over x), gy: 16 (over z, core).
Axes of the slice: x: 4, y: 4, z: 8, core: 2. Of those that a mesh axis runs over, the one named last changes fastest.
Arguments:
- field: bfloat16 [4, 64, 32, 20, 2048], P('dp', 'gx', 'gy'), may hold values from -6 to 6
- cotangent: bfloat16 [4, 64, 32, 20, 2048], P('dp', 'gx', 'gy'), may hold values from -6 to 6
- spectral_weight: bfloat16 [24, 24, 20, 20, 192], P(None, None, None, None, ('gx', 'gy')), may hold values from -2.5 to 2.5
- bypass_weight: bfloat16 [20, 20], replicated, may hold values from -1.25 to 1.25
Outputs:
- grad_field: bfloat16 [4, 64, 32, 20, 2048], P('dp', 'gx', 'gy')
- grad_spectral: float32 [24, 24, 20, 20, 192], P(None, None, None, None, ('gx', 'gy'))
- grad_bypass: float32 [20, 20], replicated
All inputs are finite; a program needn't handle non-finite values.
Results may differ from a plain program's by a relative error of at most 0.034.
Values may be sent and summed in bfloat16 or wider, within the bound.
No kernel may reach another device: no remote copies, remote signals or barrier semaphores. Data moves between devices by JAX's collectives and lax.ppermute only.
A program may use at most 192 MiB of HBM per device.

v0:
```python
import math

import jax
import jax.numpy as jnp
from jax import lax
from jax.sharding import PartitionSpec as P

MX = 12
MY = 12
MZ = 12
MT = 4
NZ = 128
NT = 16


def basis(length, kept):
    places = lax.iota(jnp.int32, length)
    orders = lax.iota(jnp.int32, kept)
    cos_arg = places[:, None] * orders[None, :] % length
    sin_arg = places[:, None] * (orders[None, :] + 1) % length
    step_angle = 2.0 * math.pi / length
    scale = math.sqrt(2.0 / length)
    cos_part = jnp.cos(cos_arg.astype(jnp.float32) * step_angle)
    sin_part = jnp.sin(sin_arg.astype(jnp.float32) * step_angle)
    return jnp.concatenate([cos_part, sin_part], axis=1) * scale


def mode_dot(form, data, table):
    upper = table.astype(jnp.bfloat16)
    lower = (table - upper.astype(jnp.float32)).astype(jnp.bfloat16)
    first = jnp.einsum(form, data, upper, preferred_element_type=jnp.float32)
    return first + jnp.einsum(form, data, lower, preferred_element_type=jnp.float32)


def body(field, cotangent, spectral_weight, bypass_weight):
    cells_x = field.shape[1]
    cells_y = field.shape[2]
    channels = field.shape[3]
    parts_x = lax.axis_size("gx")
    parts_y = lax.axis_size("gy")
    table_x = basis(cells_x * parts_x, MX)
    table_y = basis(cells_y * parts_y, MY)
    table_z = basis(NZ, MZ)
    table_t = basis(NT, MT)
    modes_zt = 4 * MZ * MT
    table_zt = (table_z[:, None, :, None] * table_t[None, :, None, :]).reshape(NZ * NT, modes_zt)

    def analyze(cells):
        matrix = cells.reshape(-1, NZ * NT)
        coeff = mode_dot("rp,pq->rq", matrix, table_zt).astype(jnp.bfloat16)
        coeff = coeff.reshape(cells_x, cells_y, channels, modes_zt)
        along_x = lax.all_to_all(coeff, "gx", split_axis=3, concat_axis=0, tiled=True)
        partial_x = mode_dot("xycq,xk->kycq", along_x, table_x).astype(jnp.bfloat16)
        along_y = lax.all_to_all(partial_x, "gy", split_axis=3, concat_axis=1, tiled=True)
        return mode_dot("kycq,yl->klcq", along_y, table_y).astype(jnp.bfloat16)

    def synthesize(spectrum):
        partial_y = mode_dot("klcq,yl->kycq", spectrum, table_y).astype(jnp.bfloat16)
        returned = lax.all_to_all(partial_y, "gy", split_axis=1, concat_axis=3, tiled=True)
        partial_x = mode_dot("kycq,xk->xycq", returned, table_x).astype(jnp.bfloat16)
        coeff = lax.all_to_all(partial_x, "gx", split_axis=0, concat_axis=3, tiled=True)
        matrix = coeff.reshape(-1, modes_zt)
        values = mode_dot("rq,pq->rp", matrix, table_zt)
        return values.reshape(1, cells_x, cells_y, channels, NZ * NT)

    spectrum = analyze(field)
    mixed = jnp.einsum(
        "klcq,klcoq->kloq", spectrum, spectral_weight, preferred_element_type=jnp.float32
    ).astype(jnp.bfloat16)
    spatial = synthesize(mixed)
    bypass = jnp.einsum("bxyip,io->bxyop", field, bypass_weight, preferred_element_type=jnp.float32)
    pre = spatial + bypass
    unused, pullback = jax.vjp(jax.nn.gelu, pre)
    (slope,) = pullback(cotangent.astype(jnp.float32))
    upstream = slope.astype(jnp.bfloat16)
    bypass_term = jnp.einsum("bxyip,bxyop->io", field, upstream, preferred_element_type=jnp.float32)
    grad_bypass = lax.psum(bypass_term, ("dp", "gx", "gy"))
    spectrum_up = analyze(upstream)
    local_grad = jnp.einsum(
        "klcq,kloq->klcoq", spectrum, spectrum_up, preferred_element_type=jnp.float32
    )
    grad_spectral = lax.psum(local_grad.astype(jnp.bfloat16), "dp").astype(jnp.float32)
    spectrum_back = jnp.einsum(
        "kloq,klcoq->klcq", spectrum_up, spectral_weight, preferred_element_type=jnp.float32
    ).astype(jnp.bfloat16)
    through_bypass = jnp.einsum(
        "bxyop,io->bxyip", upstream, bypass_weight, preferred_element_type=jnp.float32
    )
    grad_field = (synthesize(spectrum_back) + through_bypass).astype(jnp.bfloat16)
    return (grad_field, grad_spectral, grad_bypass)


def solution(mesh):
    in_specs = (
        P("dp", "gx", "gy", None, None),
        P("dp", "gx", "gy", None, None),
        P(None, None, None, None, ("gx", "gy")),
        P(),
    )
    out_specs = (P("dp", "gx", "gy", None, None), P(None, None, None, None, ("gx", "gy")), P())
    return jax.shard_map(body, mesh=mesh, in_specs=in_specs, out_specs=out_specs, check_vma=False)
```

profile of v0, /device:TPU:1, one launch (start us, length us, event | category | flops | bytes accessed | tf_op | source)
XLA Modules:
  0.0 493.5 jit_solution(16601009664940160456)
XLA Ops:
  7.5 4.7 copy.145
  12.1 3.6 reshape.139
  15.8 6.2 %fusion = (bf16[128,16,24,8]{1,0,3,2:T(8,128)(2,1)}, bf16[128,16,24,8]{1,0,3,2:T(8,128)(2,1)}) fusion(f32[16,8]{0,1:T(8,128)S(1)} %maximum_multiply_fusion.3, f32[128,24]{0,1:T(8,128)S(1)} %maximum_multiply_fusion.2), kind=kLoop, calls=%fused_computation.5 | loop fusion | flops 1966080 | bytes 1585664 | tf_op jit(solution)/shard_map/convert_element_type | solution.py:30
  22.0 11.6 %convert_element_type.256 = bf16[2048,192]{0,1:T(8,128)(2,1)S(1)} reshape(bf16[128,16,24,8]{1,0,3,2:T(8,128)(2,1)} %get-tuple-element.26) | data formatting | bytes 1572864 | tf_op jit(solution)/shard_map/convert_element_type | solution.py:30
  33.7 12.3 %convert_element_type.253 = bf16[2048,192]{0,1:T(8,128)(2,1)} reshape(bf16[128,16,24,8]{1,0,3,2:T(8,128)(2,1)} %get-tuple-element.27) | data formatting | bytes 1572864 | tf_op jit(solution)/shard_map/convert_element_type | solution.py:29
  46.0 2.2 fusion.114
  48.2 1.8 fusion.30
  49.9 5.9 %reshape.160 = bf16[16,2,20,192]{2,1,0,3:T(2,128)(2,1)S(1)} reshape(bf16[640,192]{0,1:T(8,128)(2,1)} %fusion.30) | data formatting | bytes 491520 | tf_op jit(solution)/shard_map/reshape | solution.py:51
  55.9 4.2 reshape.162
  60.0 4.8 all-to-all-start
  65.0 5.3 %all-to-all-done = bf16[4,2,15360]{2,1,0:T(2,128)(2,1)S(1)} async-done(((bf16[4,2,15360]{2,1,0:T(2,128)(2,1)}), bf16[4,2,15360]{2,1,0:T(2,128)(2,1)S(1)}, u32[]{:S(2)}, u32[]{:S(2)}) %all-to-all-start) | async-done | bytes 245792 | tf_op jit(solution)/shard_map/all_to_all | solution.py:52
  70.3 4.1 reshape.163
  74.4 2.6 copy.218
  78.0 1.3 reshape.164
  79.3 10.9 %all-to-all-start.1 = ((bf16[16,2,1440]{2,1,0:T(2,128)(2,1)}), bf16[16,2,1440]{2,1,0:T(2,128)(2,1)S(1)}, u32[]{:S(2)}, u32[]{:S(2)}) async-start(bf16[16,2,1440]{2,1,0:T(2,128)(2,1)} %reshape.164), calls=%async_computation.1 | async-start | bytes 196608 | tf_op jit(solution)/shard_map/all_to_all | solution.py:54
  90.4 8.2 %all-to-all-done.1 = bf16[16,2,1440]{2,1,0:T(2,128)(2,1)S(1)} async-done(((bf16[16,2,1440]{2,1,0:T(2,128)(2,1)}), bf16[16,2,1440]{2,1,0:T(2,128)(2,1)S(1)}, u32[]{:S(2)}, u32[]{:S(2)}) %all-to-all-start.1) | async-done | bytes 92192 | tf_op jit(solution)/shard_map/all_to_all | solution.py:54
  99.8 1.2 convert_bitcast_fusion
  101.2 5.0 %multiply_reduce_fusion.1 = bf16[24,24,3,20]{1,0,2,3:T(8,128)(2,1)S(1)} fusion(f32[24,24,3,20]{1,0,2,3:T(8,128)S(1)} %copy.223, bf16[24,24,20,20,3]{1,0,4,3,2:T(8,128)(2,1)} %param.6), kind=kLoop, calls=%fused_computation.3 | loop fusion | flops 2039040 | bytes 1589760 | tf_op jit(solution)/shard_map/klcq,klcoq->kloq/dot_general | solution.py:67
  107.7 10.9 %all_to_all.138 = bf16[16,2,1440]{2,1,0:T(2,128)(2,1)S(1)} all-to-all(bf16[16,2,1440]{2,1,0:T(2,128)(2,1)S(1)} %reshape.166), channel_id=1, replica_groups=mesh['dp'=4,'gx'=4,'gy'=16] {'gy'}, dimensions={0} | all-to-all | bytes 184320 | tf_op jit(solution)/shard_map/all_to_all | solution.py:59
  121.2 1.1 reshape.168
  122.3 9.6 %all_to_all.139 = bf16[4,2,15360]{2,1,0:T(2,128)(2,1)S(1)} all-to-all(bf16[4,2,15360]{2,1,0:T(2,128)(2,1)S(1)} %reshape.168), channel_id=1, replica_groups=mesh['dp'=4,'gx'=4,'gy'=16] {'gx'}, dimensions={0} | all-to-all | bytes 491520 | tf_op jit(solution)/shard_map/all_to_all | solution.py:61
  132.7 1.1 copy.164
  133.8 1.5 reshape.141
  135.4 0.8 fusion.118
  136.2 3.3 convolution_add_fusion.1
  139.5 6.7 %reshape.142 = f32[1,16,2,20,2048]{4,3,2,1,0:T(8,128)} reshape(f32[640,2048]{1,0:T(8,128)} %convolution_add_fusion.1) | data formatting | bytes 10485760 | tf_op jit(solution)/shard_map/reshape | solution.py:64
  146.1 11.0 %fusion.4 = bf16[1,16,2,20,2048]{4,3,2,1,0:T(8,128)(2,1)} fusion(f32[1,16,2,20,2048]{4,3,2,1,0:T(8,128)} %reshape.142, bf16[1,16,2,20,2048]{4,2,3,1,0:T(2,128)(2,1)} %param.5, bf16[16,2,20,2048]{3,1,2,0:T(2,128)(2,1)} %bitcast.208, bf16[20,20]{1,0:T(8,128)(2,1)S(1)} %copy-done), kind=kOutput, calls=%fused_computation.13 | convolution fusion | flops 81264640 | bytes 13108000 | tf_op jit(solution)/shard_map/bxyip,io->bxyop/dot_general | solution.py:71
  157.1 5.3 %reshape.144 = bf16[640,2048]{1,0:T(8,128)(2,1)} reshape(bf16[1,16,2,20,2048]{4,3,2,1,0:T(8,128)(2,1)} %fusion.4) | data formatting | bytes 5242880 | tf_op jit(solution)/shard_map/reshape | solution.py:49
  162.4 2.8 fusion.119
  165.2 2.8 fusion.26
  168.0 3.8 reshape.161
  171.8 3.5 reshape.170
  175.3 8.8 %all_to_all.140 = bf16[4,2,15360]{2,1,0:T(2,128)(2,1)} all-to-all(bf16[4,2,15360]{2,1,0:T(2,128)(2,1)S(1)} %reshape.170), channel_id=1, replica_groups=mesh['dp'=4,'gx'=4,'gy'=16] {'gx'}, dimensions={0} | all-to-all | bytes 491520 | tf_op jit(solution)/shard_map/all_to_all | solution.py:52
  184.2 6.0 %reshape.171 = bf16[192,16,2,20]{3,2,1,0:T(2,128)(2,1)S(1)} reshape(bf16[4,2,15360]{2,1,0:T(2,128)(2,1)} %all_to_all.140) | data formatting | bytes 491520
  190.1 3.4 copy.221
  193.6 1.2 copy.170
  195.7 1.3 reshape.172
  196.9 5.2 %all-to-all-start.5 = ((bf16[16,2,1440]{2,1,0:T(2,128)(2,1)}), bf16[16,2,1440]{2,1,0:T(2,128)(2,1)S(1)}, u32[]{:S(2)}, u32[]{:S(2)}) async-start(bf16[16,2,1440]{2,1,0:T(2,128)(2,1)} %reshape.172), calls=%async_computation.5 | async-start | bytes 196608 | tf_op jit(solution)/shard_map/all_to_all | solution.py:54
  202.1 2.2 copy.187
  204.3 6.3 %all-to-all-done.5 = bf16[16,2,1440]{2,1,0:T(2,128)(2,1)S(1)} async-done(((bf16[16,2,1440]{2,1,0:T(2,128)(2,1)}), bf16[16,2,1440]{2,1,0:T(2,128)(2,1)S(1)}, u32[]{:S(2)}, u32[]{:S(2)}) %all-to-all-start.5) | async-done | bytes 92192 | tf_op jit(solution)/shard_map/all_to_all | solution.py:54
  211.7 1.4 convert_bitcast_fusion.1
  213.1 1.4 copy.224
  214.5 5.0 %multiply_reduce_fusion = bf16[24,24,3,20]{1,0,2,3:T(8,128)(2,1)S(1)} fusion(f32[24,24,3,20]{1,0,2,3:T(8,128)S(1)} %copy.224, bf16[24,24,20,20,3]{1,0,4,3,2:T(8,128)(2,1)} %param.6), kind=kLoop, calls=%fused_computation.2 | loop fusion | flops 2039040 | bytes 1589760 | tf_op jit(solution)/shard_map/kloq,klcoq->klcq/dot_general | solution.py:83
  220.4 1.2 reshape.174
  221.6 3.7 all-to-all-start.6
  225.3 4.9 fusion.31
  230.2 76.2 %psum.15 = f32[20,20]{0,1:T(8,128)S(1)} all-reduce(f32[20,20]{0,1:T(8,128)S(1)} %fusion.31), channel_id=1, replica_groups=mesh['dp'=4,'gx'=4,'gy'=16] {'dp','gx','gy'}, use_global_device_ids=true, to_apply=%region_1.2 | all-reduce | flops 400 | bytes 3200 | tf_op jit(solution)/shard_map/psum | solution.py:77
  307.0 2.3 copy.186
  310.3 1.0 copy.181
  311.3 1.3 fusion.122
  312.6 2.1 fusion.19
  314.7 1.4 copy.183
  316.1 1.8 reshape.176
  317.9 3.4 all-to-all-start.7
  321.4 5.3 %fusion.1 = bf16[24,24,20,20,3]{1,0,4,3,2:T(8,128)(2,1)} fusion(f32[24,24,3,20]{1,0,2,3:T(8,128)S(1)} %copy-done.3, f32[24,24,3,20]{1,0,2,3:T(8,128)} %copy.186), kind=kLoop, calls=%fused_computation.10 | loop fusion | flops 1382400 | bytes 1658880 | tf_op jit(solution)/shard_map/convert_element_type | solution.py:82
  327.7 1.1 copy.185
  328.8 1.5 reshape.146
  330.3 0.8 fusion.123
  331.1 3.2 convolution_add_fusion
  334.4 7.2 %reshape.147 = f32[1,16,2,20,2048]{4,3,2,1,0:T(8,128)} reshape(f32[640,2048]{1,0:T(8,128)} %convolution_add_fusion) | data formatting | bytes 10485760 | tf_op jit(solution)/shard_map/reshape | solution.py:64
  341.6 4.1 fusion.12
  345.7 4.2 copy.189
  349.9 126.0 %all-reduce.2.cloned.1.call-done = bf16[24,24,20,20,3]{1,0,4,3,2:T(8,128)(2,1)} async-done(((bf16[24,24,20,20,3]{1,0,4,3,2:T(8,128)(2,1)}), bf16[24,24,20,20,3]{1,0,4,3,2:T(8,128)(2,1)}) %all-reduce.2.cloned.1.call-update) | async-done | bytes 1382416 | tf_op jit(solution)/shard_map/psum | solution.py:82
  475.9 10.2 %convert_element_type.284 = f32[24,24,20,20,3]{1,0,4,3,2:T(8,128)} convert(bf16[24,24,20,20,3]{1,0,4,3,2:T(8,128)(2,1)} %all-reduce.2.cloned.1.call-done) | non-fusion elementwise | flops 691200 | bytes 4147200 | tf_op jit(solution)/shard_map/convert_element_type | solution.py:82
  (58 shorter events, 13.3 us)
Async XLA Ops:
  7.2 139.0 %copy-start = (bf16[20,20]{1,0:T(8,128)(2,1)S(1)}, bf16[20,20]{1,0:T(8,128)(2,1)}, u32[]{:S(2)}) copy-start(bf16[20,20]{1,0:T(8,128)(2,1)} %param.7) | copy-start | bytes 2404
  60.0 10.3 %all-to-all-start = ((bf16[4,2,15360]{2,1,0:T(2,128)(2,1)}), bf16[4,2,15360]{2,1,0:T(2,128)(2,1)S(1)}, u32[]{:S(2)}, u32[]{:S(2)}) async-start(bf16[4,2,15360]{2,1,0:T(2,128)(2,1)} %reshape.162), calls=%async_computation | async-start | bytes 491520 | tf_op jit(solution)/shard_map/all_to_all | solution.py:52
  79.3 19.3 %all-to-all-start.1 = ((bf16[16,2,1440]{2,1,0:T(2,128)(2,1)}), bf16[16,2,1440]{2,1,0:T(2,128)(2,1)S(1)}, u32[]{:S(2)}, u32[]{:S(2)}) async-start(bf16[16,2,1440]{2,1,0:T(2,128)(2,1)} %reshape.164), calls=%async_computation.1 | async-start | bytes 196608 | tf_op jit(solution)/shard_map/all_to_all | solution.py:54
  119.1 16.2 %copy-start.1 = (bf16[2048,192]{0,1:T(8,128)(2,1)S(1)}, bf16[2048,192]{0,1:T(8,128)(2,1)}, u32[]{:S(2)}) copy-start(bf16[2048,192]{0,1:T(8,128)(2,1)} %convert_element_type.253) | copy-start | bytes 2359300
  196.9 13.7 %all-to-all-start.5 = ((bf16[16,2,1440]{2,1,0:T(2,128)(2,1)}), bf16[16,2,1440]{2,1,0:T(2,128)(2,1)S(1)}, u32[]{:S(2)}, u32[]{:S(2)}) async-start(bf16[16,2,1440]{2,1,0:T(2,128)(2,1)} %reshape.172), calls=%async_computation.5 | async-start | bytes 196608 | tf_op jit(solution)/shard_map/all_to_all | solution.py:54
  221.6 87.7 %all-to-all-start.6 = ((bf16[16,2,1440]{2,1,0:T(2,128)(2,1)}), bf16[16,2,1440]{2,1,0:T(2,128)(2,1)S(1)}, u32[]{:S(2)}, u32[]{:S(2)}) async-start(bf16[16,2,1440]{2,1,0:T(2,128)(2,1)} %reshape.174), calls=%async_computation.6 | async-start | bytes 196608 | tf_op jit(solution)/shard_map/all_to_all | solution.py:59
  230.2 91.2 %copy-start.3 = (f32[24,24,3,20]{1,0,2,3:T(8,128)S(1)}, f32[24,24,3,20]{1,0,2,3:T(8,128)}, u32[]{:S(2)}) copy-start(f32[24,24,3,20]{1,0,2,3:T(8,128)} %copy.187) | copy-start | bytes 414724
  317.9 9.0 %all-to-all-start.7 = ((bf16[4,2,15360]{2,1,0:T(2,128)(2,1)}), bf16[4,2,15360]{2,1,0:T(2,128)(2,1)S(1)}, u32[]{:S(2)}, u32[]{:S(2)}) async-start(bf16[4,2,15360]{2,1,0:T(2,128)(2,1)} %reshape.176), calls=%async_computation.7 | async-start | bytes 491520 | tf_op jit(solution)/shard_map/all_to_all | solution.py:61
  321.3 154.6 %all-reduce.2.cloned.1.call-start = ((), (), s32[]{:S(2)}) async-start(), calls=%async_computation.8 | async-start | bytes 14745600 | tf_op jit(solution)/shard_map/psum | solution.py:82
  334.4 7.2 %copy-start.2 = (bf16[1,16,2,20,2048]{4,3,2,1,0:T(8,128)(2,1)S(1)}, bf16[1,16,2,20,2048]{4,3,2,1,0:T(8,128)(2,1)}, u32[]{:S(2)}) copy-start(bf16[1,16,2,20,2048]{4,3,2,1,0:T(8,128)(2,1)} %fusion.4) | copy-start | bytes 7864324
Sparse Core Ops, SparseCore 0:
  326.8 149.0 all-reduce.1
where the time goes:
time: 503 us; the launch traced here: 493 us
  waiting for transfers between devices  146 us (29%)
  local copies, waits for them, and re-layouts  120 us (24%)
  blocking collectives  105 us (21%)
  matrix products  46.5 us (9%)
  other arithmetic  32.3 us (6%)
  starting transfers between devices  28 us (6%)
  between operations  15.1 us (3%)
    psum x1, waiting for transfers between devices, body(): lax.psum(local_grad.astype(jnp.bfloat16), 'dp').astype(jnp.float32)  126 us
    psum x1, blocking collectives, body(): grad_bypass = lax.psum(bypass_term, ('dp', 'gx', 'gy'))  76.2 us
    unnamed x29, local copies, waits for them, and re-layouts  39.6 us
    dot_general x12, matrix products, mode_dot(): jnp.einsum(form, data, lower, preferred_element_type=jnp.float32)  16.9 us
    all_to_all x2, starting transfers between devices, analyze(): lax.all_to_all(partial_x, 'gy', split_axis=3, concat_axis=1, tiled=True)  16.1 us
    all_to_all x2, waiting for transfers between devices, analyze(): lax.all_to_all(partial_x, 'gy', split_axis=3, concat_axis=1, tiled=True)  14.5 us
    reshape x2, local copies, waits for them, and re-layouts, synthesize(): return values.reshape(1, cells_x, cells_y, channels, NZ * NT)  13.9 us
    convert_element_type x1, local copies, waits for them, and re-layouts, mode_dot(): upper = table.astype(jnp.bfloat16)  12.3 us
  transfers between devices with their start and end apart: 6, of which 5 were waited for; matrix products, arithmetic and copies ran while one was open for 8% of the time, Pallas kernels for 0%

commit v1 on v0

v1 whole, which is shorter than its diff:
```python
import math

import jax
import jax.numpy as jnp
import ml_dtypes
import numpy as np
from jax import lax
from jax.experimental import pallas as pl
from jax.experimental.pallas import tpu as pltpu
from jax.sharding import PartitionSpec as P

MX = 12
MY = 12
MZ = 12
MT = 4
NZ = 128
NT = 16
NX = 64
NY = 32
C = 20
KX = 2 * MX
KY = 2 * MY
PX = 4
PY = 16
DEV = PX * PY
CX = NX // PX
CY = NY // PY
NP = NZ * NT
TILES = NP // 128
GROUPS = C // 4
ROWS = C * CX * CY
Q3 = 3
CHUNK = 16
SPEC = Q3 * GROUPS * KY
XB = 4
BLOCK = C * XB * CY
F32 = jnp.float32
BF16 = jnp.bfloat16
MIB = 2**20
VMEM = pl.BlockSpec(memory_space=pltpu.VMEM)
ANY = pl.BlockSpec(memory_space=pl.ANY)


def basis(length, kept):
    places = np.arange(length)[:, None]
    orders = np.arange(kept)[None, :]
    cos_part = np.cos(2 * np.pi * ((places * orders) % length) / length)
    sin_part = np.sin(2 * np.pi * ((places * (orders + 1)) % length) / length)
    return np.concatenate([cos_part, sin_part], axis=1) * math.sqrt(2.0 / length)


def tables():
    fx, fy = basis(NX, MX), basis(NY, MY)
    fzt = (basis(NZ, MZ)[:, None, :, None] * basis(NT, MT)[None, :, None, :]).reshape(NP, -1)
    by_slot = fzt.reshape(NP, DEV, Q3).transpose(0, 2, 1).reshape(NP, Q3 * DEV)
    ahead = np.zeros((NP, 256))
    ahead[:, : Q3 * DEV] = by_slot
    eye4, eye2 = np.eye(4), np.eye(CY)
    slots = np.eye(CHUNK)[:, : Q3 * GROUPS]
    fx32 = np.zeros((NX, 32))
    fx32[:, :KX] = fx
    x_ahead = np.einsum(
        "gxk,cd,yz->gxcyzdk", fx32.reshape(PX, CX, 32), eye4, eye2
    ).reshape(PX * 128, CY * 128)
    y_ahead = np.einsum("gyl,rs->slygr", fy.reshape(PY, CY, KY), slots).reshape(
        SPEC, CY * PY * CHUNK
    )
    spread = np.einsum("cd,kl,e->ckdel", eye4, np.eye(32), np.ones(4)).reshape(128, 512)
    channel = np.einsum("jk,x,cd,y->jxcykd", np.eye(GROUPS), np.ones(XB), eye4, np.ones(CY))
    channel = channel.reshape(BLOCK, C)
    cell = np.einsum("j,xw,c,yz->jxcywz", np.ones(GROUPS), np.eye(XB), np.ones(4), eye2)
    cell = cell.reshape(BLOCK, XB * CY)
    return {
        "zt_ahead": ahead,
        "zt_back": by_slot.T,
        "x_ahead": x_ahead,
        "x_back": x_ahead.T,
        "y_ahead": y_ahead,
        "y_back": y_ahead.T,
        "spread": spread,
        "channel": channel,
        "same": cell @ cell.T,
    }


TABLES = {name: value.astype(ml_dtypes.bfloat16) for name, value in tables().items()}


def dot(a, b, form=((1,), (0,)), precision=None):
    return lax.dot_general(
        a, b, (form, ((), ())), preferred_element_type=F32, precision=precision
    )


def copies(field_ref, rows_ref, sems, back=False):
    made = []
    for tile in range(TILES):
        for j in range(GROUPS):
            outer = field_ref.at[:, pl.ds(4 * j, 4), :, pl.ds(128 * tile, 128)]
            inner = rows_ref.at[tile, j]
            pair = (inner, outer) if back else (outer, inner)
            made.append(pltpu.make_async_copy(*pair, sems.at[tile, j]))
    return made


def pack_chunks(coeff_ref, stage, extra, send_ref):
    for j in range(GROUPS):
        turned = coeff_ref[pl.ds(128 * j, 128), :].T
        for s in range(Q3):
            stage[pl.ds(s * GROUPS + j, DEV, stride=CHUNK), :] = turned[s * DEV : (s + 1) * DEV]
    stage[pl.ds(CHUNK - 1, DEV, stride=CHUNK), :] = extra
    send_ref[...] = stage[...].astype(BF16).reshape(DEV, CHUNK, 128)


def unpack_chunks(recv_ref, stage, coeff_ref):
    stage[...] = recv_ref[...].reshape(DEV * CHUNK, 128).astype(F32)
    for j in range(GROUPS):
        parts = [stage[pl.ds(s * GROUPS + j, DEV, stride=CHUNK), :] for s in range(Q3)]
        coeff_ref[pl.ds(128 * j, 128), :] = jnp.concatenate(parts, axis=0).T.astype(BF16)


def split_three(value):
    high = value.astype(BF16).astype(F32)
    rest = value - high
    middle = rest.astype(BF16).astype(F32)
    low = (rest - middle).astype(BF16).astype(F32)
    return high + pltpu.roll(middle, 32, 1) + pltpu.roll(low, 64, 1)


def join_three(value):
    lanes = lax.broadcasted_iota(jnp.int32, value.shape, 1)
    whole = value + (pltpu.roll(value, 96, 1) + pltpu.roll(value, 64, 1))
    return jnp.where(lanes < 32, whole, 0.0)


def analyze_kernel(field_ref, zt_ref, send_ref, rows_ref, coeff, stage, sems):
    made = copies(field_ref, rows_ref, sems)
    for copy in made:
        copy.start()
    rows = rows_ref.reshape(TILES, ROWS, 128)
    step = 4
    for first in range(0, TILES, step):
        for copy in made[first * GROUPS : (first + step) * GROUPS]:
            copy.wait()
        part = jnp.concatenate([rows[t] for t in range(first, first + step)], axis=1)
        term = dot(part, zt_ref[pl.ds(128 * first, 128 * step), :])
        if first:
            coeff[...] += term
        else:
            coeff[...] = term
    pack_chunks(coeff, stage, jnp.zeros((DEV, 128), F32), send_ref)


def weights_kernel(weight_ref, out_ref):
    gap = jnp.zeros((8, KY), F32)

    def one(o, carry):
        parts = []
        for s in range(Q3):
            for j in range(GROUPS):
                pieces = []
                for c in range(4):
                    pieces += [weight_ref[4 * j + c, o, s].astype(F32), gap]
                parts.append(jnp.concatenate(pieces, axis=0).T)
        out_ref[o] = jnp.concatenate(parts, axis=0).astype(BF16)
        return carry

    lax.fori_loop(0, C, one, 0)


def to_modes(recv_ref, x_ref, y_ref):
    pieces = recv_ref[...].reshape(PX, PY * CHUNK, 128)
    wide = jnp.concatenate([pieces[g] for g in range(PX)], axis=1)
    along = dot(wide, x_ref[...]).astype(BF16)
    tall = jnp.concatenate([along[:, :128], along[:, 128:]], axis=0)
    return dot(y_ref[...], tall).astype(BF16)


def from_modes(modes, y_ref, x_ref):
    tall = dot(y_ref[...], modes.astype(BF16)).astype(BF16)
    half = PY * CHUNK
    wide = jnp.concatenate([tall[:half], tall[half:]], axis=1)
    return dot(wide, x_ref[...])


def write_chunks(values, send_ref):
    for g in range(PX):
        part = values[:, 128 * g : 128 * (g + 1)].astype(BF16)
        send_ref[pl.ds(g * PY, PY)] = part.reshape(PY, CHUNK, 128)


def mix_kernel(
    recv_ref, weight_ref, cot_ref, xa_ref, ya_ref, yb_ref, xb_ref,
    send_ref, spec_ref, rows_ref, modes, sems,
):
    made = copies(cot_ref, rows_ref, sems)
    for copy in made:
        copy.start()
    spec = to_modes(recv_ref, xa_ref, ya_ref)
    spec_ref[...] = spec
    spec = spec.astype(F32)
    group = lax.broadcasted_iota(jnp.int32, (Q3 * KY, 128), 1) // 32
    for jo in range(GROUPS):
        total = jnp.zeros((Q3 * KY, 128), F32)
        for o4 in range(4):
            term = spec * weight_ref[4 * jo + o4].astype(F32)
            sums = []
            for s in range(Q3):
                at = s * GROUPS * KY
                acc = term[at : at + KY]
                for j in range(1, GROUPS):
                    acc = acc + term[at + j * KY : at + (j + 1) * KY]
                sums.append(acc)
            summed = jnp.concatenate(sums, axis=0)
            summed = summed + pltpu.roll(summed, 64, 1)
            summed = summed + pltpu.roll(summed, 32, 1)
            total = jnp.where(group == o4, summed, total)
        for s in range(Q3):
            modes[pl.ds((s * GROUPS + jo) * KY, KY), :] = total[s * KY : (s + 1) * KY]
    write_chunks(from_modes(modes[...], yb_ref, xb_ref), send_ref)
    for copy in made:
        copy.wait()


def mix_back_kernel(
    recv_ref, weight_ref, spread_ref, xa_ref, ya_ref, yb_ref, xb_ref,
    send_ref, spec_ref, stage,
):
    spec = to_modes(recv_ref, xa_ref, ya_ref)
    spec_ref[...] = spec
    copied = dot(spec, spread_ref[...])
    modes = [jnp.zeros((KY, 128), F32) for _ in range(Q3 * GROUPS)]
    for o in range(C):
        weight = weight_ref[o].astype(F32)
        for s in range(Q3):
            at = (s * GROUPS + o // 4) * KY
            source = copied[at : at + KY, 128 * (o % 4) : 128 * (o % 4 + 1)]
            for j in range(GROUPS):
                k = s * GROUPS + j
                modes[k] = modes[k] + weight[k * KY : (k + 1) * KY] * source
    values = from_modes(jnp.concatenate(modes, axis=0), yb_ref, xb_ref)
    stage[...] = recv_ref[...].reshape(DEV * CHUNK, 128).astype(F32)
    extra = stage[pl.ds(CHUNK - 1, DEV, stride=CHUNK), :]
    extra = jnp.broadcast_to(jnp.sum(extra, axis=0, keepdims=True), (8, 128))
    extra = split_three(join_three(extra))[:1]
    row = lax.broadcasted_iota(jnp.int32, values.shape, 0) % CHUNK
    extra = jnp.concatenate([extra] * PX, axis=1)
    write_chunks(jnp.where(row == CHUNK - 1, extra, values), send_ref)


def block_rows(ref, tile, b):
    return [ref[tile, pl.ds(j * 128 + b * 32, 32), :] for j in range(GROUPS)]


def block_of(ref, n, b):
    left = jnp.concatenate(block_rows(ref, 2 * n, b), axis=0)
    right = jnp.concatenate(block_rows(ref, 2 * n + 1, b), axis=0)
    return jnp.concatenate([left, right], axis=1)


def block_store(ref, n, b, value):
    for half in range(2):
        for j in range(GROUPS):
            ref[2 * n + half, pl.ds(j * 128 + b * 32, 32), :] = value[
                32 * j : 32 * (j + 1), 128 * half : 128 * (half + 1)
            ]


def block_rows_of(ref, b):
    return jnp.concatenate([ref[pl.ds(j * 128 + b * 32, 32), :] for j in range(GROUPS)], axis=0)


def bypass_matrix(bypass_ref, channel_ref, same_ref, form):
    half = dot(channel_ref[...], bypass_ref[...], form).astype(BF16)
    whole = dot(half, channel_ref[...], ((1,), (1,)))
    return (whole * same_ref[...].astype(F32)).astype(BF16)


K0 = math.sqrt(2.0 / math.pi)
K1 = 0.044715


def gelu_slope(x):
    square = x * x
    bend = jnp.tanh(x * (K0 + (K0 * K1) * square))
    inner = x * (K0 + (3.0 * K0 * K1) * square)
    return (0.5 + 0.5 * bend) * (1.0 + inner * (1.0 - bend))


def point_kernel(
    recv_ref, field_ref, cot_ref, bypass_ref, channel_ref, same_ref, back_ref, ahead_ref,
    send_ref, up_ref, stage, inverse, coeff, cross, matrix,
):
    unpack_chunks(recv_ref, stage, inverse)
    matrix[...] = bypass_matrix(bypass_ref, channel_ref, same_ref, ((1,), (1,)))
    coeff[...] = jnp.zeros_like(coeff)
    cross[...] = jnp.zeros_like(cross)
    field = field_ref.reshape(TILES, ROWS, 128)
    cot = cot_ref.reshape(TILES, ROWS, 128)

    def part(n, carry):
        lanes = pl.ds(pl.multiple_of(n * 256, 256), 256)
        for b in range(CX // XB):
            cells = block_of(field, n, b)
            pre = dot(block_rows_of(inverse, b), back_ref[:, lanes]) + dot(matrix[...], cells)
            slope = gelu_slope(pre) * block_of(cot, n, b).astype(F32)
            up = slope.astype(BF16)
            block_store(up_ref, n, b, up)
            term = dot(up, ahead_ref[lanes, :])
            for j in range(GROUPS):
                coeff[pl.ds(j * 128 + b * 32, 32), :] += term[32 * j : 32 * (j + 1)]
            cross[...] += dot(cells, up, ((1,), (1,)))
        return carry

    lax.fori_loop(0, TILES // 2, part, 0)
    kept = cross[...] * same_ref[...].astype(F32)
    channel = channel_ref[...].astype(F32)
    high = lax.Precision.HIGHEST
    small = dot(dot(channel, kept, ((0,), (0,)), high), channel, ((1,), (0,)), high)
    small = jnp.concatenate([small, jnp.zeros((C, 128 - C), F32)], axis=1)
    small = jnp.concatenate([small, jnp.zeros((DEV - C, 128), F32)], axis=0)
    pack_chunks(coeff, stage, split_three(small), send_ref)


def final_kernel(
    recv_ref, up_ref, bypass_ref, channel_ref, same_ref, back_ref,
    out_ref, small_ref, stage, inverse, matrix, rows_ref, sems,
):
    unpack_chunks(recv_ref, stage, inverse)
    small_ref[...] = join_three(stage[pl.ds(CHUNK - 1, DEV, stride=CHUNK), :][:24])
    matrix[...] = bypass_matrix(bypass_ref, channel_ref, same_ref, ((1,), (0,)))
    made = copies(out_ref, rows_ref, sems, back=True)
    rows = rows_ref.reshape(TILES, ROWS, 128)
    for n in range(TILES // 2):
        for b in range(CX // XB):
            value = dot(block_rows_of(inverse, b), back_ref[:, 256 * n : 256 * (n + 1)])
            value = value + dot(matrix[...], block_of(up_ref, n, b))
            block_store(rows, n, b, value.astype(BF16))
        for copy in made[2 * n * GROUPS : 2 * (n + 1) * GROUPS]:
            copy.start()
    for copy in made:
        copy.wait()


def outer_kernel(*refs):
    specs, out_ref, first, second = refs[:8], refs[8], refs[9], refs[10]

    @pl.when(pl.program_id(0) == 0)
    def _():
        for b in range(4):
            for ref, tiles in ((specs[b], first), (specs[4 + b], second)):
                value = ref[...].astype(F32)
                for s in range(Q3):
                    for j in range(GROUPS):
                        at = (s * GROUPS + j) * KY
                        turned = value[at : at + KY].T
                        for c in range(4):
                            tiles[4 * j + c, s, b] = turned[32 * c : 32 * c + KX]

    c = pl.program_id(0)
    for s in range(Q3):
        own = [first[c, s, b] for b in range(4)]

        def one(o, carry):
            terms = [own[b] * second[o, s, b] for b in range(4)]
            out_ref[0, o, s] = (terms[0] + terms[2]) + (terms[1] + terms[3])
            return carry

        lax.fori_loop(0, C, one, 0, unroll=4)


def call(kernel, out, in_specs, scratch, **more):
    return pl.pallas_call(
        kernel,
        out_shape=out,
        in_specs=in_specs,
        scratch_shapes=scratch,
        compiler_params=pltpu.CompilerParams(vmem_limit_bytes=40 * MIB),
        **more,
    )


def around(value):
    return [value] + [
        lax.ppermute(value, "dp", [(i, (i + k) % 4) for i in range(4)]) for k in (1, 2, 3)
    ]


def body(field, cotangent, spectral_weight, bypass_weight):
    table = {name: jnp.asarray(value) for name, value in TABLES.items()}
    shape = jax.ShapeDtypeStruct
    chunks = shape((DEV, CHUNK, 128), BF16)
    modes = shape((SPEC, 128), BF16)
    cells = shape((TILES, GROUPS, CX, 4, CY, 128), BF16)
    rows = shape((TILES, ROWS, 128), BF16)
    stage = pltpu.VMEM((DEV * CHUNK, 128), F32)
    sems = pltpu.SemaphoreType.DMA((TILES, GROUPS))
    field_t = jnp.transpose(field[0], (0, 2, 1, 3))
    cot_t = jnp.transpose(cotangent[0], (0, 2, 1, 3))
    weight_t = jnp.transpose(spectral_weight, (2, 3, 4, 0, 1))

    def exchange(value):
        return lax.all_to_all(value, ("gx", "gy"), 0, 0, tiled=True)

    send, field_rows = call(
        analyze_kernel, (chunks, cells), [ANY, VMEM], [pltpu.VMEM((ROWS, 256), F32), stage, sems],
        out_specs=(VMEM, VMEM),
    )(field_t, table["zt_ahead"])
    recv = exchange(send)
    weight = call(
        weights_kernel, shape((C, SPEC, 128), BF16), [VMEM], [], out_specs=VMEM,
    )(weight_t)
    send, spec, cot_rows = call(
        mix_kernel, (chunks, modes, cells), [VMEM, VMEM, ANY] + [VMEM] * 4,
        [pltpu.VMEM((SPEC, 128), F32), sems], out_specs=(VMEM,) * 3,
    )(recv, weight, cot_t, table["x_ahead"], table["y_ahead"], table["y_back"], table["x_back"])
    recv = exchange(send)
    specs = around(spec)
    send, up = call(
        point_kernel, (chunks, rows), [VMEM] * 8,
        [stage, pltpu.VMEM((ROWS, Q3 * DEV), BF16), pltpu.VMEM((ROWS, 256), F32),
         pltpu.VMEM((BLOCK, BLOCK), F32), pltpu.VMEM((BLOCK, BLOCK), BF16)],
        out_specs=(VMEM,) * 2,
    )(recv, field_rows, cot_rows, bypass_weight, table["channel"], table["same"],
      table["zt_back"], table["zt_ahead"])
    recv = exchange(send)
    send, spec_up = call(
        mix_back_kernel, (chunks, modes), [VMEM] * 7, [stage], out_specs=(VMEM,) * 2,
    )(recv, weight, table["spread"], table["x_ahead"], table["y_ahead"], table["y_back"],
      table["x_back"])
    recv = exchange(send)
    specs_up = around(spec_up)
    grad_field, small = call(
        final_kernel, (shape((CX, C, CY, NP), BF16), shape((24, 128), F32)), [VMEM] * 6,
        [stage, pltpu.VMEM((ROWS, Q3 * DEV), BF16), pltpu.VMEM((BLOCK, BLOCK), BF16),
         pltpu.VMEM((TILES, GROUPS, CX, 4, CY, 128), BF16), sems],
        out_specs=(ANY, VMEM),
    )(recv, up, bypass_weight, table["channel"], table["same"], table["zt_back"])
    smalls = around(small)
    grad_bypass = ((smalls[0] + smalls[2]) + (smalls[1] + smalls[3]))[:C, :C]
    grad_spectral = pl.pallas_call(
        outer_kernel,
        grid=(C,),
        out_shape=shape((C, C, Q3, KX, KY), F32),
        in_specs=[pl.BlockSpec((SPEC, 128), lambda c: (0, 0))] * 8,
        out_specs=pl.BlockSpec((1, C, Q3, KX, KY), lambda c: (c, 0, 0, 0, 0)),
        scratch_shapes=[pltpu.VMEM((C, Q3, 4, KX, KY), F32)] * 2,
        compiler_params=pltpu.CompilerParams(vmem_limit_bytes=40 * MIB),
    )(*specs, *specs_up)
    return (
        jnp.transpose(grad_field, (0, 2, 1, 3))[None],
        jnp.transpose(grad_spectral, (3, 4, 0, 1, 2)),
        grad_bypass,
    )


def solution(mesh):
    in_specs = (
        P("dp", "gx", "gy", None, None),
        P("dp", "gx", "gy", None, None),
        P(None, None, None, None, ("gx", "gy")),
        P(),
    )
    out_specs = (P("dp", "gx", "gy", None, None), P(None, None, None, None, ("gx", "gy")), P())
    return jax.shard_map(body, mesh=mesh, in_specs=in_specs, out_specs=out_specs, check_vma=False)
```

time: 503 us -> 135 us (0.27); the launches traced: 493 us -> 134 us
  waiting for transfers between devices: 146 us -> 10.2 us
  local copies, waits for them, and re-layouts: 120 us -> 16 us
  blocking collectives: 105 us -> 35.7 us
  matrix products: 46.5 us -> 0 us
  Pallas kernels: 0 us -> 40.2 us
  other arithmetic: 32.3 us -> 0.61 us
  between operations: 15.1 us -> 0.86 us
    psum x1 -> x0, waiting for transfers between devices: 126 us -> none  [body(): lax.psum(local_grad.astype(jnp.bfloat16), 'dp').astype(jnp.float32)]
    psum x1 -> x0, blocking collectives: 76.2 us -> none  [body(): grad_bypass = lax.psum(bypass_term, ('dp', 'gx', 'gy'))]
    dot_general x27 -> x0, matrix products: 46.5 us -> none  [the longest x12 16.9 us: mode_dot(): jnp.einsum(form, data, lower, preferred_element_type=jnp.float32)]
    pallas_call x0 -> x7, Pallas kernels: none -> 40.2 us  [the longest x1 12.3 us: body(): pl.pallas_call(outer_kernel, grid=(C,), out_shape=shape((C, C, Q3, KX, KY...]
    reshape x8 -> x0, local copies, waits for them, and re-layouts: 35.6 us -> none  [the longest x2 13.9 us: synthesize(): return values.reshape(1, cells_x, cells_y, channels, NZ * NT)]
    convert_element_type x8 -> x0, local copies, waits for them, and re-layouts: 27.6 us -> none  [the longest x1 12.3 us: mode_dot(): upper = table.astype(jnp.bfloat16)]
    unnamed x29 -> x50, local copies, waits for them, and re-layouts: 39.6 us -> 16 us
    convert_element_type x5 -> x0, other arithmetic: 21.8 us -> none  [the longest x1 10.2 us: body(): lax.psum(local_grad.astype(jnp.bfloat16), 'dp').astype(jnp.float32)]
  transfers between devices with their start and end apart: 6 -> 11, of which waited for: 5 -> 2; matrix products, arithmetic and copies ran while one was open for 8% -> 0% of each run, Pallas kernels for 0% -> 15%
where the time goes in v1:
time: 135 us; the launch traced here: 134 us
  Pallas kernels  40.2 us (30%)
  blocking collectives  35.7 us (26%)
  starting transfers between devices  30.9 us (23%)
  local copies, waits for them, and re-layouts  16 us (12%)
  waiting for transfers between devices  10.2 us (8%)
    all_to_all x2, blocking collectives, exchange(): return lax.all_to_all(value, ('gx', 'gy'), 0, 0, tiled=True)  35.7 us
    all_to_all x2, starting transfers between devices, exchange(): return lax.all_to_all(value, ('gx', 'gy'), 0, 0, tiled=True)  19.1 us
    unnamed x50, local copies, waits for them, and re-layouts  16 us
    pallas_call x1, Pallas kernels, body(): pl.pallas_call(outer_kernel, grid=(C,), out_shape=shape((C, C, Q3, KX, KY...  12.3 us
    ppermute x9, starting transfers between devices, around(): lax.ppermute(value, 'dp', [(i, (i + k) % 4) for i in range(4)])  11.7 us
    all_to_all x2, waiting for transfers between devices, exchange(): return lax.all_to_all(value, ('gx', 'gy'), 0, 0, tiled=True)  10.2 us
    pallas_call x1, Pallas kernels, body(): call(point_kernel, (chunks, rows), [VMEM] * 8, [stage, pltpu.VMEM((ROWS,...  8.56 us
    pallas_call x1, Pallas kernels, body(): call(analyze_kernel, (chunks, cells), [ANY, VMEM], [pltpu.VMEM((ROWS, 256...  5.24 us
  transfers between devices with their start and end apart: 11, of which 2 were waited for; matrix products, arithmetic and copies ran while one was open for 0% of the time, Pallas kernels for 15%

profile of v1, /device:TPU:1, one launch (start us, length us, event | category | flops | bytes accessed | tf_op | source)
XLA Modules:
  0.0 134.3 jit_solution(1951856493031414439)
XLA Ops:
  0.6 0.0 copy-start.1
  0.6 1.2 copy-done.1
  1.9 1.7 %copy-done.4 = bf16[1,16,2,20,2048]{4,2,3,1,0:T(2,128)(2,1)S(1)} copy-done((bf16[1,16,2,20,2048]{4,2,3,1,0:T(2,128)(2,1)S(1)}, bf16[1,16,2,20,2048]{4,2,3,1,0:T(2,128)(2,1)}, u32[]{:S(2)}) %copy-start.4) | copy-done | bytes 2621464
  3.6 5.2 %shard_map.148 = (bf16[64,16,128]{2,1,0:T(8,128)(2,1)}, bf16[16,5,16,4,2,128]{5,4,3,2,1,0:T(2,128)(2,1)S(1)}) custom-call(bf16[16,20,2,2048]{3,2,1,0:T(2,128)(2,1)S(1)} %bitcast.12, bf16[2048,256]{1,0:T(8,128)(2,1)S(1)} %copy-done.1), custom_call_target="tpu_custom_call" | custom-call | tf_op jit(solution)/shard_map/pallas_call | solution.py:405
  8.8 0.0 copy-start.6
  8.9 1.5 %copy-done.6 = bf16[16,5,16,4,2,128]{5,4,3,2,1,0:T(2,128)(2,1)} copy-done((bf16[16,5,16,4,2,128]{5,4,3,2,1,0:T(2,128)(2,1)}, bf16[16,5,16,4,2,128]{5,4,3,2,1,0:T(2,128)(2,1)S(1)}, u32[]{:S(2)}) %copy-start.6) | copy-done | bytes 2621464
  10.3 13.0 %all-to-all-start = ((bf16[64,16,128]{2,1,0:T(8,128)(2,1)}), bf16[64,16,128]{2,1,0:T(8,128)(2,1)S(1)}, u32[]{:S(2)}, u32[]{:S(2)}) async-start(bf16[64,16,128]{2,1,0:T(8,128)(2,1)} %get-tuple-element.14), calls=%async_computation | async-start | bytes 524288 | tf_op jit(solution)/shard_map/all_to_all | solution.py:403
  23.3 0.0 copy-start
  23.3 3.1 %copy-done = bf16[24,24,20,20,3]{1,0,4,3,2:T(8,128)(2,1)S(1)} copy-done((bf16[24,24,20,20,3]{1,0,4,3,2:T(8,128)(2,1)S(1)}, bf16[24,24,20,20,3]{1,0,4,3,2:T(8,128)(2,1)}, u32[]{:S(2)}) %copy-start) | copy-done | bytes 1382424
  26.4 3.5 %shard_map.149.weight_ref = bf16[20,360,128]{2,1,0:T(8,128)(2,1)S(1)} custom-call(bf16[20,20,3,24,24]{4,3,2,1,0:T(8,128)(2,1)S(1)} %bitcast.11), custom_call_target="tpu_custom_call" | custom-call | tf_op jit(solution)/shard_map/pallas_call | solution.py:410
  29.9 5.4 %all-to-all-done.recv_ref = bf16[64,16,128]{2,1,0:T(8,128)(2,1)S(1)} async-done(((bf16[64,16,128]{2,1,0:T(8,128)(2,1)}), bf16[64,16,128]{2,1,0:T(8,128)(2,1)S(1)}, u32[]{:S(2)}, u32[]{:S(2)}) %all-to-all-start) | async-done | bytes 262176 | tf_op jit(solution)/shard_map/all_to_all | solution.py:403
  35.3 0.7 copy-done.14
  36.0 0.0 copy-done.10
  36.0 0.0 copy-done.11
  36.0 1.7 %copy-done.5 = bf16[1,16,2,20,2048]{4,2,3,1,0:T(2,128)(2,1)S(1)} copy-done((bf16[1,16,2,20,2048]{4,2,3,1,0:T(2,128)(2,1)S(1)}, bf16[1,16,2,20,2048]{4,2,3,1,0:T(2,128)(2,1)}, u32[]{:S(2)}) %copy-start.5) | copy-done | bytes 2621464
  37.8 0.9 copy-done.12
  38.7 0.9 copy-done.13
  39.7 0.9 copy-done.15
  40.6 0.0 copy-start.18
  40.7 0.0 copy-start.24
  40.7 4.2 %shard_map.150 = (bf16[64,16,128]{2,1,0:T(8,128)(2,1)S(1)}, bf16[360,128]{1,0:T(8,128)(2,1)S(1)}, bf16[16,5,16,4,2,128]{5,4,3,2,1,0:T(2,128)(2,1)S(1)}) custom-call(bf16[64,16,128]{2,1,0:T(8,128)(2,1)S(1)} %copy-done.15, bf16[20,360,128]{2,1,0:T(8,128)(2,1)S(1)} %shard_map.149.weight_ref, bf16[16,20,2,2048]{3,2,1,0:T(2,128)(2,1)S(1)} %bitcast.13, ...), custom_call_target="tpu_custom_call" | custom-call | tf_op jit(solution)/shard_map/pallas_call | solution.py:413
  44.9 0.0 copy-start.20
  44.9 17.8 %all_to_all.20.recv_ref = bf16[64,16,128]{2,1,0:T(8,128)(2,1)S(1)} all-to-all(bf16[64,16,128]{2,1,0:T(8,128)(2,1)S(1)} %get-tuple-element.15), channel_id=1, replica_groups=mesh['dp'=4,'gx'=4,'gy'=16] {'gx','gy'}, dimensions={0} | all-to-all | bytes 524288 | tf_op jit(solution)/shard_map/all_to_all | solution.py:403
  62.7 0.0 copy-done.20
  62.7 0.0 copy-done.2
  62.7 0.0 copy-done.3
  62.7 0.0 copy-done.7
  62.7 0.0 copy-done.16
  62.7 0.0 copy-done.18
  62.7 0.0 copy-done.24
  62.7 0.0 copy-start.19
  62.8 8.6 %shard_map.151 = (bf16[64,16,128]{2,1,0:T(8,128)(2,1)S(1)}, bf16[16,640,128]{2,1,0:T(8,128)(2,1)S(1)}) custom-call(bf16[64,16,128]{2,1,0:T(8,128)(2,1)S(1)} %all_to_all.20.recv_ref, bf16[16,5,16,4,2,128]{5,4,3,2,1,0:T(2,128)(2,1)S(1)} %copy-done.7, bf16[16,5,16,4,2,128]{5,4,3,2,1,0:T(2,128)(2,1)S(1)} %get-tuple-element.17.cot_ref, ...), custom_call_target="tpu_custom_call" | custom-call | tf_op jit(solution)/shard_map/pallas_call | solution.py:419
  71.3 0.0 copy-start.8
  71.3 17.8 %all_to_all.21.recv_ref = bf16[64,16,128]{2,1,0:T(8,128)(2,1)S(1)} all-to-all(bf16[64,16,128]{2,1,0:T(8,128)(2,1)S(1)} %get-tuple-element.18), channel_id=1, replica_groups=mesh['dp'=4,'gx'=4,'gy'=16] {'gx','gy'}, dimensions={0} | all-to-all | bytes 524288 | tf_op jit(solution)/shard_map/all_to_all | solution.py:403
  89.2 0.0 copy-done.19
  89.2 1.4 %shard_map.152 = (bf16[64,16,128]{2,1,0:T(8,128)(2,1)S(1)}, bf16[360,128]{1,0:T(8,128)(2,1)S(1)}) custom-call(bf16[64,16,128]{2,1,0:T(8,128)(2,1)S(1)} %all_to_all.21.recv_ref, bf16[20,360,128]{2,1,0:T(8,128)(2,1)S(1)} %shard_map.149.weight_ref, bf16[128,512]{1,0:T(8,128)(2,1)S(1)} %copy-done.19, bf16[512,256]{1,0:T(8,128)(2,1)S(1)} %copy-done.13, ...), custom_call_target="tpu_custom_call" | custom-call | tf_op jit(solution)/shard_map/pallas_call | solution.py:427
  90.6 0.0 copy-done.8
  90.6 0.0 copy-start.17
  90.6 0.7 copy-done.17
  91.3 0.6 copy-done.22
  91.9 6.2 %all-to-all-start.3 = ((bf16[64,16,128]{2,1,0:T(8,128)(2,1)}), bf16[64,16,128]{2,1,0:T(8,128)(2,1)S(1)}, u32[]{:S(2)}, u32[]{:S(2)}) async-start(bf16[64,16,128]{2,1,0:T(8,128)(2,1)} %copy-done.17), calls=%async_computation.3 | async-start | bytes 524288 | tf_op jit(solution)/shard_map/all_to_all | solution.py:403
  98.1 2.8 %collective-permute-start.2 = (bf16[360,128]{1,0:T(8,128)(2,1)}, bf16[360,128]{1,0:T(8,128)(2,1)S(1)}, u32[]{:S(2)}, u32[]{:S(2)}) collective-permute-start(bf16[360,128]{1,0:T(8,128)(2,1)} %copy-done.20), channel_id=1, source_target_pairs={{0,192},{64,0},{128,64},{192,128},{1,193},{65,1},{129,65},{193,129... | collective-permute-start | bytes 276488 | tf_op jit(solution)/shard_map/ppermute | solution.py:385
  100.9 0.3 collective-permute-start.1
  101.3 0.7 collective-permute-start
  102.0 2.0 %collective-permute-start.5 = (bf16[360,128]{1,0:T(8,128)(2,1)}, bf16[360,128]{1,0:T(8,128)(2,1)S(1)}, u32[]{:S(2)}, u32[]{:S(2)}) collective-permute-start(bf16[360,128]{1,0:T(8,128)(2,1)} %copy-done.22), channel_id=1, source_target_pairs={{0,192},{64,0},{128,64},{192,128},{1,193},{65,1},{129,65},{193,129... | collective-permute-start | bytes 276488 | tf_op jit(solution)/shard_map/ppermute | solution.py:385
  103.9 1.4 %collective-permute-start.4 = (bf16[360,128]{1,0:T(8,128)(2,1)}, bf16[360,128]{1,0:T(8,128)(2,1)S(1)}, u32[]{:S(2)}, u32[]{:S(2)}) collective-permute-start(bf16[360,128]{1,0:T(8,128)(2,1)} %copy-done.22), channel_id=1, source_target_pairs={{0,128},{64,192},{128,0},{192,64},{1,129},{65,193},{129,1},{193,65... | collective-permute-start | bytes 276488 | tf_op jit(solution)/shard_map/ppermute | solution.py:385
  105.4 0.0 collective-permute-done.2.refs_3_
  105.4 0.0 collective-permute-start.3
  105.4 4.7 %all-to-all-done.3.recv_ref = bf16[64,16,128]{2,1,0:T(8,128)(2,1)S(1)} async-done(((bf16[64,16,128]{2,1,0:T(8,128)(2,1)}), bf16[64,16,128]{2,1,0:T(8,128)(2,1)S(1)}, u32[]{:S(2)}, u32[]{:S(2)}) %all-to-all-start.3) | async-done | bytes 262176 | tf_op jit(solution)/shard_map/all_to_all | solution.py:403
  110.1 1.7 %copy-done.9 = bf16[16,640,128]{2,1,0:T(8,128)(2,1)S(1)} copy-done((bf16[16,640,128]{2,1,0:T(8,128)(2,1)S(1)}, bf16[16,640,128]{2,1,0:T(8,128)(2,1)}, u32[]{:S(2)}) %copy-start.9) | copy-done | bytes 2621464
  111.8 5.0 %shard_map.153 = (bf16[16,20,2,2048]{3,2,1,0:T(2,128)(2,1)}, f32[24,128]{1,0:T(8,128)S(1)}) custom-call(bf16[64,16,128]{2,1,0:T(8,128)(2,1)S(1)} %all-to-all-done.3.recv_ref, bf16[16,640,128]{2,1,0:T(8,128)(2,1)S(1)} %copy-done.9, bf16[20,20]{1,0:T(8,128)(2,1)S(1)} %copy-done.24, bf16[160,20]{1,0:T(8,128)(2,1)S(1)} %copy-done.18, ...), custom_call_target="tpu_custom_call" | custom-call | tf_op jit(solution)/shard_map/pallas_call | solution.py:433
  116.9 0.0 collective-permute-done.1.refs_2_
  116.9 2.8 %collective-permute-start.8 = (f32[24,128]{1,0:T(8,128)S(1)}, f32[24,128]{1,0:T(8,128)S(1)}, u32[]{:S(2)}, u32[]{:S(2)}) collective-permute-start(f32[24,128]{1,0:T(8,128)S(1)} %get-tuple-element.24), channel_id=1, source_target_pairs={{0,192},{64,0},{128,64},{192,128},{1,193},{65,1},{129,65},{193,129... | collective-permute-start | bytes 36872 | tf_op jit(solution)/shard_map/ppermute | solution.py:385
  119.7 0.0 collective-permute-done.refs_1_
  119.7 0.0 collective-permute-start.7
  119.7 0.0 collective-permute-done.5.refs_7_
  119.7 1.6 %collective-permute-start.6 = (f32[24,128]{1,0:T(8,128)S(1)}, f32[24,128]{1,0:T(8,128)S(1)}, u32[]{:S(2)}, u32[]{:S(2)}) collective-permute-start(f32[24,128]{1,0:T(8,128)S(1)} %get-tuple-element.24), channel_id=1, source_target_pairs={{0,128},{64,192},{128,0},{192,64},{1,129},{65,193},{129,1},{193,65... | collective-permute-start | bytes 36872 | tf_op jit(solution)/shard_map/ppermute | solution.py:385
  121.3 0.0 collective-permute-done.4.refs_6_
  121.3 0.0 collective-permute-done.3.refs_5_
  121.4 12.3 %shard_map.154 = f32[20,20,3,24,24]{4,3,2,1,0:T(8,128)} custom-call(bf16[360,128]{1,0:T(8,128)(2,1)S(1)} %copy-done.21, bf16[360,128]{1,0:T(8,128)(2,1)S(1)} %collective-permute-done.refs_1_, bf16[360,128]{1,0:T(8,128)(2,1)S(1)} %collective-permute-done.1.refs_2_, bf16[360,128]{1,0:T(8,128)(2,1)S(1)} %collective-permute-done.2.refs_3_, ...), custom_call_target="tpu_custom_call" | custom-call | tf_op jit(solution)/shard_map/pallas_call | solution.py:441
  133.7 0.0 collective-permute-done.8
  133.7 0.0 collective-permute-done.7
  133.7 0.0 collective-permute-done.6
  133.7 0.6 fusion
  (18 shorter events, 0.0 us)
Async XLA Ops:
  0.6 1.2 copy-start.1
  1.9 1.7 %copy-start.4 = (bf16[1,16,2,20,2048]{4,2,3,1,0:T(2,128)(2,1)S(1)}, bf16[1,16,2,20,2048]{4,2,3,1,0:T(2,128)(2,1)}, u32[]{:S(2)}) copy-start(bf16[1,16,2,20,2048]{4,2,3,1,0:T(2,128)(2,1)} %param.13) | copy-start | bytes 7864324
  8.8 1.5 %copy-start.6 = (bf16[16,5,16,4,2,128]{5,4,3,2,1,0:T(2,128)(2,1)}, bf16[16,5,16,4,2,128]{5,4,3,2,1,0:T(2,128)(2,1)S(1)}, u32[]{:S(2)}) copy-start(bf16[16,5,16,4,2,128]{5,4,3,2,1,0:T(2,128)(2,1)S(1)} %get-tuple-element.16.field_ref) | copy-start | bytes 7864324
  10.3 25.0 %all-to-all-start = ((bf16[64,16,128]{2,1,0:T(8,128)(2,1)}), bf16[64,16,128]{2,1,0:T(8,128)(2,1)S(1)}, u32[]{:S(2)}, u32[]{:S(2)}) async-start(bf16[64,16,128]{2,1,0:T(8,128)(2,1)} %get-tuple-element.14), calls=%async_computation | async-start | bytes 524288 | tf_op jit(solution)/shard_map/all_to_all | solution.py:403
  23.3 3.1 %copy-start = (bf16[24,24,20,20,3]{1,0,4,3,2:T(8,128)(2,1)S(1)}, bf16[24,24,20,20,3]{1,0,4,3,2:T(8,128)(2,1)}, u32[]{:S(2)}) copy-start(bf16[24,24,20,20,3]{1,0,4,3,2:T(8,128)(2,1)} %param.15) | copy-start | bytes 4147204
  26.4 9.6 %copy-start.10 = (bf16[512,360]{1,0:T(8,128)(2,1)S(1)}, bf16[512,360]{1,0:T(8,128)(2,1)}, u32[]{:S(2)}) copy-start(bf16[512,360]{1,0:T(8,128)(2,1)} %constant.23.clone.yb_ref) | copy-start | bytes 1105924
  26.4 9.6 %copy-start.11 = (bf16[360,512]{1,0:T(8,128)(2,1)S(1)}, bf16[360,512]{1,0:T(8,128)(2,1)}, u32[]{:S(2)}) copy-start(bf16[360,512]{1,0:T(8,128)(2,1)} %constant.22.clone.ya_ref) | copy-start | bytes 1105924
  35.3 0.7 copy-start.14
  36.0 1.7 %copy-start.5 = (bf16[1,16,2,20,2048]{4,2,3,1,0:T(2,128)(2,1)S(1)}, bf16[1,16,2,20,2048]{4,2,3,1,0:T(2,128)(2,1)}, u32[]{:S(2)}) copy-start(bf16[1,16,2,20,2048]{4,2,3,1,0:T(2,128)(2,1)} %param.14) | copy-start | bytes 7864324
  37.8 0.9 copy-start.12
  38.7 0.9 copy-start.13
  39.7 0.9 copy-start.15
  40.6 22.1 %copy-start.2 = (bf16[2048,256]{1,0:T(8,128)(2,1)S(1)}, bf16[2048,256]{1,0:T(8,128)(2,1)}, u32[]{:S(2)}) copy-start(bf16[2048,256]{1,0:T(8,128)(2,1)} %constant.18.clone.zt_ref.ahead_ref) | copy-start | bytes 3145732
  40.6 22.1 %copy-start.3 = (bf16[192,2048]{1,0:T(8,128)(2,1)S(1)}, bf16[192,2048]{1,0:T(8,128)(2,1)}, u32[]{:S(2)}) copy-start(bf16[192,2048]{1,0:T(8,128)(2,1)} %constant.19.clone.back_ref) | copy-start | bytes 2359300
  40.6 22.1 %copy-start.7 = (bf16[16,5,16,4,2,128]{5,4,3,2,1,0:T(2,128)(2,1)S(1)}, bf16[16,5,16,4,2,128]{5,4,3,2,1,0:T(2,128)(2,1)}, u32[]{:S(2)}) copy-start(bf16[16,5,16,4,2,128]{5,4,3,2,1,0:T(2,128)(2,1)} %copy-done.6) | copy-start | bytes 7864324
  40.6 22.1 %copy-start.16 = (bf16[160,160]{1,0:T(8,128)(2,1)S(1)}, bf16[160,160]{1,0:T(8,128)(2,1)}, u32[]{:S(2)}) copy-start(bf16[160,160]{1,0:T(8,128)(2,1)} %constant.26.clone.same_ref) | copy-start | bytes 153604
  40.6 22.1 %copy-start.18 = (bf16[160,20]{1,0:T(8,128)(2,1)S(1)}, bf16[160,20]{1,0:T(8,128)(2,1)}, u32[]{:S(2)}) copy-start(bf16[160,20]{1,0:T(8,128)(2,1)} %constant.25.clone.channel_ref) | copy-start | bytes 19204
  40.7 22.1 %copy-start.24 = (bf16[20,20]{1,0:T(8,128)(2,1)S(1)}, bf16[20,20]{1,0:T(8,128)(2,1)}, u32[]{:S(2)}) copy-start(bf16[20,20]{1,0:T(8,128)(2,1)} %bypass_ref.3) | copy-start | bytes 2404
  44.9 17.8 %copy-start.20 = (bf16[360,128]{1,0:T(8,128)(2,1)}, bf16[360,128]{1,0:T(8,128)(2,1)S(1)}, u32[]{:S(2)}) copy-start(bf16[360,128]{1,0:T(8,128)(2,1)S(1)} %get-tuple-element.22.refs_0_) | copy-start | bytes 276484
  62.7 26.4 %copy-start.19 = (bf16[128,512]{1,0:T(8,128)(2,1)S(1)}, bf16[128,512]{1,0:T(8,128)(2,1)}, u32[]{:S(2)}) copy-start(bf16[128,512]{1,0:T(8,128)(2,1)} %constant.24.clone.spread_ref) | copy-start | bytes 393220
  71.3 19.3 %copy-start.8 = (bf16[16,640,128]{2,1,0:T(8,128)(2,1)}, bf16[16,640,128]{2,1,0:T(8,128)(2,1)S(1)}, u32[]{:S(2)}) copy-start(bf16[16,640,128]{2,1,0:T(8,128)(2,1)S(1)} %get-tuple-element.20.up_ref) | copy-start | bytes 7864324
  90.6 0.7 copy-start.17
  91.3 0.6 copy-start.22
  91.9 29.4 %copy-start.21 = (bf16[360,128]{1,0:T(8,128)(2,1)S(1)}, bf16[360,128]{1,0:T(8,128)(2,1)}, u32[]{:S(2)}) copy-start(bf16[360,128]{1,0:T(8,128)(2,1)} %copy-done.20) | copy-start | bytes 276484
  91.9 29.4 %copy-start.23 = (bf16[360,128]{1,0:T(8,128)(2,1)S(1)}, bf16[360,128]{1,0:T(8,128)(2,1)}, u32[]{:S(2)}) copy-start(bf16[360,128]{1,0:T(8,128)(2,1)} %copy-done.22) | copy-start | bytes 276484
  91.9 18.2 %all-to-all-start.3 = ((bf16[64,16,128]{2,1,0:T(8,128)(2,1)}), bf16[64,16,128]{2,1,0:T(8,128)(2,1)S(1)}, u32[]{:S(2)}, u32[]{:S(2)}) async-start(bf16[64,16,128]{2,1,0:T(8,128)(2,1)} %copy-done.17), calls=%async_computation.3 | async-start | bytes 524288 | tf_op jit(solution)/shard_map/all_to_all | solution.py:403
  98.1 7.3 %collective-permute-start.2 = (bf16[360,128]{1,0:T(8,128)(2,1)}, bf16[360,128]{1,0:T(8,128)(2,1)S(1)}, u32[]{:S(2)}, u32[]{:S(2)}) collective-permute-start(bf16[360,128]{1,0:T(8,128)(2,1)} %copy-done.20), channel_id=1, source_target_pairs={{0,192},{64,0},{128,64},{192,128},{1,193},{65,1},{129,65},{193,129... | collective-permute-start | bytes 276488 | tf_op jit(solution)/shard_map/ppermute | solution.py:385
  100.9 15.9 %collective-permute-start.1 = (bf16[360,128]{1,0:T(8,128)(2,1)}, bf16[360,128]{1,0:T(8,128)(2,1)S(1)}, u32[]{:S(2)}, u32[]{:S(2)}) collective-permute-start(bf16[360,128]{1,0:T(8,128)(2,1)} %copy-done.20), channel_id=1, source_target_pairs={{0,128},{64,192},{128,0},{192,64},{1,129},{65,193},{129,1},{193,65... | collective-permute-start | bytes 276488 | tf_op jit(solution)/shard_map/ppermute | solution.py:385
  101.3 18.4 %collective-permute-start = (bf16[360,128]{1,0:T(8,128)(2,1)}, bf16[360,128]{1,0:T(8,128)(2,1)S(1)}, u32[]{:S(2)}, u32[]{:S(2)}) collective-permute-start(bf16[360,128]{1,0:T(8,128)(2,1)} %copy-done.20), channel_id=1, source_target_pairs={{0,64},{64,128},{128,192},{192,0},{1,65},{65,129},{129,193},{193,1... | collective-permute-start | bytes 276488 | tf_op jit(solution)/shard_map/ppermute | solution.py:385
  102.0 17.7 %collective-permute-start.5 = (bf16[360,128]{1,0:T(8,128)(2,1)}, bf16[360,128]{1,0:T(8,128)(2,1)S(1)}, u32[]{:S(2)}, u32[]{:S(2)}) collective-permute-start(bf16[360,128]{1,0:T(8,128)(2,1)} %copy-done.22), channel_id=1, source_target_pairs={{0,192},{64,0},{128,64},{192,128},{1,193},{65,1},{129,65},{193,129... | collective-permute-start | bytes 276488 | tf_op jit(solution)/shard_map/ppermute | solution.py:385
  103.9 17.4 %collective-permute-start.4 = (bf16[360,128]{1,0:T(8,128)(2,1)}, bf16[360,128]{1,0:T(8,128)(2,1)S(1)}, u32[]{:S(2)}, u32[]{:S(2)}) collective-permute-start(bf16[360,128]{1,0:T(8,128)(2,1)} %copy-done.22), channel_id=1, source_target_pairs={{0,128},{64,192},{128,0},{192,64},{1,129},{65,193},{129,1},{193,65... | collective-permute-start | bytes 276488 | tf_op jit(solution)/shard_map/ppermute | solution.py:385
  105.4 16.0 %collective-permute-start.3 = (bf16[360,128]{1,0:T(8,128)(2,1)}, bf16[360,128]{1,0:T(8,128)(2,1)S(1)}, u32[]{:S(2)}, u32[]{:S(2)}) collective-permute-start(bf16[360,128]{1,0:T(8,128)(2,1)} %copy-done.22), channel_id=1, source_target_pairs={{0,64},{64,128},{128,192},{192,0},{1,65},{65,129},{129,193},{193,1... | collective-permute-start | bytes 276488 | tf_op jit(solution)/shard_map/ppermute | solution.py:385
  110.1 1.7 %copy-start.9 = (bf16[16,640,128]{2,1,0:T(8,128)(2,1)S(1)}, bf16[16,640,128]{2,1,0:T(8,128)(2,1)}, u32[]{:S(2)}) copy-start(bf16[16,640,128]{2,1,0:T(8,128)(2,1)} %copy-done.8) | copy-start | bytes 7864324
  116.9 16.8 %collective-permute-start.8 = (f32[24,128]{1,0:T(8,128)S(1)}, f32[24,128]{1,0:T(8,128)S(1)}, u32[]{:S(2)}, u32[]{:S(2)}) collective-permute-start(f32[24,128]{1,0:T(8,128)S(1)} %get-tuple-element.24), channel_id=1, source_target_pairs={{0,192},{64,0},{128,64},{192,128},{1,193},{65,1},{129,65},{193,129... | collective-permute-start | bytes 36872 | tf_op jit(solution)/shard_map/ppermute | solution.py:385
  119.7 14.0 %collective-permute-start.7 = (f32[24,128]{1,0:T(8,128)S(1)}, f32[24,128]{1,0:T(8,128)S(1)}, u32[]{:S(2)}, u32[]{:S(2)}) collective-permute-start(f32[24,128]{1,0:T(8,128)S(1)} %get-tuple-element.24), channel_id=1, source_target_pairs={{0,64},{64,128},{128,192},{192,0},{1,65},{65,129},{129,193},{193,1... | collective-permute-start | bytes 36872 | tf_op jit(solution)/shard_map/ppermute | solution.py:385
  119.7 14.0 %collective-permute-start.6 = (f32[24,128]{1,0:T(8,128)S(1)}, f32[24,128]{1,0:T(8,128)S(1)}, u32[]{:S(2)}, u32[]{:S(2)}) collective-permute-start(f32[24,128]{1,0:T(8,128)S(1)} %get-tuple-element.24), channel_id=1, source_target_pairs={{0,128},{64,192},{128,0},{192,64},{1,129},{65,193},{129,1},{193,65... | collective-permute-start | bytes 36872 | tf_op jit(solution)/shard_map/ppermute | solution.py:385

commit v2 on v1

--- a/solution.py
+++ b/solution.py
@@ -32,13 +32,18 @@
 Q3 = 3
 CHUNK = 16
 SPEC = Q3 * GROUPS * KY
-XB = 4
+XB = 8
+PART = 4 * XB * CY
+WIDE = 512
+STEPS = NP // WIDE
+PER = WIDE // 128
+NQ = Q3 * DEV
 BLOCK = C * XB * CY
 F32 = jnp.float32
 BF16 = jnp.bfloat16
 MIB = 2**20
 VMEM = pl.BlockSpec(memory_space=pltpu.VMEM)
-ANY = pl.BlockSpec(memory_space=pl.ANY)
+HBM = pl.BlockSpec(memory_space=pl.ANY)
 
 
 def basis(length, kept):
@@ -79,7 +84,7 @@
         "y_back": y_ahead.T,
         "spread": spread,
         "channel": channel,
-        "same": cell @ cell.T,
+        "same": np.concatenate([np.zeros((BLOCK, 64)), cell @ cell.T], axis=1),
     }
 
 
@@ -112,11 +117,13 @@
     send_ref[...] = stage[...].astype(BF16).reshape(DEV, CHUNK, 128)
 
 
-def unpack_chunks(recv_ref, stage, coeff_ref):
+def unpack_chunks(recv_ref, stage, left_ref):
     stage[...] = recv_ref[...].reshape(DEV * CHUNK, 128).astype(F32)
     for j in range(GROUPS):
         parts = [stage[pl.ds(s * GROUPS + j, DEV, stride=CHUNK), :] for s in range(Q3)]
-        coeff_ref[pl.ds(128 * j, 128), :] = jnp.concatenate(parts, axis=0).T.astype(BF16)
+        turned = jnp.concatenate(parts, axis=0).T.astype(BF16)
+        for b in range(CX // XB):
+            left_ref[b, pl.ds(PART * j, PART), pl.ds(0, NQ)] = turned[PART * b : PART * (b + 1)]
 
 
 def split_three(value):
@@ -133,15 +140,32 @@
     return jnp.where(lanes < 32, whole, 0.0)
 
 
-def analyze_kernel(field_ref, zt_ref, send_ref, rows_ref, coeff, stage, sems):
-    made = copies(field_ref, rows_ref, sems)
+def start_all(*pairs):
+    made = [pltpu.make_async_copy(*pair) for pair in pairs]
     for copy in made:
         copy.start()
+    return made
+
+
+def analyze_kernel(
+    field_ref, zt_hbm, send_ref, rows_hbm, rows_ref, zt_ref, coeff, stage, sems, zt_sems, out_sems,
+):
+    made = copies(field_ref, rows_ref, sems)
+    step = 4
+    zt_made = []
+    for first in range(0, TILES, step):
+        part = pl.ds(128 * first, 128 * step)
+        zt_made += start_all((zt_hbm.at[part], zt_ref.at[part], zt_sems.at[first // step]))
+        for copy in made[first * GROUPS : (first + step) * GROUPS]:
+            copy.start()
     rows = rows_ref.reshape(TILES, ROWS, 128)
-    step = 4
+    kept = []
     for first in range(0, TILES, step):
+        zt_made[first // step].wait()
         for copy in made[first * GROUPS : (first + step) * GROUPS]:
             copy.wait()
+        some = pl.ds(first, step)
+        kept += start_all((rows_ref.at[some], rows_hbm.at[some], out_sems.at[first // step]))
         part = jnp.concatenate([rows[t] for t in range(first, first + step)], axis=1)
         term = dot(part, zt_ref[pl.ds(128 * first, 128 * step), :])
         if first:
@@ -149,9 +173,14 @@
         else:
             coeff[...] = term
     pack_chunks(coeff, stage, jnp.zeros((DEV, 128), F32), send_ref)
-
-
-def weights_kernel(weight_ref, out_ref):
+    for copy in kept:
+        copy.wait()
+
+
+def weights_kernel(weight_ref, cot_ref, out_ref, rows_ref, sems):
+    made = copies(cot_ref, rows_ref, sems)
+    for copy in made:
+        copy.start()
     gap = jnp.zeros((8, KY), F32)
 
     def one(o, carry):
@@ -166,6 +195,8 @@
         return carry
 
     lax.fori_loop(0, C, one, 0)
+    for copy in made:
+        copy.wait()
 
 
 def to_modes(recv_ref, x_ref, y_ref):
@@ -190,12 +221,8 @@
 
 
 def mix_kernel(
-    recv_ref, weight_ref, cot_ref, xa_ref, ya_ref, yb_ref, xb_ref,
-    send_ref, spec_ref, rows_ref, modes, sems,
+    recv_ref, weight_ref, xa_ref, ya_ref, yb_ref, xb_ref, send_ref, spec_ref, modes,
 ):
-    made = copies(cot_ref, rows_ref, sems)
-    for copy in made:
-        copy.start()
     spec = to_modes(recv_ref, xa_ref, ya_ref)
     spec_ref[...] = spec
     spec = spec.astype(F32)
@@ -218,13 +245,10 @@
         for s in range(Q3):
             modes[pl.ds((s * GROUPS + jo) * KY, KY), :] = total[s * KY : (s + 1) * KY]
     write_chunks(from_modes(modes[...], yb_ref, xb_ref), send_ref)
-    for copy in made:
-        copy.wait()
 
 
 def mix_back_kernel(
-    recv_ref, weight_ref, spread_ref, xa_ref, ya_ref, yb_ref, xb_ref,
-    send_ref, spec_ref, stage,
+    recv_ref, weight_ref, spread_ref, xa_ref, ya_ref, yb_ref, xb_ref, send_ref, spec_ref, stage,
 ):
     spec = to_modes(recv_ref, xa_ref, ya_ref)
     spec_ref[...] = spec
@@ -248,32 +272,29 @@
     write_chunks(jnp.where(row == CHUNK - 1, extra, values), send_ref)
 
 
-def block_rows(ref, tile, b):
-    return [ref[tile, pl.ds(j * 128 + b * 32, 32), :] for j in range(GROUPS)]
-
-
-def block_of(ref, n, b):
-    left = jnp.concatenate(block_rows(ref, 2 * n, b), axis=0)
-    right = jnp.concatenate(block_rows(ref, 2 * n + 1, b), axis=0)
-    return jnp.concatenate([left, right], axis=1)
-
-
-def block_store(ref, n, b, value):
-    for half in range(2):
+def block_of(ref, first, b):
+    tiles = []
+    for t in range(PER):
+        rows = [ref[first + t, pl.ds(j * 128 + b * PART, PART), :] for j in range(GROUPS)]
+        tiles.append(jnp.concatenate(rows, axis=0))
+    return jnp.concatenate(tiles, axis=1)
+
+
+def block_store(ref, first, b, value):
+    for t in range(PER):
         for j in range(GROUPS):
-            ref[2 * n + half, pl.ds(j * 128 + b * 32, 32), :] = value[
-                32 * j : 32 * (j + 1), 128 * half : 128 * (half + 1)
+            ref[first + t, pl.ds(j * 128 + b * PART, PART), :] = value[
+                PART * j : PART * (j + 1), 128 * t : 128 * (t + 1)
             ]
 
 
-def block_rows_of(ref, b):
-    return jnp.concatenate([ref[pl.ds(j * 128 + b * 32, 32), :] for j in range(GROUPS)], axis=0)
-
-
-def bypass_matrix(bypass_ref, channel_ref, same_ref, form):
+def bypass_matrix(bypass_ref, channel_ref, same_ref, form, left_ref):
     half = dot(channel_ref[...], bypass_ref[...], form).astype(BF16)
-    whole = dot(half, channel_ref[...], ((1,), (1,)))
-    return (whole * same_ref[...].astype(F32)).astype(BF16)
+    shifted = jnp.concatenate([jnp.zeros((64, C), F32), channel_ref[...].astype(F32)], axis=0)
+    whole = dot(half, shifted.astype(BF16), ((1,), (1,)))
+    whole = (whole * same_ref[...].astype(F32)).astype(BF16)
+    for b in range(CX // XB):
+        left_ref[b, :, pl.ds(128, BLOCK + 64)] = whole
 
 
 K0 = math.sqrt(2.0 / math.pi)
@@ -288,94 +309,129 @@
 
 
 def point_kernel(
-    recv_ref, field_ref, cot_ref, bypass_ref, channel_ref, same_ref, back_ref, ahead_ref,
-    send_ref, up_ref, stage, inverse, coeff, cross, matrix,
+    recv_ref, field_hbm, cot_hbm, bypass_ref, channel_ref, same_ref, back_hbm, ahead_hbm,
+    send_ref, up_hbm,
+    field_ref, cot_ref, back_ref, ahead_ref, up_ref, stage, left, coeff, cross, table_sems, sems,
 ):
-    unpack_chunks(recv_ref, stage, inverse)
-    matrix[...] = bypass_matrix(bypass_ref, channel_ref, same_ref, ((1,), (1,)))
+    field_hbm = field_hbm.reshape(TILES, ROWS, 128)
+    cot_hbm = cot_hbm.reshape(TILES, ROWS, 128)
+    tables_made = start_all((back_hbm, back_ref, table_sems.at[0]))
+    made = []
+    for n in range(STEPS):
+        some = pl.ds(PER * n, PER)
+        made.append(
+            start_all(
+                (field_hbm.at[some], field_ref.at[some], sems.at[0, n]),
+                (cot_hbm.at[some], cot_ref.at[some], sems.at[1, n]),
+            )
+        )
+        if n == 0:
+            tables_made += start_all((ahead_hbm, ahead_ref, table_sems.at[1]))
+    bypass_matrix(bypass_ref, channel_ref, same_ref, ((1,), (1,)), left)
+    unpack_chunks(recv_ref, stage, left)
     coeff[...] = jnp.zeros_like(coeff)
     cross[...] = jnp.zeros_like(cross)
-    field = field_ref.reshape(TILES, ROWS, 128)
-    cot = cot_ref.reshape(TILES, ROWS, 128)
-
-    def part(n, carry):
-        lanes = pl.ds(pl.multiple_of(n * 256, 256), 256)
+    tables_made[0].wait()
+    kept = []
+    for n in range(STEPS):
+        for copy in made[n]:
+            copy.wait()
         for b in range(CX // XB):
-            cells = block_of(field, n, b)
-            pre = dot(block_rows_of(inverse, b), back_ref[:, lanes]) + dot(matrix[...], cells)
-            slope = gelu_slope(pre) * block_of(cot, n, b).astype(F32)
+            cells = block_of(field_ref, PER * n, b)
+            right = jnp.concatenate([back_ref[:, WIDE * n : WIDE * (n + 1)], cells], axis=0)
+            pre = dot(left[b], right)
+            slope = gelu_slope(pre) * block_of(cot_ref, PER * n, b).astype(F32)
             up = slope.astype(BF16)
-            block_store(up_ref, n, b, up)
-            term = dot(up, ahead_ref[lanes, :])
+            block_store(up_ref, PER * n, b, up)
+            if n == 0 and b == 0:
+                tables_made[1].wait()
+            term = dot(up, ahead_ref[WIDE * n : WIDE * (n + 1), :])
             for j in range(GROUPS):
-                coeff[pl.ds(j * 128 + b * 32, 32), :] += term[32 * j : 32 * (j + 1)]
+                coeff[pl.ds(j * 128 + b * PART, PART), :] += term[PART * j : PART * (j + 1)]
             cross[...] += dot(cells, up, ((1,), (1,)))
-        return carry
-
-    lax.fori_loop(0, TILES // 2, part, 0)
-    kept = cross[...] * same_ref[...].astype(F32)
+        some = pl.ds(PER * n, PER)
+        kept += start_all((up_ref.at[some], up_hbm.at[some], sems.at[2, n]))
+    kept_cross = cross[...] * same_ref[:, 64:].astype(F32)
     channel = channel_ref[...].astype(F32)
     high = lax.Precision.HIGHEST
-    small = dot(dot(channel, kept, ((0,), (0,)), high), channel, ((1,), (0,)), high)
+    small = dot(dot(channel, kept_cross, ((0,), (0,)), high), channel, ((1,), (0,)), high)
     small = jnp.concatenate([small, jnp.zeros((C, 128 - C), F32)], axis=1)
     small = jnp.concatenate([small, jnp.zeros((DEV - C, 128), F32)], axis=0)
     pack_chunks(coeff, stage, split_three(small), send_ref)
+    for copy in kept:
+        copy.wait()
 
 
 def final_kernel(
-    recv_ref, up_ref, bypass_ref, channel_ref, same_ref, back_ref,
-    out_ref, small_ref, stage, inverse, matrix, rows_ref, sems,
+    recv_ref, up_hbm, bypass_ref, channel_ref, same_ref, back_hbm,
+    out_ref, up_ref, back_ref, stage, left, rows_ref, table_sem, up_sems, sems,
 ):
-    unpack_chunks(recv_ref, stage, inverse)
-    small_ref[...] = join_three(stage[pl.ds(CHUNK - 1, DEV, stride=CHUNK), :][:24])
-    matrix[...] = bypass_matrix(bypass_ref, channel_ref, same_ref, ((1,), (0,)))
+    (table_made,) = start_all((back_hbm, back_ref, table_sem))
+    up_made = []
+    for n in range(STEPS):
+        some = pl.ds(PER * n, PER)
+        up_made += start_all((up_hbm.at[some], up_ref.at[some], up_sems.at[n]))
+    bypass_matrix(bypass_ref, channel_ref, same_ref, ((1,), (0,)), left)
+    unpack_chunks(recv_ref, stage, left)
     made = copies(out_ref, rows_ref, sems, back=True)
     rows = rows_ref.reshape(TILES, ROWS, 128)
-    for n in range(TILES // 2):
+    table_made.wait()
+    for n in range(STEPS):
+        up_made[n].wait()
         for b in range(CX // XB):
-            value = dot(block_rows_of(inverse, b), back_ref[:, 256 * n : 256 * (n + 1)])
-            value = value + dot(matrix[...], block_of(up_ref, n, b))
-            block_store(rows, n, b, value.astype(BF16))
-        for copy in made[2 * n * GROUPS : 2 * (n + 1) * GROUPS]:
+            cells = block_of(up_ref, PER * n, b)
+            right = jnp.concatenate([back_ref[:, WIDE * n : WIDE * (n + 1)], cells], axis=0)
+            block_store(rows, PER * n, b, dot(left[b], right).astype(BF16))
+        for copy in made[PER * n * GROUPS : PER * (n + 1) * GROUPS]:
             copy.start()
     for copy in made:
         copy.wait()
 
 
+def turn(ref, b, tiles):
+    value = ref[...].astype(F32)
+    for s in range(Q3):
+        for j in range(GROUPS):
+            at = (s * GROUPS + j) * KY
+            turned = value[at : at + KY].T
+            for c in range(4):
+                tiles[4 * j + c, s, b] = turned[32 * c : 32 * c + KX]
+
+
+PAIR = 4
+
+
 def outer_kernel(*refs):
-    specs, out_ref, first, second = refs[:8], refs[8], refs[9], refs[10]
+    out_ref, first, second = refs[8:]
 
     @pl.when(pl.program_id(0) == 0)
     def _():
         for b in range(4):
-            for ref, tiles in ((specs[b], first), (specs[4 + b], second)):
-                value = ref[...].astype(F32)
-                for s in range(Q3):
-                    for j in range(GROUPS):
-                        at = (s * GROUPS + j) * KY
-                        turned = value[at : at + KY].T
-                        for c in range(4):
-                            tiles[4 * j + c, s, b] = turned[32 * c : 32 * c + KX]
-
-    c = pl.program_id(0)
+            turn(refs[b], b, first)
+            turn(refs[4 + b], b, second)
+
+    c = pl.program_id(0) * PAIR
     for s in range(Q3):
-        own = [first[c, s, b] for b in range(4)]
-
-        def one(o, carry):
-            terms = [own[b] * second[o, s, b] for b in range(4)]
-            out_ref[0, o, s] = (terms[0] + terms[2]) + (terms[1] + terms[3])
-            return carry
-
-        lax.fori_loop(0, C, one, 0, unroll=4)
-
-
-def call(kernel, out, in_specs, scratch, **more):
+        own = [[first[c + i, s, b] for b in range(4)] for i in range(PAIR)]
+        for o in range(C):
+            other = [second[o, s, b] for b in range(4)]
+            for i in range(PAIR):
+                terms = [own[i][b] * other[b] for b in range(4)]
+                out_ref[i, o, s] = (terms[0] + terms[2]) + (terms[1] + terms[3])
+
+
+def small_kernel(recv_ref, small_ref, stage):
+    stage[...] = recv_ref[pl.ds(0, 24)].astype(F32)
+    small_ref[...] = join_three(stage[:, CHUNK - 1, :])
+
+
+def call(kernel, out, in_specs, scratch, limit=12, **more):
     return pl.pallas_call(
         kernel,
         out_shape=out,
         in_specs=in_specs,
         scratch_shapes=scratch,
-        compiler_params=pltpu.CompilerParams(vmem_limit_bytes=40 * MIB),
+        compiler_params=pltpu.CompilerParams(vmem_limit_bytes=limit * MIB),
         **more,
     )
 
@@ -394,7 +450,8 @@
     cells = shape((TILES, GROUPS, CX, 4, CY, 128), BF16)
     rows = shape((TILES, ROWS, 128), BF16)
     stage = pltpu.VMEM((DEV * CHUNK, 128), F32)
-    sems = pltpu.SemaphoreType.DMA((TILES, GROUPS))
+    dma = lambda *count: pltpu.SemaphoreType.DMA(count)
+    sems = dma(TILES, GROUPS)
     field_t = jnp.transpose(field[0], (0, 2, 1, 3))
     cot_t = jnp.transpose(cotangent[0], (0, 2, 1, 3))
     weight_t = jnp.transpose(spectral_weight, (2, 3, 4, 0, 1))
@@ -403,24 +460,31 @@
         return lax.all_to_all(value, ("gx", "gy"), 0, 0, tiled=True)
 
     send, field_rows = call(
-        analyze_kernel, (chunks, cells), [ANY, VMEM], [pltpu.VMEM((ROWS, 256), F32), stage, sems],
-        out_specs=(VMEM, VMEM),
+        analyze_kernel, (chunks, cells), [HBM, HBM],
+        [pltpu.VMEM(cells.shape, BF16), pltpu.VMEM((NP, 256), BF16),
+         pltpu.VMEM((ROWS, 256), F32), stage, sems, dma(4), dma(4)],
+        out_specs=(VMEM, HBM), limit=62,
     )(field_t, table["zt_ahead"])
     recv = exchange(send)
-    weight = call(
-        weights_kernel, shape((C, SPEC, 128), BF16), [VMEM], [], out_specs=VMEM,
-    )(weight_t)
-    send, spec, cot_rows = call(
-        mix_kernel, (chunks, modes, cells), [VMEM, VMEM, ANY] + [VMEM] * 4,
-        [pltpu.VMEM((SPEC, 128), F32), sems], out_specs=(VMEM,) * 3,
-    )(recv, weight, cot_t, table["x_ahead"], table["y_ahead"], table["y_back"], table["x_back"])
+    weight, cot_rows = call(
+        weights_kernel, (shape((C, SPEC, 128), BF16), cells), [VMEM, HBM], [sems],
+        out_specs=(VMEM,) * 2, limit=60,
+    )(weight_t, cot_t)
+    send, spec = call(
+        mix_kernel, (chunks, modes), [VMEM] * 6, [pltpu.VMEM((SPEC, 128), F32)],
+        out_specs=(VMEM,) * 2,
+    )(recv, weight, table["x_ahead"], table["y_ahead"], table["y_back"], table["x_back"])
     recv = exchange(send)
     specs = around(spec)
+    left = pltpu.VMEM((CX // XB, BLOCK, NQ + BLOCK), BF16)
+    held = pltpu.VMEM(rows.shape, BF16)
+    back = pltpu.VMEM((NQ, NP), BF16)
+    recv, *specs = lax.optimization_barrier((recv, *specs))
     send, up = call(
-        point_kernel, (chunks, rows), [VMEM] * 8,
-        [stage, pltpu.VMEM((ROWS, Q3 * DEV), BF16), pltpu.VMEM((ROWS, 256), F32),
-         pltpu.VMEM((BLOCK, BLOCK), F32), pltpu.VMEM((BLOCK, BLOCK), BF16)],
-        out_specs=(VMEM,) * 2,
+        point_kernel, (chunks, rows), [VMEM, HBM, HBM, VMEM, VMEM, VMEM, HBM, HBM],
+        [held, held, back, pltpu.VMEM((NP, 256), BF16), held, stage, left,
+         pltpu.VMEM((ROWS, 256), F32), pltpu.VMEM((BLOCK, BLOCK), F32), dma(2), dma(3, STEPS)],
+        out_specs=(VMEM, HBM), limit=60,
     )(recv, field_rows, cot_rows, bypass_weight, table["channel"], table["same"],
       table["zt_back"], table["zt_ahead"])
     recv = exchange(send)
@@ -430,23 +494,31 @@
       table["x_back"])
     recv = exchange(send)
     specs_up = around(spec_up)
-    grad_field, small = call(
-        final_kernel, (shape((CX, C, CY, NP), BF16), shape((24, 128), F32)), [VMEM] * 6,
-        [stage, pltpu.VMEM((ROWS, Q3 * DEV), BF16), pltpu.VMEM((BLOCK, BLOCK), BF16),
-         pltpu.VMEM((TILES, GROUPS, CX, 4, CY, 128), BF16), sems],
-        out_specs=(ANY, VMEM),
-    )(recv, up, bypass_weight, table["channel"], table["same"], table["zt_back"])
-    smalls = around(small)
-    grad_bypass = ((smalls[0] + smalls[2]) + (smalls[1] + smalls[3]))[:C, :C]
     grad_spectral = pl.pallas_call(
         outer_kernel,
-        grid=(C,),
+        grid=(C // PAIR,),
         out_shape=shape((C, C, Q3, KX, KY), F32),
-        in_specs=[pl.BlockSpec((SPEC, 128), lambda c: (0, 0))] * 8,
-        out_specs=pl.BlockSpec((1, C, Q3, KX, KY), lambda c: (c, 0, 0, 0, 0)),
+        in_specs=[VMEM] * 8,
+        out_specs=pl.BlockSpec((PAIR, C, Q3, KX, KY), lambda c: (c, 0, 0, 0, 0)),
         scratch_shapes=[pltpu.VMEM((C, Q3, 4, KX, KY), F32)] * 2,
-        compiler_params=pltpu.CompilerParams(vmem_limit_bytes=40 * MIB),
+        compiler_params=pltpu.CompilerParams(vmem_limit_bytes=24 * MIB),
+        cost_estimate=pl.CostEstimate(
+            flops=10**9, bytes_accessed=10**8, transcendentals=0
+        ),
     )(*specs, *specs_up)
+    recv, grad_spectral = lax.optimization_barrier((recv, grad_spectral))
+    small = call(
+        small_kernel, shape((24, 128), F32), [VMEM], [pltpu.VMEM((24, CHUNK, 128), F32)],
+        out_specs=VMEM,
+    )(recv)
+    smalls = around(small)
+    grad_field = call(
+        final_kernel, shape((CX, C, CY, NP), BF16), [VMEM, HBM, VMEM, VMEM, VMEM, HBM],
+        [held, back, stage, left, pltpu.VMEM(cells.shape, BF16), pltpu.SemaphoreType.DMA,
+         dma(STEPS), sems],
+        out_specs=HBM, limit=60,
+    )(recv, up, bypass_weight, table["channel"], table["same"], table["zt_back"])
+    grad_bypass = ((smalls[0] + smalls[2]) + (smalls[1] + smalls[3]))[:C, :C]
     return (
         jnp.transpose(grad_field, (0, 2, 1, 3))[None],
         jnp.transpose(grad_spectral, (3, 4, 0, 1, 2)),

time: 135 us -> 124 us (0.919)
  blocking collectives: 35.7 us -> 21.3 us
  local copies, waits for them, and re-layouts: 16 us -> 2.25 us
  waiting for transfers between devices: 10.2 us -> 16.9 us
  Pallas kernels: 40.2 us -> 46.1 us
  starting transfers between devices: 30.9 us -> 34.2 us
    all_to_all x2 -> x1, blocking collectives: 35.7 us -> 21.3 us  [exchange(): return lax.all_to_all(value, ('gx', 'gy'), 0, 0, tiled=True)]
    unnamed x50 -> x18, local copies, waits for them, and re-layouts: 16 us -> 2.25 us
    ppermute x9, waiting for transfers between devices: 0.02 us -> 13.4 us  [around(): lax.ppermute(value, 'dp', [(i, (i + k) % 4) for i in range(4)])]
    all_to_all x2 -> x3, starting transfers between devices: 19.1 us -> 27.3 us  [exchange(): return lax.all_to_all(value, ('gx', 'gy'), 0, 0, tiled=True)]
    all_to_all x2 -> x3, waiting for transfers between devices: 10.2 us -> 3.55 us  [exchange(): return lax.all_to_all(value, ('gx', 'gy'), 0, 0, tiled=True)]
    pallas_call x6 -> x7, Pallas kernels: 38.8 us -> 44 us  [the longest x1 11.5 us: body(): call(point_kernel, (chunks, rows), [VMEM, HBM, HBM, VMEM, VMEM, VMEM, HBM...]
    ppermute x9, starting transfers between devices: 11.7 us -> 6.87 us  [around(): lax.ppermute(value, 'dp', [(i, (i + k) % 4) for i in range(4)])]
  transfers between devices with their start and end apart: 11 -> 12, of which waited for: 2 -> 8; matrix products, arithmetic and copies ran while one was open for 0% -> 0% of each run, Pallas kernels for 15% -> 21%
where the time goes in v2:
time: 124 us; the launch traced here: 122 us
  Pallas kernels  46.1 us (37%)
  starting transfers between devices  34.2 us (28%)
  blocking collectives  21.3 us (17%)
  waiting for transfers between devices  16.9 us (14%)
  local copies, waits for them, and re-layouts  2.25 us (2%)
    all_to_all x3, starting transfers between devices, exchange(): return lax.all_to_all(value, ('gx', 'gy'), 0, 0, tiled=True)  27.3 us
    all_to_all x1, blocking collectives, exchange(): return lax.all_to_all(value, ('gx', 'gy'), 0, 0, tiled=True)  21.3 us
    ppermute x9, waiting for transfers between devices, around(): lax.ppermute(value, 'dp', [(i, (i + k) % 4) for i in range(4)])  13.4 us
    pallas_call x1, Pallas kernels, body(): call(point_kernel, (chunks, rows), [VMEM, HBM, HBM, VMEM, VMEM, VMEM, HBM...  11.5 us
    pallas_call x1, Pallas kernels, body(): call(weights_kernel, (shape((C, SPEC, 128), BF16), cells), [VMEM, HBM], [...  9.87 us
    pallas_call x1, Pallas kernels, body(): pl.pallas_call(outer_kernel, grid=(C // PAIR,), out_shape=shape((C, C, Q3...  7.98 us
    pallas_call x1, Pallas kernels, body(): call(final_kernel, shape((CX, C, CY, NP), BF16), [VMEM, HBM, VMEM, VMEM,...  7.24 us
    ppermute x9, starting transfers between devices, around(): lax.ppermute(value, 'dp', [(i, (i + k) % 4) for i in range(4)])  6.87 us
  transfers between devices with their start and end apart: 12, of which 8 were waited for; matrix products, arithmetic and copies ran while one was open for 0% of the time, Pallas kernels for 21%

profile of v2, /device:TPU:1, one launch (start us, length us, event | category | flops | bytes accessed | tf_op | source)
XLA Modules:
  0.0 122.2 jit_solution(8208596661441477558)
XLA Ops:
  0.6 5.1 %shard_map.148 = (bf16[64,16,128]{2,1,0:T(8,128)(2,1)}, bf16[16,5,16,4,2,128]{5,4,3,2,1,0:T(2,128)(2,1)}) custom-call(bf16[16,20,2,2048]{3,2,1,0:T(2,128)(2,1)} %bitcast.13, bf16[2048,256]{1,0:T(8,128)(2,1)} %constant.18.clone.zt_hbm.ahead_hbm), custom_call_target="tpu_custom_call" | custom-call | tf_op jit(solution)/shard_map/pallas_call | solution.py:462
  5.7 13.0 %all-to-all-start = ((bf16[64,16,128]{2,1,0:T(8,128)(2,1)}), bf16[64,16,128]{2,1,0:T(8,128)(2,1)S(1)}, u32[]{:S(2)}, u32[]{:S(2)}) async-start(bf16[64,16,128]{2,1,0:T(8,128)(2,1)} %get-tuple-element.20), calls=%async_computation | async-start | bytes 524288 | tf_op jit(solution)/shard_map/all_to_all | solution.py:460
  18.7 0.0 copy-start.3
  18.8 0.0 copy-start.4
  18.8 0.0 copy-start.5
  18.8 0.0 copy-start.6
  18.8 9.9 %shard_map.149 = (bf16[20,360,128]{2,1,0:T(8,128)(2,1)}, bf16[16,5,16,4,2,128]{5,4,3,2,1,0:T(2,128)(2,1)}) custom-call(bf16[20,20,3,24,24]{4,3,2,1,0:T(8,128)(2,1)} %bitcast.12, bf16[16,20,2,2048]{3,2,1,0:T(2,128)(2,1)} %bitcast.15), custom_call_target="tpu_custom_call" | custom-call | tf_op jit(solution)/shard_map/pallas_call | solution.py:469
  28.7 2.1 %all-to-all-done.recv_ref = bf16[64,16,128]{2,1,0:T(8,128)(2,1)S(1)} async-done(((bf16[64,16,128]{2,1,0:T(8,128)(2,1)}), bf16[64,16,128]{2,1,0:T(8,128)(2,1)S(1)}, u32[]{:S(2)}, u32[]{:S(2)}) %all-to-all-start) | async-done | bytes 262176 | tf_op jit(solution)/shard_map/all_to_all | solution.py:460
  30.7 0.0 copy-done.3
  30.7 0.0 copy-done.4
  30.7 0.0 copy-done.5
  30.8 0.0 copy-done.6
  30.8 0.0 copy-start
  30.8 1.5 %copy-done = bf16[20,360,128]{2,1,0:T(8,128)(2,1)S(1)} copy-done((bf16[20,360,128]{2,1,0:T(8,128)(2,1)S(1)}, bf16[20,360,128]{2,1,0:T(8,128)(2,1)}, u32[]{:S(2)}) %copy-start) | copy-done | bytes 1843224
  32.3 2.2 %shard_map.150 = (bf16[64,16,128]{2,1,0:T(8,128)(2,1)}, bf16[360,128]{1,0:T(8,128)(2,1)S(1)}) custom-call(bf16[64,16,128]{2,1,0:T(8,128)(2,1)S(1)} %all-to-all-done.recv_ref, bf16[20,360,128]{2,1,0:T(8,128)(2,1)S(1)} %copy-done, bf16[512,256]{1,0:T(8,128)(2,1)S(1)} %copy-done.6, bf16[360,512]{1,0:T(8,128)(2,1)S(1)} %copy-done.4, ...), custom_call_target="tpu_custom_call" | custom-call | tf_op jit(solution)/shard_map/pallas_call | solution.py:473
  34.5 8.3 %all-to-all-start.1 = ((bf16[64,16,128]{2,1,0:T(8,128)(2,1)}), bf16[64,16,128]{2,1,0:T(8,128)(2,1)S(1)}, u32[]{:S(2)}, u32[]{:S(2)}) async-start(bf16[64,16,128]{2,1,0:T(8,128)(2,1)} %get-tuple-element.22), calls=%async_computation.1 | async-start | bytes 524288 | tf_op jit(solution)/shard_map/all_to_all | solution.py:460
  42.7 2.8 %collective-permute-start.2 = (bf16[360,128]{1,0:T(8,128)(2,1)S(1)}, bf16[360,128]{1,0:T(8,128)(2,1)S(1)}, u32[]{:S(2)}, u32[]{:S(2)}) collective-permute-start(bf16[360,128]{1,0:T(8,128)(2,1)S(1)} %get-tuple-element.29.refs_0_), channel_id=1, source_target_pairs={{0,192},{64,0},{128,64},{192,128},{1,193},{65,1},{129,65},{193,129... | collective-permute-start | bytes 276488 | tf_op jit(solution)/shard_map/ppermute | solution.py:441
  45.5 0.3 collective-permute-start.1
  45.9 0.7 collective-permute-start
  46.6 0.5 collective-permute-done.2.refs_3_
  47.1 3.6 %collective-permute-done.1.refs_2_ = bf16[360,128]{1,0:T(8,128)(2,1)S(1)} collective-permute-done((bf16[360,128]{1,0:T(8,128)(2,1)S(1)}, bf16[360,128]{1,0:T(8,128)(2,1)S(1)}, u32[]{:S(2)}, u32[]{:S(2)}) %collective-permute-start.1) | collective-permute-done | bytes 92192 | tf_op jit(solution)/shard_map/ppermute | solution.py:441
  50.8 2.5 %collective-permute-done.refs_1_ = bf16[360,128]{1,0:T(8,128)(2,1)S(1)} collective-permute-done((bf16[360,128]{1,0:T(8,128)(2,1)S(1)}, bf16[360,128]{1,0:T(8,128)(2,1)S(1)}, u32[]{:S(2)}, u32[]{:S(2)}) %collective-permute-start) | collective-permute-done | bytes 92192 | tf_op jit(solution)/shard_map/ppermute | solution.py:441
  53.3 1.5 %all-to-all-done.1.recv_ref = bf16[64,16,128]{2,1,0:T(8,128)(2,1)S(1)} async-done(((bf16[64,16,128]{2,1,0:T(8,128)(2,1)}), bf16[64,16,128]{2,1,0:T(8,128)(2,1)S(1)}, u32[]{:S(2)}, u32[]{:S(2)}) %all-to-all-start.1) | async-done | bytes 262176 | tf_op jit(solution)/shard_map/all_to_all | solution.py:460
  54.7 0.0 copy-start.8
  54.7 0.7 copy-done.8
  55.5 0.0 copy-start.1
  55.5 0.0 copy-start.7
  55.5 11.5 %shard_map.151 = (bf16[64,16,128]{2,1,0:T(8,128)(2,1)}, bf16[16,640,128]{2,1,0:T(8,128)(2,1)}) custom-call(bf16[64,16,128]{2,1,0:T(8,128)(2,1)} %copy-done.8, bf16[16,5,16,4,2,128]{5,4,3,2,1,0:T(2,128)(2,1)} %get-tuple-element.25.field_hbm, bf16[16,5,16,4,2,128]{5,4,3,2,1,0:T(2,128)(2,1)} %get-tuple-element.26.cot_hbm, bf16[20,20]{1,0:T(8,128)(2,1)} %bypass_ref.3, ...), custom_call_target="tpu_custom_call" | custom-call | tf_op jit(solution)/shard_map/pallas_call | solution.py:483
  67.0 21.3 %all_to_all.20.recv_ref = bf16[64,16,128]{2,1,0:T(8,128)(2,1)S(1)} all-to-all(bf16[64,16,128]{2,1,0:T(8,128)(2,1)} %get-tuple-element.27), channel_id=1, replica_groups=mesh['dp'=4,'gx'=4,'gy'=16] {'gx','gy'}, dimensions={0} | all-to-all | bytes 524288 | tf_op jit(solution)/shard_map/all_to_all | solution.py:460
  88.3 0.0 copy-done.1
  88.3 0.0 copy-done.7
  88.3 2.1 %shard_map.152 = (bf16[64,16,128]{2,1,0:T(8,128)(2,1)}, bf16[360,128]{1,0:T(8,128)(2,1)S(1)}) custom-call(bf16[64,16,128]{2,1,0:T(8,128)(2,1)S(1)} %all_to_all.20.recv_ref, bf16[20,360,128]{2,1,0:T(8,128)(2,1)S(1)} %copy-done.1, bf16[128,512]{1,0:T(8,128)(2,1)S(1)} %copy-done.7, bf16[512,256]{1,0:T(8,128)(2,1)S(1)} %copy-done.6, ...), custom_call_target="tpu_custom_call" | custom-call | tf_op jit(solution)/shard_map/pallas_call | solution.py:491
  90.4 6.0 %all-to-all-start.3 = ((bf16[64,16,128]{2,1,0:T(8,128)(2,1)}), bf16[64,16,128]{2,1,0:T(8,128)(2,1)S(1)}, u32[]{:S(2)}, u32[]{:S(2)}) async-start(bf16[64,16,128]{2,1,0:T(8,128)(2,1)} %get-tuple-element.28), calls=%async_computation.3 | async-start | bytes 524288 | tf_op jit(solution)/shard_map/all_to_all | solution.py:460
  96.4 0.4 collective-permute-start.5
  96.8 0.3 collective-permute-start.4
  97.2 0.8 collective-permute-start.3
  98.0 2.3 %collective-permute-done.5.refs_7_ = bf16[360,128]{1,0:T(8,128)(2,1)S(1)} collective-permute-done((bf16[360,128]{1,0:T(8,128)(2,1)S(1)}, bf16[360,128]{1,0:T(8,128)(2,1)S(1)}, u32[]{:S(2)}, u32[]{:S(2)}) %collective-permute-start.5) | collective-permute-done | bytes 92192 | tf_op jit(solution)/shard_map/ppermute | solution.py:441
  100.3 1.7 %collective-permute-done.4.refs_6_ = bf16[360,128]{1,0:T(8,128)(2,1)S(1)} collective-permute-done((bf16[360,128]{1,0:T(8,128)(2,1)S(1)}, bf16[360,128]{1,0:T(8,128)(2,1)S(1)}, u32[]{:S(2)}, u32[]{:S(2)}) %collective-permute-start.4) | collective-permute-done | bytes 92192 | tf_op jit(solution)/shard_map/ppermute | solution.py:441
  102.0 2.7 %collective-permute-done.3.refs_5_ = bf16[360,128]{1,0:T(8,128)(2,1)S(1)} collective-permute-done((bf16[360,128]{1,0:T(8,128)(2,1)S(1)}, bf16[360,128]{1,0:T(8,128)(2,1)S(1)}, u32[]{:S(2)}, u32[]{:S(2)}) %collective-permute-start.3) | collective-permute-done | bytes 92192 | tf_op jit(solution)/shard_map/ppermute | solution.py:441
  104.7 8.0 %shard_map.153 = f32[20,20,3,24,24]{4,3,2,1,0:T(8,128)} custom-call(bf16[360,128]{1,0:T(8,128)(2,1)S(1)} %get-tuple-element.29.refs_0_, bf16[360,128]{1,0:T(8,128)(2,1)S(1)} %collective-permute-done.refs_1_, bf16[360,128]{1,0:T(8,128)(2,1)S(1)} %collective-permute-done.1.refs_2_, bf16[360,128]{1,0:T(8,128)(2,1)S(1)} %collective-permute-done.2.refs_3_, ...), custom_call_target="tpu_custom_call" | custom-call | flops 1000000000 | bytes 100000000 | tf_op jit(solution)/shard_map/pallas_call | solution.py:497
  112.7 0.0 all-to-all-done.3.recv_ref
  112.7 0.0 copy-start.2
  112.7 0.1 shard_map.155
  112.8 0.0 collective-permute-start.8
  112.8 1.5 %collective-permute-start.7 = (f32[24,128]{1,0:T(8,128)S(1)}, f32[24,128]{1,0:T(8,128)S(1)}, u32[]{:S(2)}, u32[]{:S(2)}) collective-permute-start(f32[24,128]{1,0:T(8,128)S(1)} %shard_map.155), channel_id=1, source_target_pairs={{0,64},{64,128},{128,192},{192,0},{1,65},{65,129},{129,193},{193,1... | collective-permute-start | bytes 36872 | tf_op jit(solution)/shard_map/ppermute | solution.py:441
  114.3 0.0 collective-permute-start.6
  114.3 0.0 copy-done.2
  114.3 7.2 %shard_map.154 = bf16[16,20,2,2048]{3,2,1,0:T(2,128)(2,1)} custom-call(bf16[64,16,128]{2,1,0:T(8,128)(2,1)} %copy-done.2, bf16[16,640,128]{2,1,0:T(8,128)(2,1)} %get-tuple-element.35.up_hbm, bf16[20,20]{1,0:T(8,128)(2,1)} %bypass_ref.3, bf16[320,20]{1,0:T(8,128)(2,1)} %constant.25.clone.channel_ref, bf16[320,384]{1,0:T(8,128)(2,1)} %constant.26.clone.same_ref, ...), custom_call_target="tpu_custom_call" | custom-call | tf_op jit(solution)/shard_map/pallas_call | solution.py:515
  121.5 0.0 collective-permute-done.8
  121.5 0.0 collective-permute-done.7
  121.5 0.0 collective-permute-done.6
  121.5 0.6 fusion
Async XLA Ops:
  5.7 25.0 %all-to-all-start = ((bf16[64,16,128]{2,1,0:T(8,128)(2,1)}), bf16[64,16,128]{2,1,0:T(8,128)(2,1)S(1)}, u32[]{:S(2)}, u32[]{:S(2)}) async-start(bf16[64,16,128]{2,1,0:T(8,128)(2,1)} %get-tuple-element.20), calls=%async_computation | async-start | bytes 524288 | tf_op jit(solution)/shard_map/all_to_all | solution.py:460
  18.7 12.0 %copy-start.3 = (bf16[512,360]{1,0:T(8,128)(2,1)S(1)}, bf16[512,360]{1,0:T(8,128)(2,1)}, u32[]{:S(2)}) copy-start(bf16[512,360]{1,0:T(8,128)(2,1)} %constant.23.clone.yb_ref) | copy-start | bytes 1105924
  18.8 12.0 %copy-start.4 = (bf16[360,512]{1,0:T(8,128)(2,1)S(1)}, bf16[360,512]{1,0:T(8,128)(2,1)}, u32[]{:S(2)}) copy-start(bf16[360,512]{1,0:T(8,128)(2,1)} %constant.22.clone.ya_ref) | copy-start | bytes 1105924
  18.8 12.0 %copy-start.5 = (bf16[256,512]{1,0:T(8,128)(2,1)S(1)}, bf16[256,512]{1,0:T(8,128)(2,1)}, u32[]{:S(2)}) copy-start(bf16[256,512]{1,0:T(8,128)(2,1)} %constant.21.clone.xb_ref) | copy-start | bytes 786436
  18.8 12.0 %copy-start.6 = (bf16[512,256]{1,0:T(8,128)(2,1)S(1)}, bf16[512,256]{1,0:T(8,128)(2,1)}, u32[]{:S(2)}) copy-start(bf16[512,256]{1,0:T(8,128)(2,1)} %constant.20.clone.xa_ref) | copy-start | bytes 786436
  30.8 1.5 %copy-start = (bf16[20,360,128]{2,1,0:T(8,128)(2,1)S(1)}, bf16[20,360,128]{2,1,0:T(8,128)(2,1)}, u32[]{:S(2)}) copy-start(bf16[20,360,128]{2,1,0:T(8,128)(2,1)} %get-tuple-element.21.weight_ref) | copy-start | bytes 5529604
  34.5 20.3 %all-to-all-start.1 = ((bf16[64,16,128]{2,1,0:T(8,128)(2,1)}), bf16[64,16,128]{2,1,0:T(8,128)(2,1)S(1)}, u32[]{:S(2)}, u32[]{:S(2)}) async-start(bf16[64,16,128]{2,1,0:T(8,128)(2,1)} %get-tuple-element.22), calls=%async_computation.1 | async-start | bytes 524288 | tf_op jit(solution)/shard_map/all_to_all | solution.py:460
  42.7 4.4 %collective-permute-start.2 = (bf16[360,128]{1,0:T(8,128)(2,1)S(1)}, bf16[360,128]{1,0:T(8,128)(2,1)S(1)}, u32[]{:S(2)}, u32[]{:S(2)}) collective-permute-start(bf16[360,128]{1,0:T(8,128)(2,1)S(1)} %get-tuple-element.29.refs_0_), channel_id=1, source_target_pairs={{0,192},{64,0},{128,64},{192,128},{1,193},{65,1},{129,65},{193,129... | collective-permute-start | bytes 276488 | tf_op jit(solution)/shard_map/ppermute | solution.py:441
  45.5 5.2 %collective-permute-start.1 = (bf16[360,128]{1,0:T(8,128)(2,1)S(1)}, bf16[360,128]{1,0:T(8,128)(2,1)S(1)}, u32[]{:S(2)}, u32[]{:S(2)}) collective-permute-start(bf16[360,128]{1,0:T(8,128)(2,1)S(1)} %get-tuple-element.29.refs_0_), channel_id=1, source_target_pairs={{0,128},{64,192},{128,0},{192,64},{1,129},{65,193},{129,1},{193,65... | collective-permute-start | bytes 276488 | tf_op jit(solution)/shard_map/ppermute | solution.py:441
  45.9 7.4 %collective-permute-start = (bf16[360,128]{1,0:T(8,128)(2,1)S(1)}, bf16[360,128]{1,0:T(8,128)(2,1)S(1)}, u32[]{:S(2)}, u32[]{:S(2)}) collective-permute-start(bf16[360,128]{1,0:T(8,128)(2,1)S(1)} %get-tuple-element.29.refs_0_), channel_id=1, source_target_pairs={{0,64},{64,128},{128,192},{192,0},{1,65},{65,129},{129,193},{193,1... | collective-permute-start | bytes 276488 | tf_op jit(solution)/shard_map/ppermute | solution.py:441
  54.7 0.7 copy-start.8
  55.5 32.9 %copy-start.1 = (bf16[20,360,128]{2,1,0:T(8,128)(2,1)S(1)}, bf16[20,360,128]{2,1,0:T(8,128)(2,1)}, u32[]{:S(2)}) copy-start(bf16[20,360,128]{2,1,0:T(8,128)(2,1)} %get-tuple-element.21.weight_ref) | copy-start | bytes 5529604
  55.5 32.9 %copy-start.7 = (bf16[128,512]{1,0:T(8,128)(2,1)S(1)}, bf16[128,512]{1,0:T(8,128)(2,1)}, u32[]{:S(2)}) copy-start(bf16[128,512]{1,0:T(8,128)(2,1)} %constant.24.clone.spread_ref) | copy-start | bytes 393220
  90.4 22.3 %all-to-all-start.3 = ((bf16[64,16,128]{2,1,0:T(8,128)(2,1)}), bf16[64,16,128]{2,1,0:T(8,128)(2,1)S(1)}, u32[]{:S(2)}, u32[]{:S(2)}) async-start(bf16[64,16,128]{2,1,0:T(8,128)(2,1)} %get-tuple-element.28), calls=%async_computation.3 | async-start | bytes 524288 | tf_op jit(solution)/shard_map/all_to_all | solution.py:460
  96.4 3.9 %collective-permute-start.5 = (bf16[360,128]{1,0:T(8,128)(2,1)S(1)}, bf16[360,128]{1,0:T(8,128)(2,1)S(1)}, u32[]{:S(2)}, u32[]{:S(2)}) collective-permute-start(bf16[360,128]{1,0:T(8,128)(2,1)S(1)} %get-tuple-element.33.refs_4_), channel_id=1, source_target_pairs={{0,192},{64,0},{128,64},{192,128},{1,193},{65,1},{129,65},{193,129... | collective-permute-start | bytes 276488 | tf_op jit(solution)/shard_map/ppermute | solution.py:441
  96.8 5.2 %collective-permute-start.4 = (bf16[360,128]{1,0:T(8,128)(2,1)S(1)}, bf16[360,128]{1,0:T(8,128)(2,1)S(1)}, u32[]{:S(2)}, u32[]{:S(2)}) collective-permute-start(bf16[360,128]{1,0:T(8,128)(2,1)S(1)} %get-tuple-element.33.refs_4_), channel_id=1, source_target_pairs={{0,128},{64,192},{128,0},{192,64},{1,129},{65,193},{129,1},{193,65... | collective-permute-start | bytes 276488 | tf_op jit(solution)/shard_map/ppermute | solution.py:441
  97.2 7.6 %collective-permute-start.3 = (bf16[360,128]{1,0:T(8,128)(2,1)S(1)}, bf16[360,128]{1,0:T(8,128)(2,1)S(1)}, u32[]{:S(2)}, u32[]{:S(2)}) collective-permute-start(bf16[360,128]{1,0:T(8,128)(2,1)S(1)} %get-tuple-element.33.refs_4_), channel_id=1, source_target_pairs={{0,64},{64,128},{128,192},{192,0},{1,65},{65,129},{129,193},{193,1... | collective-permute-start | bytes 276488 | tf_op jit(solution)/shard_map/ppermute | solution.py:441
  112.7 1.6 %copy-start.2 = (bf16[64,16,128]{2,1,0:T(8,128)(2,1)}, bf16[64,16,128]{2,1,0:T(8,128)(2,1)S(1)}, u32[]{:S(2)}) copy-start(bf16[64,16,128]{2,1,0:T(8,128)(2,1)S(1)} %all-to-all-done.3.recv_ref) | copy-start | bytes 786436
  112.8 8.7 %collective-permute-start.8 = (f32[24,128]{1,0:T(8,128)S(1)}, f32[24,128]{1,0:T(8,128)S(1)}, u32[]{:S(2)}, u32[]{:S(2)}) collective-permute-start(f32[24,128]{1,0:T(8,128)S(1)} %shard_map.155), channel_id=1, source_target_pairs={{0,192},{64,0},{128,64},{192,128},{1,193},{65,1},{129,65},{193,129... | collective-permute-start | bytes 36872 | tf_op jit(solution)/shard_map/ppermute | solution.py:441
  112.8 8.7 %collective-permute-start.7 = (f32[24,128]{1,0:T(8,128)S(1)}, f32[24,128]{1,0:T(8,128)S(1)}, u32[]{:S(2)}, u32[]{:S(2)}) collective-permute-start(f32[24,128]{1,0:T(8,128)S(1)} %shard_map.155), channel_id=1, source_target_pairs={{0,64},{64,128},{128,192},{192,0},{1,65},{65,129},{129,193},{193,1... | collective-permute-start | bytes 36872 | tf_op jit(solution)/shard_map/ppermute | solution.py:441
  114.3 7.3 %collective-permute-start.6 = (f32[24,128]{1,0:T(8,128)S(1)}, f32[24,128]{1,0:T(8,128)S(1)}, u32[]{:S(2)}, u32[]{:S(2)}) collective-permute-start(f32[24,128]{1,0:T(8,128)S(1)} %shard_map.155), channel_id=1, source_target_pairs={{0,128},{64,192},{128,0},{192,64},{1,129},{65,193},{129,1},{193,65... | collective-permute-start | bytes 36872 | tf_op jit(solution)/shard_map/ppermute | solution.py:441

commit v3 on v2

--- a/solution.py
+++ b/solution.py
@@ -34,7 +34,7 @@
 SPEC = Q3 * GROUPS * KY
 XB = 8
 PART = 4 * XB * CY
-WIDE = 512
+WIDE = 256
 STEPS = NP // WIDE
 PER = WIDE // 128
 NQ = Q3 * DEV
@@ -79,9 +79,7 @@
         "zt_ahead": ahead,
         "zt_back": by_slot.T,
         "x_ahead": x_ahead,
-        "x_back": x_ahead.T,
         "y_ahead": y_ahead,
-        "y_back": y_ahead.T,
         "spread": spread,
         "channel": channel,
         "same": np.concatenate([np.zeros((BLOCK, 64)), cell @ cell.T], axis=1),
@@ -151,7 +149,7 @@
     field_ref, zt_hbm, send_ref, rows_hbm, rows_ref, zt_ref, coeff, stage, sems, zt_sems, out_sems,
 ):
     made = copies(field_ref, rows_ref, sems)
-    step = 4
+    step = 2
     zt_made = []
     for first in range(0, TILES, step):
         part = pl.ds(128 * first, 128 * step)
@@ -208,10 +206,10 @@
 
 
 def from_modes(modes, y_ref, x_ref):
-    tall = dot(y_ref[...], modes.astype(BF16)).astype(BF16)
+    tall = dot(y_ref[...], modes.astype(BF16), ((0,), (0,))).astype(BF16)
     half = PY * CHUNK
     wide = jnp.concatenate([tall[:half], tall[half:]], axis=1)
-    return dot(wide, x_ref[...])
+    return dot(wide, x_ref[...], ((1,), (1,)))
 
 
 def write_chunks(values, send_ref):
@@ -221,7 +219,7 @@
 
 
 def mix_kernel(
-    recv_ref, weight_ref, xa_ref, ya_ref, yb_ref, xb_ref, send_ref, spec_ref, modes,
+    recv_ref, weight_ref, xa_ref, ya_ref, send_ref, spec_ref, modes,
 ):
     spec = to_modes(recv_ref, xa_ref, ya_ref)
     spec_ref[...] = spec
@@ -244,11 +242,11 @@
             total = jnp.where(group == o4, summed, total)
         for s in range(Q3):
             modes[pl.ds((s * GROUPS + jo) * KY, KY), :] = total[s * KY : (s + 1) * KY]
-    write_chunks(from_modes(modes[...], yb_ref, xb_ref), send_ref)
+    write_chunks(from_modes(modes[...], ya_ref, xa_ref), send_ref)
 
 
 def mix_back_kernel(
-    recv_ref, weight_ref, spread_ref, xa_ref, ya_ref, yb_ref, xb_ref, send_ref, spec_ref, stage,
+    recv_ref, weight_ref, spread_ref, xa_ref, ya_ref, send_ref, spec_ref, stage,
 ):
     spec = to_modes(recv_ref, xa_ref, ya_ref)
     spec_ref[...] = spec
@@ -262,7 +260,7 @@
             for j in range(GROUPS):
                 k = s * GROUPS + j
                 modes[k] = modes[k] + weight[k * KY : (k + 1) * KY] * source
-    values = from_modes(jnp.concatenate(modes, axis=0), yb_ref, xb_ref)
+    values = from_modes(jnp.concatenate(modes, axis=0), ya_ref, xa_ref)
     stage[...] = recv_ref[...].reshape(DEV * CHUNK, 128).astype(F32)
     extra = stage[pl.ds(CHUNK - 1, DEV, stride=CHUNK), :]
     extra = jnp.broadcast_to(jnp.sum(extra, axis=0, keepdims=True), (8, 128))
@@ -315,23 +313,21 @@
 ):
     field_hbm = field_hbm.reshape(TILES, ROWS, 128)
     cot_hbm = cot_hbm.reshape(TILES, ROWS, 128)
-    tables_made = start_all((back_hbm, back_ref, table_sems.at[0]))
     made = []
     for n in range(STEPS):
-        some = pl.ds(PER * n, PER)
+        some, lanes = pl.ds(PER * n, PER), pl.ds(WIDE * n, WIDE)
         made.append(
             start_all(
+                (back_hbm.at[:, lanes], back_ref.at[:, lanes], table_sems.at[0, n]),
                 (field_hbm.at[some], field_ref.at[some], sems.at[0, n]),
                 (cot_hbm.at[some], cot_ref.at[some], sems.at[1, n]),
+                (ahead_hbm.at[lanes], ahead_ref.at[lanes], table_sems.at[1, n]),
             )
         )
-        if n == 0:
-            tables_made += start_all((ahead_hbm, ahead_ref, table_sems.at[1]))
     bypass_matrix(bypass_ref, channel_ref, same_ref, ((1,), (1,)), left)
     unpack_chunks(recv_ref, stage, left)
     coeff[...] = jnp.zeros_like(coeff)
     cross[...] = jnp.zeros_like(cross)
-    tables_made[0].wait()
     kept = []
     for n in range(STEPS):
         for copy in made[n]:
@@ -343,8 +339,6 @@
             slope = gelu_slope(pre) * block_of(cot_ref, PER * n, b).astype(F32)
             up = slope.astype(BF16)
             block_store(up_ref, PER * n, b, up)
-            if n == 0 and b == 0:
-                tables_made[1].wait()
             term = dot(up, ahead_ref[WIDE * n : WIDE * (n + 1), :])
             for j in range(GROUPS):
                 coeff[pl.ds(j * 128 + b * PART, PART), :] += term[PART * j : PART * (j + 1)]
@@ -364,20 +358,24 @@
 
 def final_kernel(
     recv_ref, up_hbm, bypass_ref, channel_ref, same_ref, back_hbm,
-    out_ref, up_ref, back_ref, stage, left, rows_ref, table_sem, up_sems, sems,
+    out_ref, up_ref, back_ref, stage, left, rows_ref, table_sems, up_sems, sems,
 ):
-    (table_made,) = start_all((back_hbm, back_ref, table_sem))
-    up_made = []
+    loads = []
     for n in range(STEPS):
-        some = pl.ds(PER * n, PER)
-        up_made += start_all((up_hbm.at[some], up_ref.at[some], up_sems.at[n]))
+        some, lanes = pl.ds(PER * n, PER), pl.ds(WIDE * n, WIDE)
+        loads.append(
+            start_all(
+                (back_hbm.at[:, lanes], back_ref.at[:, lanes], table_sems.at[n]),
+                (up_hbm.at[some], up_ref.at[some], up_sems.at[n]),
+            )
+        )
     bypass_matrix(bypass_ref, channel_ref, same_ref, ((1,), (0,)), left)
     unpack_chunks(recv_ref, stage, left)
     made = copies(out_ref, rows_ref, sems, back=True)
     rows = rows_ref.reshape(TILES, ROWS, 128)
-    table_made.wait()
     for n in range(STEPS):
-        up_made[n].wait()
+        for copy in loads[n]:
+            copy.wait()
         for b in range(CX // XB):
             cells = block_of(up_ref, PER * n, b)
             right = jnp.concatenate([back_ref[:, WIDE * n : WIDE * (n + 1)], cells], axis=0)
@@ -462,7 +460,7 @@
     send, field_rows = call(
         analyze_kernel, (chunks, cells), [HBM, HBM],
         [pltpu.VMEM(cells.shape, BF16), pltpu.VMEM((NP, 256), BF16),
-         pltpu.VMEM((ROWS, 256), F32), stage, sems, dma(4), dma(4)],
+         pltpu.VMEM((ROWS, 256), F32), stage, sems, dma(8), dma(8)],
         out_specs=(VMEM, HBM), limit=62,
     )(field_t, table["zt_ahead"])
     recv = exchange(send)
@@ -471,9 +469,9 @@
         out_specs=(VMEM,) * 2, limit=60,
     )(weight_t, cot_t)
     send, spec = call(
-        mix_kernel, (chunks, modes), [VMEM] * 6, [pltpu.VMEM((SPEC, 128), F32)],
+        mix_kernel, (chunks, modes), [VMEM] * 4, [pltpu.VMEM((SPEC, 128), F32)],
         out_specs=(VMEM,) * 2,
-    )(recv, weight, table["x_ahead"], table["y_ahead"], table["y_back"], table["x_back"])
+    )(recv, weight, table["x_ahead"], table["y_ahead"])
     recv = exchange(send)
     specs = around(spec)
     left = pltpu.VMEM((CX // XB, BLOCK, NQ + BLOCK), BF16)
@@ -483,15 +481,14 @@
     send, up = call(
         point_kernel, (chunks, rows), [VMEM, HBM, HBM, VMEM, VMEM, VMEM, HBM, HBM],
         [held, held, back, pltpu.VMEM((NP, 256), BF16), held, stage, left,
-         pltpu.VMEM((ROWS, 256), F32), pltpu.VMEM((BLOCK, BLOCK), F32), dma(2), dma(3, STEPS)],
+         pltpu.VMEM((ROWS, 256), F32), pltpu.VMEM((BLOCK, BLOCK), F32), dma(2, STEPS), dma(3, STEPS)],
         out_specs=(VMEM, HBM), limit=60,
     )(recv, field_rows, cot_rows, bypass_weight, table["channel"], table["same"],
       table["zt_back"], table["zt_ahead"])
     recv = exchange(send)
     send, spec_up = call(
-        mix_back_kernel, (chunks, modes), [VMEM] * 7, [stage], out_specs=(VMEM,) * 2,
-    )(recv, weight, table["spread"], table["x_ahead"], table["y_ahead"], table["y_back"],
-      table["x_back"])
+        mix_back_kernel, (chunks, modes), [VMEM] * 5, [stage], out_specs=(VMEM,) * 2,
+    )(recv, weight, table["spread"], table["x_ahead"], table["y_ahead"])
     recv = exchange(send)
     specs_up = around(spec_up)
     grad_spectral = pl.pallas_call(
@@ -514,7 +511,7 @@
     smalls = around(small)
     grad_field = call(
         final_kernel, shape((CX, C, CY, NP), BF16), [VMEM, HBM, VMEM, VMEM, VMEM, HBM],
-        [held, back, stage, left, pltpu.VMEM(cells.shape, BF16), pltpu.SemaphoreType.DMA,
+        [held, back, stage, left, pltpu.VMEM(cells.shape, BF16), dma(STEPS),
          dma(STEPS), sems],
         out_specs=HBM, limit=60,
     )(recv, up, bypass_weight, table["channel"], table["same"], table["zt_back"])

time: 124 us -> 126 us (1.016)
  Pallas kernels: 46.1 us -> 47.8 us
    pallas_call x1, Pallas kernels: 11.5 us -> 12.9 us  [body(): call(point_kernel, (chunks, rows), [VMEM, HBM, HBM, VMEM, VMEM, VMEM, HBM...]
  transfers between devices with their start and end apart: 12 -> 12, of which waited for: 8 -> 8; matrix products, arithmetic and copies ran while one was open for 0% -> 0% of each run, Pallas kernels for 21% -> 20%
where the time goes in v3:
time: 126 us; the launch traced here: 124 us
  Pallas kernels  47.8 us (38%)
  starting transfers between devices  34.1 us (27%)
  blocking collectives  21.3 us (17%)
  waiting for transfers between devices  17 us (13%)
  local copies, waits for them, and re-layouts  2.23 us (2%)
    all_to_all x3, starting transfers between devices, exchange(): return lax.all_to_all(value, ('gx', 'gy'), 0, 0, tiled=True)  27.2 us
    all_to_all x1, blocking collectives, exchange(): return lax.all_to_all(value, ('gx', 'gy'), 0, 0, tiled=True)  21.3 us
    ppermute x9, waiting for transfers between devices, around(): lax.ppermute(value, 'dp', [(i, (i + k) % 4) for i in range(4)])  13.4 us
    pallas_call x1, Pallas kernels, body(): call(point_kernel, (chunks, rows), [VMEM, HBM, HBM, VMEM, VMEM, VMEM, HBM...  12.9 us
    pallas_call x1, Pallas kernels, body(): call(weights_kernel, (shape((C, SPEC, 128), BF16), cells), [VMEM, HBM], [...  9.84 us
    pallas_call x1, Pallas kernels, body(): pl.pallas_call(outer_kernel, grid=(C // PAIR,), out_shape=shape((C, C, Q3...  7.98 us
    pallas_call x1, Pallas kernels, body(): call(final_kernel, shape((CX, C, CY, NP), BF16), [VMEM, HBM, VMEM, VMEM,...  7.56 us
    ppermute x9, starting transfers between devices, around(): lax.ppermute(value, 'dp', [(i, (i + k) % 4) for i in range(4)])  6.87 us
  transfers between devices with their start and end apart: 12, of which 8 were waited for; matrix products, arithmetic and copies ran while one was open for 0% of the time, Pallas kernels for 20%

profile of v3, /device:TPU:1, one launch (start us, length us, event | category | flops | bytes accessed | tf_op | source)
XLA Modules:
  0.0 123.9 jit_solution(2234152845391358554)
XLA Ops:
  0.6 5.1 %shard_map.130 = (bf16[64,16,128]{2,1,0:T(8,128)(2,1)}, bf16[16,5,16,4,2,128]{5,4,3,2,1,0:T(2,128)(2,1)}) custom-call(bf16[16,20,2,2048]{3,2,1,0:T(2,128)(2,1)} %bitcast.13, bf16[2048,256]{1,0:T(8,128)(2,1)} %constant.14.clone.zt_hbm.ahead_hbm), custom_call_target="tpu_custom_call" | custom-call | tf_op jit(solution)/shard_map/pallas_call | solution.py:460
  5.7 13.0 %all-to-all-start = ((bf16[64,16,128]{2,1,0:T(8,128)(2,1)}), bf16[64,16,128]{2,1,0:T(8,128)(2,1)S(1)}, u32[]{:S(2)}, u32[]{:S(2)}) async-start(bf16[64,16,128]{2,1,0:T(8,128)(2,1)} %get-tuple-element.20), calls=%async_computation | async-start | bytes 524288 | tf_op jit(solution)/shard_map/all_to_all | solution.py:458
  18.7 0.0 copy-start.3
  18.7 0.0 copy-start.4
  18.8 9.8 %shard_map.131 = (bf16[20,360,128]{2,1,0:T(8,128)(2,1)}, bf16[16,5,16,4,2,128]{5,4,3,2,1,0:T(2,128)(2,1)}) custom-call(bf16[20,20,3,24,24]{4,3,2,1,0:T(8,128)(2,1)} %bitcast.12, bf16[16,20,2,2048]{3,2,1,0:T(2,128)(2,1)} %bitcast.15), custom_call_target="tpu_custom_call" | custom-call | tf_op jit(solution)/shard_map/pallas_call | solution.py:467
  28.6 2.1 %all-to-all-done.recv_ref = bf16[64,16,128]{2,1,0:T(8,128)(2,1)S(1)} async-done(((bf16[64,16,128]{2,1,0:T(8,128)(2,1)}), bf16[64,16,128]{2,1,0:T(8,128)(2,1)S(1)}, u32[]{:S(2)}, u32[]{:S(2)}) %all-to-all-start) | async-done | bytes 262176 | tf_op jit(solution)/shard_map/all_to_all | solution.py:458
  30.7 0.0 copy-done.3
  30.7 0.0 copy-done.4
  30.7 0.0 copy-start
  30.7 1.5 %copy-done = bf16[20,360,128]{2,1,0:T(8,128)(2,1)S(1)} copy-done((bf16[20,360,128]{2,1,0:T(8,128)(2,1)S(1)}, bf16[20,360,128]{2,1,0:T(8,128)(2,1)}, u32[]{:S(2)}) %copy-start) | copy-done | bytes 1843224
  32.2 2.2 %shard_map.132 = (bf16[64,16,128]{2,1,0:T(8,128)(2,1)}, bf16[360,128]{1,0:T(8,128)(2,1)S(1)}) custom-call(bf16[64,16,128]{2,1,0:T(8,128)(2,1)S(1)} %all-to-all-done.recv_ref, bf16[20,360,128]{2,1,0:T(8,128)(2,1)S(1)} %copy-done, bf16[512,256]{1,0:T(8,128)(2,1)S(1)} %copy-done.4, bf16[360,512]{1,0:T(8,128)(2,1)S(1)} %copy-done.3), custom_call_target="tpu_custom_call" | custom-call | tf_op jit(solution)/shard_map/pallas_call | solution.py:471
  34.5 8.2 %all-to-all-start.1 = ((bf16[64,16,128]{2,1,0:T(8,128)(2,1)}), bf16[64,16,128]{2,1,0:T(8,128)(2,1)S(1)}, u32[]{:S(2)}, u32[]{:S(2)}) async-start(bf16[64,16,128]{2,1,0:T(8,128)(2,1)} %get-tuple-element.22), calls=%async_computation.1 | async-start | bytes 524288 | tf_op jit(solution)/shard_map/all_to_all | solution.py:458
  42.7 2.8 %collective-permute-start.2 = (bf16[360,128]{1,0:T(8,128)(2,1)S(1)}, bf16[360,128]{1,0:T(8,128)(2,1)S(1)}, u32[]{:S(2)}, u32[]{:S(2)}) collective-permute-start(bf16[360,128]{1,0:T(8,128)(2,1)S(1)} %get-tuple-element.29.refs_0_), channel_id=1, source_target_pairs={{0,192},{64,0},{128,64},{192,128},{1,193},{65,1},{129,65},{193,129... | collective-permute-start | bytes 276488 | tf_op jit(solution)/shard_map/ppermute | solution.py:439
  45.5 0.4 collective-permute-start.1
  45.8 0.7 collective-permute-start
  46.5 0.5 collective-permute-done.2.refs_3_
  47.1 3.6 %collective-permute-done.1.refs_2_ = bf16[360,128]{1,0:T(8,128)(2,1)S(1)} collective-permute-done((bf16[360,128]{1,0:T(8,128)(2,1)S(1)}, bf16[360,128]{1,0:T(8,128)(2,1)S(1)}, u32[]{:S(2)}, u32[]{:S(2)}) %collective-permute-start.1) | collective-permute-done | bytes 92192 | tf_op jit(solution)/shard_map/ppermute | solution.py:439
  50.7 2.5 %collective-permute-done.refs_1_ = bf16[360,128]{1,0:T(8,128)(2,1)S(1)} collective-permute-done((bf16[360,128]{1,0:T(8,128)(2,1)S(1)}, bf16[360,128]{1,0:T(8,128)(2,1)S(1)}, u32[]{:S(2)}, u32[]{:S(2)}) %collective-permute-start) | collective-permute-done | bytes 92192 | tf_op jit(solution)/shard_map/ppermute | solution.py:439
  53.2 1.5 %all-to-all-done.1.recv_ref = bf16[64,16,128]{2,1,0:T(8,128)(2,1)S(1)} async-done(((bf16[64,16,128]{2,1,0:T(8,128)(2,1)}), bf16[64,16,128]{2,1,0:T(8,128)(2,1)S(1)}, u32[]{:S(2)}, u32[]{:S(2)}) %all-to-all-start.1) | async-done | bytes 262176 | tf_op jit(solution)/shard_map/all_to_all | solution.py:458
  54.7 0.0 copy-start.6
  54.7 0.7 copy-done.6
  55.4 0.0 copy-start.1
  55.4 0.0 copy-start.5
  55.4 12.9 %shard_map.133 = (bf16[64,16,128]{2,1,0:T(8,128)(2,1)}, bf16[16,640,128]{2,1,0:T(8,128)(2,1)}) custom-call(bf16[64,16,128]{2,1,0:T(8,128)(2,1)} %copy-done.6, bf16[16,5,16,4,2,128]{5,4,3,2,1,0:T(2,128)(2,1)} %get-tuple-element.25.field_hbm, bf16[16,5,16,4,2,128]{5,4,3,2,1,0:T(2,128)(2,1)} %get-tuple-element.26.cot_hbm, bf16[20,20]{1,0:T(8,128)(2,1)} %bypass_ref.3, ...), custom_call_target="tpu_custom_call" | custom-call | tf_op jit(solution)/shard_map/pallas_call | solution.py:481
  68.3 21.3 %all_to_all.20.recv_ref = bf16[64,16,128]{2,1,0:T(8,128)(2,1)S(1)} all-to-all(bf16[64,16,128]{2,1,0:T(8,128)(2,1)} %get-tuple-element.27), channel_id=1, replica_groups=mesh['dp'=4,'gx'=4,'gy'=16] {'gx','gy'}, dimensions={0} | all-to-all | bytes 524288 | tf_op jit(solution)/shard_map/all_to_all | solution.py:458
  89.7 0.0 copy-done.1
  89.7 0.0 copy-done.5
  89.7 2.1 %shard_map.134 = (bf16[64,16,128]{2,1,0:T(8,128)(2,1)}, bf16[360,128]{1,0:T(8,128)(2,1)S(1)}) custom-call(bf16[64,16,128]{2,1,0:T(8,128)(2,1)S(1)} %all_to_all.20.recv_ref, bf16[20,360,128]{2,1,0:T(8,128)(2,1)S(1)} %copy-done.1, bf16[128,512]{1,0:T(8,128)(2,1)S(1)} %copy-done.5, bf16[512,256]{1,0:T(8,128)(2,1)S(1)} %copy-done.4, bf16[360,512]{1,0:T(8,128)(2,1)S(1)} %copy-done.3), custom_call_target="tpu_custom_call" | custom-call | tf_op jit(solution)/shard_map/pallas_call | solution.py:489
  91.8 6.0 %all-to-all-start.3 = ((bf16[64,16,128]{2,1,0:T(8,128)(2,1)}), bf16[64,16,128]{2,1,0:T(8,128)(2,1)S(1)}, u32[]{:S(2)}, u32[]{:S(2)}) async-start(bf16[64,16,128]{2,1,0:T(8,128)(2,1)} %get-tuple-element.28), calls=%async_computation.3 | async-start | bytes 524288 | tf_op jit(solution)/shard_map/all_to_all | solution.py:458
  97.8 0.4 collective-permute-start.5
  98.2 0.3 collective-permute-start.4
  98.5 0.8 collective-permute-start.3
  99.4 2.3 %collective-permute-done.5.refs_7_ = bf16[360,128]{1,0:T(8,128)(2,1)S(1)} collective-permute-done((bf16[360,128]{1,0:T(8,128)(2,1)S(1)}, bf16[360,128]{1,0:T(8,128)(2,1)S(1)}, u32[]{:S(2)}, u32[]{:S(2)}) %collective-permute-start.5) | collective-permute-done | bytes 92192 | tf_op jit(solution)/shard_map/ppermute | solution.py:439
  101.7 1.7 %collective-permute-done.4.refs_6_ = bf16[360,128]{1,0:T(8,128)(2,1)S(1)} collective-permute-done((bf16[360,128]{1,0:T(8,128)(2,1)S(1)}, bf16[360,128]{1,0:T(8,128)(2,1)S(1)}, u32[]{:S(2)}, u32[]{:S(2)}) %collective-permute-start.4) | collective-permute-done | bytes 92192 | tf_op jit(solution)/shard_map/ppermute | solution.py:439
  103.4 2.7 %collective-permute-done.3.refs_5_ = bf16[360,128]{1,0:T(8,128)(2,1)S(1)} collective-permute-done((bf16[360,128]{1,0:T(8,128)(2,1)S(1)}, bf16[360,128]{1,0:T(8,128)(2,1)S(1)}, u32[]{:S(2)}, u32[]{:S(2)}) %collective-permute-start.3) | collective-permute-done | bytes 92192 | tf_op jit(solution)/shard_map/ppermute | solution.py:439
  106.1 8.0 %shard_map.135 = f32[20,20,3,24,24]{4,3,2,1,0:T(8,128)} custom-call(bf16[360,128]{1,0:T(8,128)(2,1)S(1)} %get-tuple-element.29.refs_0_, bf16[360,128]{1,0:T(8,128)(2,1)S(1)} %collective-permute-done.refs_1_, bf16[360,128]{1,0:T(8,128)(2,1)S(1)} %collective-permute-done.1.refs_2_, bf16[360,128]{1,0:T(8,128)(2,1)S(1)} %collective-permute-done.2.refs_3_, ...), custom_call_target="tpu_custom_call" | custom-call | flops 1000000000 | bytes 100000000 | tf_op jit(solution)/shard_map/pallas_call | solution.py:494
  114.1 0.0 all-to-all-done.3.recv_ref
  114.1 0.0 copy-start.2
  114.1 0.1 shard_map.137
  114.2 0.0 collective-permute-start.8
  114.2 1.5 %collective-permute-start.7 = (f32[24,128]{1,0:T(8,128)S(1)}, f32[24,128]{1,0:T(8,128)S(1)}, u32[]{:S(2)}, u32[]{:S(2)}) collective-permute-start(f32[24,128]{1,0:T(8,128)S(1)} %shard_map.137), channel_id=1, source_target_pairs={{0,64},{64,128},{128,192},{192,0},{1,65},{65,129},{129,193},{193,1... | collective-permute-start | bytes 36872 | tf_op jit(solution)/shard_map/ppermute | solution.py:439
  115.6 0.0 collective-permute-start.6
  115.6 0.0 copy-done.2
  115.7 7.6 %shard_map.136 = bf16[16,20,2,2048]{3,2,1,0:T(2,128)(2,1)} custom-call(bf16[64,16,128]{2,1,0:T(8,128)(2,1)} %copy-done.2, bf16[16,640,128]{2,1,0:T(8,128)(2,1)} %get-tuple-element.35.up_hbm, bf16[20,20]{1,0:T(8,128)(2,1)} %bypass_ref.3, bf16[320,20]{1,0:T(8,128)(2,1)} %constant.19.clone.channel_ref, bf16[320,384]{1,0:T(8,128)(2,1)} %constant.20.clone.same_ref, ...), custom_call_target="tpu_custom_call" | custom-call | tf_op jit(solution)/shard_map/pallas_call | solution.py:512
  123.2 0.0 collective-permute-done.8
  123.2 0.0 collective-permute-done.7
  123.2 0.0 collective-permute-done.6
  123.3 0.6 fusion
Async XLA Ops:
  5.7 25.0 %all-to-all-start = ((bf16[64,16,128]{2,1,0:T(8,128)(2,1)}), bf16[64,16,128]{2,1,0:T(8,128)(2,1)S(1)}, u32[]{:S(2)}, u32[]{:S(2)}) async-start(bf16[64,16,128]{2,1,0:T(8,128)(2,1)} %get-tuple-element.20), calls=%async_computation | async-start | bytes 524288 | tf_op jit(solution)/shard_map/all_to_all | solution.py:458
  18.7 12.0 %copy-start.3 = (bf16[360,512]{1,0:T(8,128)(2,1)S(1)}, bf16[360,512]{1,0:T(8,128)(2,1)}, u32[]{:S(2)}) copy-start(bf16[360,512]{1,0:T(8,128)(2,1)} %constant.17.clone.ya_ref) | copy-start | bytes 1105924
  18.7 12.0 %copy-start.4 = (bf16[512,256]{1,0:T(8,128)(2,1)S(1)}, bf16[512,256]{1,0:T(8,128)(2,1)}, u32[]{:S(2)}) copy-start(bf16[512,256]{1,0:T(8,128)(2,1)} %constant.16.clone.xa_ref) | copy-start | bytes 786436
  30.7 1.5 %copy-start = (bf16[20,360,128]{2,1,0:T(8,128)(2,1)S(1)}, bf16[20,360,128]{2,1,0:T(8,128)(2,1)}, u32[]{:S(2)}) copy-start(bf16[20,360,128]{2,1,0:T(8,128)(2,1)} %get-tuple-element.21.weight_ref) | copy-start | bytes 5529604
  34.5 20.2 %all-to-all-start.1 = ((bf16[64,16,128]{2,1,0:T(8,128)(2,1)}), bf16[64,16,128]{2,1,0:T(8,128)(2,1)S(1)}, u32[]{:S(2)}, u32[]{:S(2)}) async-start(bf16[64,16,128]{2,1,0:T(8,128)(2,1)} %get-tuple-element.22), calls=%async_computation.1 | async-start | bytes 524288 | tf_op jit(solution)/shard_map/all_to_all | solution.py:458
  42.7 4.4 %collective-permute-start.2 = (bf16[360,128]{1,0:T(8,128)(2,1)S(1)}, bf16[360,128]{1,0:T(8,128)(2,1)S(1)}, u32[]{:S(2)}, u32[]{:S(2)}) collective-permute-start(bf16[360,128]{1,0:T(8,128)(2,1)S(1)} %get-tuple-element.29.refs_0_), channel_id=1, source_target_pairs={{0,192},{64,0},{128,64},{192,128},{1,193},{65,1},{129,65},{193,129... | collective-permute-start | bytes 276488 | tf_op jit(solution)/shard_map/ppermute | solution.py:439
  45.5 5.2 %collective-permute-start.1 = (bf16[360,128]{1,0:T(8,128)(2,1)S(1)}, bf16[360,128]{1,0:T(8,128)(2,1)S(1)}, u32[]{:S(2)}, u32[]{:S(2)}) collective-permute-start(bf16[360,128]{1,0:T(8,128)(2,1)S(1)} %get-tuple-element.29.refs_0_), channel_id=1, source_target_pairs={{0,128},{64,192},{128,0},{192,64},{1,129},{65,193},{129,1},{193,65... | collective-permute-start | bytes 276488 | tf_op jit(solution)/shard_map/ppermute | solution.py:439
  45.8 7.4 %collective-permute-start = (bf16[360,128]{1,0:T(8,128)(2,1)S(1)}, bf16[360,128]{1,0:T(8,128)(2,1)S(1)}, u32[]{:S(2)}, u32[]{:S(2)}) collective-permute-start(bf16[360,128]{1,0:T(8,128)(2,1)S(1)} %get-tuple-element.29.refs_0_), channel_id=1, source_target_pairs={{0,64},{64,128},{128,192},{192,0},{1,65},{65,129},{129,193},{193,1... | collective-permute-start | bytes 276488 | tf_op jit(solution)/shard_map/ppermute | solution.py:439
  54.7 0.7 copy-start.6
  55.4 34.3 %copy-start.1 = (bf16[20,360,128]{2,1,0:T(8,128)(2,1)S(1)}, bf16[20,360,128]{2,1,0:T(8,128)(2,1)}, u32[]{:S(2)}) copy-start(bf16[20,360,128]{2,1,0:T(8,128)(2,1)} %get-tuple-element.21.weight_ref) | copy-start | bytes 5529604
  55.4 34.3 %copy-start.5 = (bf16[128,512]{1,0:T(8,128)(2,1)S(1)}, bf16[128,512]{1,0:T(8,128)(2,1)}, u32[]{:S(2)}) copy-start(bf16[128,512]{1,0:T(8,128)(2,1)} %constant.18.clone.spread_ref) | copy-start | bytes 393220
  91.8 22.3 %all-to-all-start.3 = ((bf16[64,16,128]{2,1,0:T(8,128)(2,1)}), bf16[64,16,128]{2,1,0:T(8,128)(2,1)S(1)}, u32[]{:S(2)}, u32[]{:S(2)}) async-start(bf16[64,16,128]{2,1,0:T(8,128)(2,1)} %get-tuple-element.28), calls=%async_computation.3 | async-start | bytes 524288 | tf_op jit(solution)/shard_map/all_to_all | solution.py:458
  97.8 3.9 %collective-permute-start.5 = (bf16[360,128]{1,0:T(8,128)(2,1)S(1)}, bf16[360,128]{1,0:T(8,128)(2,1)S(1)}, u32[]{:S(2)}, u32[]{:S(2)}) collective-permute-start(bf16[360,128]{1,0:T(8,128)(2,1)S(1)} %get-tuple-element.33.refs_4_), channel_id=1, source_target_pairs={{0,192},{64,0},{128,64},{192,128},{1,193},{65,1},{129,65},{193,129... | collective-permute-start | bytes 276488 | tf_op jit(solution)/shard_map/ppermute | solution.py:439
  98.2 5.2 %collective-permute-start.4 = (bf16[360,128]{1,0:T(8,128)(2,1)S(1)}, bf16[360,128]{1,0:T(8,128)(2,1)S(1)}, u32[]{:S(2)}, u32[]{:S(2)}) collective-permute-start(bf16[360,128]{1,0:T(8,128)(2,1)S(1)} %get-tuple-element.33.refs_4_), channel_id=1, source_target_pairs={{0,128},{64,192},{128,0},{192,64},{1,129},{65,193},{129,1},{193,65... | collective-permute-start | bytes 276488 | tf_op jit(solution)/shard_map/ppermute | solution.py:439
  98.5 7.6 %collective-permute-start.3 = (bf16[360,128]{1,0:T(8,128)(2,1)S(1)}, bf16[360,128]{1,0:T(8,128)(2,1)S(1)}, u32[]{:S(2)}, u32[]{:S(2)}) collective-permute-start(bf16[360,128]{1,0:T(8,128)(2,1)S(1)} %get-tuple-element.33.refs_4_), channel_id=1, source_target_pairs={{0,64},{64,128},{128,192},{192,0},{1,65},{65,129},{129,193},{193,1... | collective-permute-start | bytes 276488 | tf_op jit(solution)/shard_map/ppermute | solution.py:439
  114.1 1.6 %copy-start.2 = (bf16[64,16,128]{2,1,0:T(8,128)(2,1)}, bf16[64,16,128]{2,1,0:T(8,128)(2,1)S(1)}, u32[]{:S(2)}) copy-start(bf16[64,16,128]{2,1,0:T(8,128)(2,1)S(1)} %all-to-all-done.3.recv_ref) | copy-start | bytes 786436
  114.2 9.1 %collective-permute-start.8 = (f32[24,128]{1,0:T(8,128)S(1)}, f32[24,128]{1,0:T(8,128)S(1)}, u32[]{:S(2)}, u32[]{:S(2)}) collective-permute-start(f32[24,128]{1,0:T(8,128)S(1)} %shard_map.137), channel_id=1, source_target_pairs={{0,192},{64,0},{128,64},{192,128},{1,193},{65,1},{129,65},{193,129... | collective-permute-start | bytes 36872 | tf_op jit(solution)/shard_map/ppermute | solution.py:439
  114.2 9.0 %collective-permute-start.7 = (f32[24,128]{1,0:T(8,128)S(1)}, f32[24,128]{1,0:T(8,128)S(1)}, u32[]{:S(2)}, u32[]{:S(2)}) collective-permute-start(f32[24,128]{1,0:T(8,128)S(1)} %shard_map.137), channel_id=1, source_target_pairs={{0,64},{64,128},{128,192},{192,0},{1,65},{65,129},{129,193},{193,1... | collective-permute-start | bytes 36872 | tf_op jit(solution)/shard_map/ppermute | solution.py:439
  115.6 7.6 %collective-permute-start.6 = (f32[24,128]{1,0:T(8,128)S(1)}, f32[24,128]{1,0:T(8,128)S(1)}, u32[]{:S(2)}, u32[]{:S(2)}) collective-permute-start(f32[24,128]{1,0:T(8,128)S(1)} %shard_map.137), channel_id=1, source_target_pairs={{0,128},{64,192},{128,0},{192,64},{1,129},{65,193},{129,1},{193,65... | collective-permute-start | bytes 36872 | tf_op jit(solution)/shard_map/ppermute | solution.py:439

commit v4 on v2

--- a/solution.py
+++ b/solution.py
@@ -32,6 +32,7 @@
 Q3 = 3
 CHUNK = 16
 SPEC = Q3 * GROUPS * KY
+PACK = (SPEC + KY) // 4
 XB = 8
 PART = 4 * XB * CY
 WIDE = 512
@@ -79,9 +80,7 @@
         "zt_ahead": ahead,
         "zt_back": by_slot.T,
         "x_ahead": x_ahead,
-        "x_back": x_ahead.T,
         "y_ahead": y_ahead,
-        "y_back": y_ahead.T,
         "spread": spread,
         "channel": channel,
         "same": np.concatenate([np.zeros((BLOCK, 64)), cell @ cell.T], axis=1),
@@ -208,10 +207,31 @@
 
 
 def from_modes(modes, y_ref, x_ref):
-    tall = dot(y_ref[...], modes.astype(BF16)).astype(BF16)
+    tall = dot(y_ref[...], modes.astype(BF16), ((0,), (0,))).astype(BF16)
     half = PY * CHUNK
     wide = jnp.concatenate([tall[:half], tall[half:]], axis=1)
-    return dot(wide, x_ref[...])
+    return dot(wide, x_ref[...], ((1,), (1,)))
+
+
+def pack_modes(spec):
+    full = jnp.concatenate([spec, jnp.zeros((KY, 128), F32)], axis=0)
+    last = full[3 * PACK :]
+    inside = lax.broadcasted_iota(jnp.int32, (PACK, 128), 1) % 32 < KX
+    parts = []
+    for i in range(3):
+        moved = pltpu.roll(last, KX - 8 * i, 1)
+        parts.append(jnp.where(inside, full[PACK * i : PACK * (i + 1)], moved))
+    return jnp.concatenate(parts, axis=0).astype(BF16)
+
+
+def unpack_modes(packed):
+    lane = lax.broadcasted_iota(jnp.int32, (PACK, 128), 1) % 32
+    last = jnp.zeros((PACK, 128), F32)
+    for i in range(3):
+        part = packed[PACK * i : PACK * (i + 1)]
+        moved = pltpu.roll(part, 128 - KX + 8 * i, 1)
+        last = jnp.where((lane >= 8 * i) & (lane < 8 * (i + 1)), moved, last)
+    return jnp.concatenate([packed, last], axis=0)
 
 
 def write_chunks(values, send_ref):
@@ -221,11 +241,10 @@
 
 
 def mix_kernel(
-    recv_ref, weight_ref, xa_ref, ya_ref, yb_ref, xb_ref, send_ref, spec_ref, modes,
+    recv_ref, weight_ref, xa_ref, ya_ref, send_ref, spec_ref, modes,
 ):
-    spec = to_modes(recv_ref, xa_ref, ya_ref)
-    spec_ref[...] = spec
-    spec = spec.astype(F32)
+    spec = to_modes(recv_ref, xa_ref, ya_ref).astype(F32)
+    spec_ref[...] = pack_modes(spec)
     group = lax.broadcasted_iota(jnp.int32, (Q3 * KY, 128), 1) // 32
     for jo in range(GROUPS):
         total = jnp.zeros((Q3 * KY, 128), F32)
@@ -244,14 +263,15 @@
             total = jnp.where(group == o4, summed, total)
         for s in range(Q3):
             modes[pl.ds((s * GROUPS + jo) * KY, KY), :] = total[s * KY : (s + 1) * KY]
-    write_chunks(from_modes(modes[...], yb_ref, xb_ref), send_ref)
+    write_chunks(from_modes(modes[...], ya_ref, xa_ref), send_ref)
 
 
 def mix_back_kernel(
-    recv_ref, weight_ref, spread_ref, xa_ref, ya_ref, yb_ref, xb_ref, send_ref, spec_ref, stage,
+    recv_ref, weight_ref, spread_ref, xa_ref, ya_ref, own_ref, send_ref, spec_ref, stage,
 ):
     spec = to_modes(recv_ref, xa_ref, ya_ref)
-    spec_ref[...] = spec
+    spec_ref[pl.ds(0, 3 * PACK), :] = own_ref[...]
+    spec_ref[pl.ds(3 * PACK, 3 * PACK), :] = pack_modes(spec.astype(F32))
     copied = dot(spec, spread_ref[...])
     modes = [jnp.zeros((KY, 128), F32) for _ in range(Q3 * GROUPS)]
     for o in range(C):
@@ -262,7 +282,7 @@
             for j in range(GROUPS):
                 k = s * GROUPS + j
                 modes[k] = modes[k] + weight[k * KY : (k + 1) * KY] * source
-    values = from_modes(jnp.concatenate(modes, axis=0), yb_ref, xb_ref)
+    values = from_modes(jnp.concatenate(modes, axis=0), ya_ref, xa_ref)
     stage[...] = recv_ref[...].reshape(DEV * CHUNK, 128).astype(F32)
     extra = stage[pl.ds(CHUNK - 1, DEV, stride=CHUNK), :]
     extra = jnp.broadcast_to(jnp.sum(extra, axis=0, keepdims=True), (8, 128))
@@ -309,29 +329,24 @@
 
 
 def point_kernel(
-    recv_ref, field_hbm, cot_hbm, bypass_ref, channel_ref, same_ref, back_hbm, ahead_hbm,
-    send_ref, up_hbm,
-    field_ref, cot_ref, back_ref, ahead_ref, up_ref, stage, left, coeff, cross, table_sems, sems,
+    recv_ref, field_hbm, cot_hbm, bypass_ref, channel_ref, same_ref, back_ref, ahead_ref,
+    send_ref, up_hbm, field_ref, cot_ref, up_ref, stage, left, coeff, cross, sems,
 ):
     field_hbm = field_hbm.reshape(TILES, ROWS, 128)
     cot_hbm = cot_hbm.reshape(TILES, ROWS, 128)
-    tables_made = start_all((back_hbm, back_ref, table_sems.at[0]))
     made = []
     for n in range(STEPS):
         some = pl.ds(PER * n, PER)
         made.append(
             start_all(
-                (field_hbm.at[some], field_ref.at[some], sems.at[0, n]),
-                (cot_hbm.at[some], cot_ref.at[some], sems.at[1, n]),
+                (field_hbm.at[some], field_ref.at[some], sems.at[1, n]),
+                (cot_hbm.at[some], cot_ref.at[some], sems.at[2, n]),
             )
         )
-        if n == 0:
-            tables_made += start_all((ahead_hbm, ahead_ref, table_sems.at[1]))
     bypass_matrix(bypass_ref, channel_ref, same_ref, ((1,), (1,)), left)
     unpack_chunks(recv_ref, stage, left)
     coeff[...] = jnp.zeros_like(coeff)
     cross[...] = jnp.zeros_like(cross)
-    tables_made[0].wait()
     kept = []
     for n in range(STEPS):
         for copy in made[n]:
@@ -343,14 +358,12 @@
             slope = gelu_slope(pre) * block_of(cot_ref, PER * n, b).astype(F32)
             up = slope.astype(BF16)
             block_store(up_ref, PER * n, b, up)
-            if n == 0 and b == 0:
-                tables_made[1].wait()
             term = dot(up, ahead_ref[WIDE * n : WIDE * (n + 1), :])
             for j in range(GROUPS):
                 coeff[pl.ds(j * 128 + b * PART, PART), :] += term[PART * j : PART * (j + 1)]
             cross[...] += dot(cells, up, ((1,), (1,)))
         some = pl.ds(PER * n, PER)
-        kept += start_all((up_ref.at[some], up_hbm.at[some], sems.at[2, n]))
+        kept += start_all((up_ref.at[some], up_hbm.at[some], sems.at[0, n]))
     kept_cross = cross[...] * same_ref[:, 64:].astype(F32)
     channel = channel_ref[...].astype(F32)
     high = lax.Precision.HIGHEST
@@ -388,8 +401,7 @@
         copy.wait()
 
 
-def turn(ref, b, tiles):
-    value = ref[...].astype(F32)
+def turn(value, b, tiles):
     for s in range(Q3):
         for j in range(GROUPS):
             at = (s * GROUPS + j) * KY
@@ -402,13 +414,14 @@
 
 
 def outer_kernel(*refs):
-    out_ref, first, second = refs[8:]
+    out_ref, first, second = refs[4:]
 
     @pl.when(pl.program_id(0) == 0)
     def _():
         for b in range(4):
-            turn(refs[b], b, first)
-            turn(refs[4 + b], b, second)
+            both = refs[b][...].astype(F32)
+            turn(unpack_modes(both[: 3 * PACK]), b, first)
+            turn(unpack_modes(both[3 * PACK :]), b, second)
 
     c = pl.program_id(0) * PAIR
     for s in range(Q3):
@@ -446,7 +459,6 @@
     table = {name: jnp.asarray(value) for name, value in TABLES.items()}
     shape = jax.ShapeDtypeStruct
     chunks = shape((DEV, CHUNK, 128), BF16)
-    modes = shape((SPEC, 128), BF16)
     cells = shape((TILES, GROUPS, CX, 4, CY, 128), BF16)
     rows = shape((TILES, ROWS, 128), BF16)
     stage = pltpu.VMEM((DEV * CHUNK, 128), F32)
@@ -470,42 +482,40 @@
         weights_kernel, (shape((C, SPEC, 128), BF16), cells), [VMEM, HBM], [sems],
         out_specs=(VMEM,) * 2, limit=60,
     )(weight_t, cot_t)
-    send, spec = call(
-        mix_kernel, (chunks, modes), [VMEM] * 6, [pltpu.VMEM((SPEC, 128), F32)],
-        out_specs=(VMEM,) * 2,
-    )(recv, weight, table["x_ahead"], table["y_ahead"], table["y_back"], table["x_back"])
+    send, own = call(
+        mix_kernel, (chunks, shape((3 * PACK, 128), BF16)), [VMEM] * 4,
+        [pltpu.VMEM((SPEC, 128), F32)], out_specs=(VMEM,) * 2, limit=12,
+    )(recv, weight, table["x_ahead"], table["y_ahead"])
     recv = exchange(send)
-    specs = around(spec)
     left = pltpu.VMEM((CX // XB, BLOCK, NQ + BLOCK), BF16)
     held = pltpu.VMEM(rows.shape, BF16)
     back = pltpu.VMEM((NQ, NP), BF16)
-    recv, *specs = lax.optimization_barrier((recv, *specs))
     send, up = call(
-        point_kernel, (chunks, rows), [VMEM, HBM, HBM, VMEM, VMEM, VMEM, HBM, HBM],
-        [held, held, back, pltpu.VMEM((NP, 256), BF16), held, stage, left,
-         pltpu.VMEM((ROWS, 256), F32), pltpu.VMEM((BLOCK, BLOCK), F32), dma(2), dma(3, STEPS)],
-        out_specs=(VMEM, HBM), limit=60,
+        point_kernel, (chunks, rows), [VMEM, HBM, HBM] + [VMEM] * 5,
+        [held, held, held, stage, left, pltpu.VMEM((ROWS, 256), F32),
+         pltpu.VMEM((BLOCK, BLOCK), F32), dma(3, STEPS)],
+        out_specs=(VMEM, HBM), limit=51,
     )(recv, field_rows, cot_rows, bypass_weight, table["channel"], table["same"],
       table["zt_back"], table["zt_ahead"])
     recv = exchange(send)
-    send, spec_up = call(
-        mix_back_kernel, (chunks, modes), [VMEM] * 7, [stage], out_specs=(VMEM,) * 2,
-    )(recv, weight, table["spread"], table["x_ahead"], table["y_ahead"], table["y_back"],
-      table["x_back"])
+    send, both = call(
+        mix_back_kernel, (chunks, shape((6 * PACK, 128), BF16)), [VMEM] * 6, [stage],
+        out_specs=(VMEM,) * 2,
+    )(recv, weight, table["spread"], table["x_ahead"], table["y_ahead"], own)
     recv = exchange(send)
-    specs_up = around(spec_up)
+    specs = around(both)
     grad_spectral = pl.pallas_call(
         outer_kernel,
         grid=(C // PAIR,),
         out_shape=shape((C, C, Q3, KX, KY), F32),
-        in_specs=[VMEM] * 8,
+        in_specs=[VMEM] * 4,
         out_specs=pl.BlockSpec((PAIR, C, Q3, KX, KY), lambda c: (c, 0, 0, 0, 0)),
         scratch_shapes=[pltpu.VMEM((C, Q3, 4, KX, KY), F32)] * 2,
         compiler_params=pltpu.CompilerParams(vmem_limit_bytes=24 * MIB),
         cost_estimate=pl.CostEstimate(
             flops=10**9, bytes_accessed=10**8, transcendentals=0
         ),
-    )(*specs, *specs_up)
+    )(*specs)
     recv, grad_spectral = lax.optimization_barrier((recv, grad_spectral))
     small = call(
         small_kernel, shape((24, 128), F32), [VMEM], [pltpu.VMEM((24, CHUNK, 128), F32)],

time: 124 us -> 121 us (0.976)
  blocking collectives: 21.3 us -> 38 us
  starting transfers between devices: 34.2 us -> 24.5 us
  waiting for transfers between devices: 16.9 us -> 11.4 us
  Pallas kernels: 46.1 us -> 43.3 us
    all_to_all x1 -> x2, blocking collectives: 21.3 us -> 38 us  [exchange(): return lax.all_to_all(value, ('gx', 'gy'), 0, 0, tiled=True)]
    all_to_all x3 -> x2, starting transfers between devices: 27.3 us -> 19 us  [exchange(): return lax.all_to_all(value, ('gx', 'gy'), 0, 0, tiled=True)]
    ppermute x9 -> x6, waiting for transfers between devices: 13.4 us -> 9.4 us  [around(): lax.ppermute(value, 'dp', [(i, (i + k) % 4) for i in range(4)])]
    pallas_call x3, Pallas kernels: 15.8 us -> 12.9 us  [the longest x1 9.24 us: body(): call(point_kernel, (chunks, rows), [VMEM, HBM, HBM] + [VMEM] * 5, [held,...]
    all_to_all x3 -> x2, waiting for transfers between devices: 3.55 us -> 1.98 us  [exchange(): return lax.all_to_all(value, ('gx', 'gy'), 0, 0, tiled=True)]
    ppermute x9 -> x6, starting transfers between devices: 6.87 us -> 5.43 us  [around(): lax.ppermute(value, 'dp', [(i, (i + k) % 4) for i in range(4)])]
  transfers between devices with their start and end apart: 12 -> 8, of which waited for: 8 -> 4; matrix products, arithmetic and copies ran while one was open for 0% -> 0% of each run, Pallas kernels for 21% -> 21%
where the time goes in v4:
time: 121 us; the launch traced here: 120 us
  Pallas kernels  43.3 us (36%)
  blocking collectives  38 us (31%)
  starting transfers between devices  24.5 us (20%)
  waiting for transfers between devices  11.4 us (9%)
  local copies, waits for them, and re-layouts  1.57 us (1%)
    all_to_all x2, blocking collectives, exchange(): return lax.all_to_all(value, ('gx', 'gy'), 0, 0, tiled=True)  38 us
    all_to_all x2, starting transfers between devices, exchange(): return lax.all_to_all(value, ('gx', 'gy'), 0, 0, tiled=True)  19 us
    pallas_call x1, Pallas kernels, body(): call(weights_kernel, (shape((C, SPEC, 128), BF16), cells), [VMEM, HBM], [...  9.93 us
    ppermute x6, waiting for transfers between devices, around(): lax.ppermute(value, 'dp', [(i, (i + k) % 4) for i in range(4)])  9.4 us
    pallas_call x1, Pallas kernels, body(): call(point_kernel, (chunks, rows), [VMEM, HBM, HBM] + [VMEM] * 5, [held,...  9.24 us
    pallas_call x1, Pallas kernels, body(): pl.pallas_call(outer_kernel, grid=(C // PAIR,), out_shape=shape((C, C, Q3...  8.13 us
    pallas_call x1, Pallas kernels, body(): call(final_kernel, shape((CX, C, CY, NP), BF16), [VMEM, HBM, VMEM, VMEM,...  7.24 us
    ppermute x6, starting transfers between devices, around(): lax.ppermute(value, 'dp', [(i, (i + k) % 4) for i in range(4)])  5.43 us
  transfers between devices with their start and end apart: 8, of which 4 were waited for; matrix products, arithmetic and copies ran while one was open for 0% of the time, Pallas kernels for 21%

profile of v4, /device:TPU:1, one launch (start us, length us, event | category | flops | bytes accessed | tf_op | source)
XLA Modules:
  0.0 120.2 jit_solution(2514290518846588604)
XLA Ops:
  0.6 5.1 %shard_map.130 = (bf16[64,16,128]{2,1,0:T(8,128)(2,1)}, bf16[16,5,16,4,2,128]{5,4,3,2,1,0:T(2,128)(2,1)}) custom-call(bf16[16,20,2,2048]{3,2,1,0:T(2,128)(2,1)} %bitcast.13, bf16[2048,256]{1,0:T(8,128)(2,1)} %constant.14.clone.zt_hbm.ahead_ref), custom_call_target="tpu_custom_call" | custom-call | tf_op jit(solution)/shard_map/pallas_call | solution.py:474
  5.7 13.0 %all-to-all-start = ((bf16[64,16,128]{2,1,0:T(8,128)(2,1)}), bf16[64,16,128]{2,1,0:T(8,128)(2,1)S(1)}, u32[]{:S(2)}, u32[]{:S(2)}) async-start(bf16[64,16,128]{2,1,0:T(8,128)(2,1)} %get-tuple-element.15), calls=%async_computation | async-start | bytes 524288 | tf_op jit(solution)/shard_map/all_to_all | solution.py:472
  18.7 0.0 copy-start.5
  18.7 0.0 copy-start.6
  18.8 0.0 copy-start.2
  18.8 0.0 copy-start.3
  18.8 0.0 copy-start.7
  18.8 0.0 copy-start.8
  18.8 0.0 copy-start.10
  18.8 9.9 %shard_map.131 = (bf16[20,360,128]{2,1,0:T(8,128)(2,1)}, bf16[16,5,16,4,2,128]{5,4,3,2,1,0:T(2,128)(2,1)}) custom-call(bf16[20,20,3,24,24]{4,3,2,1,0:T(8,128)(2,1)} %bitcast.12, bf16[16,20,2,2048]{3,2,1,0:T(2,128)(2,1)} %bitcast.15), custom_call_target="tpu_custom_call" | custom-call | tf_op jit(solution)/shard_map/pallas_call | solution.py:481
  28.7 2.0 %all-to-all-done.recv_ref = bf16[64,16,128]{2,1,0:T(8,128)(2,1)S(1)} async-done(((bf16[64,16,128]{2,1,0:T(8,128)(2,1)}), bf16[64,16,128]{2,1,0:T(8,128)(2,1)S(1)}, u32[]{:S(2)}, u32[]{:S(2)}) %all-to-all-start) | async-done | bytes 262176 | tf_op jit(solution)/shard_map/all_to_all | solution.py:472
  30.7 0.0 copy-done.5
  30.7 0.0 copy-done.6
  30.7 0.0 copy-start
  30.7 1.5 %copy-done = bf16[20,360,128]{2,1,0:T(8,128)(2,1)S(1)} copy-done((bf16[20,360,128]{2,1,0:T(8,128)(2,1)S(1)}, bf16[20,360,128]{2,1,0:T(8,128)(2,1)}, u32[]{:S(2)}) %copy-start) | copy-done | bytes 1843224
  32.2 1.5 %shard_map.132 = (bf16[64,16,128]{2,1,0:T(8,128)(2,1)S(1)}, bf16[288,128]{1,0:T(8,128)(2,1)S(1)}) custom-call(bf16[64,16,128]{2,1,0:T(8,128)(2,1)S(1)} %all-to-all-done.recv_ref, bf16[20,360,128]{2,1,0:T(8,128)(2,1)S(1)} %copy-done, bf16[512,256]{1,0:T(8,128)(2,1)S(1)} %copy-done.6, bf16[360,512]{1,0:T(8,128)(2,1)S(1)} %copy-done.5), custom_call_target="tpu_custom_call" | custom-call | tf_op jit(solution)/shard_map/pallas_call | solution.py:485
  33.8 20.2 %all_to_all.20.recv_ref = bf16[64,16,128]{2,1,0:T(8,128)(2,1)S(1)} all-to-all(bf16[64,16,128]{2,1,0:T(8,128)(2,1)S(1)} %get-tuple-element.17), channel_id=1, replica_groups=mesh['dp'=4,'gx'=4,'gy'=16] {'gx','gy'}, dimensions={0} | all-to-all | bytes 524288 | tf_op jit(solution)/shard_map/all_to_all | solution.py:472
  53.9 0.0 copy-done.2
  53.9 0.0 copy-done.3
  53.9 0.0 copy-done.7
  53.9 0.0 copy-done.8
  54.0 0.0 copy-done.10
  54.0 0.0 copy-start.1
  54.0 0.0 copy-start.9
  54.0 9.2 %shard_map.133 = (bf16[64,16,128]{2,1,0:T(8,128)(2,1)S(1)}, bf16[16,640,128]{2,1,0:T(8,128)(2,1)}) custom-call(bf16[64,16,128]{2,1,0:T(8,128)(2,1)S(1)} %all_to_all.20.recv_ref, bf16[16,5,16,4,2,128]{5,4,3,2,1,0:T(2,128)(2,1)} %get-tuple-element.18.field_hbm, bf16[16,5,16,4,2,128]{5,4,3,2,1,0:T(2,128)(2,1)} %get-tuple-element.19.cot_hbm, ...), custom_call_target="tpu_custom_call" | custom-call | tf_op jit(solution)/shard_map/pallas_call | solution.py:493
  63.2 17.8 %all_to_all.21.recv_ref = bf16[64,16,128]{2,1,0:T(8,128)(2,1)S(1)} all-to-all(bf16[64,16,128]{2,1,0:T(8,128)(2,1)S(1)} %get-tuple-element.20), channel_id=1, replica_groups=mesh['dp'=4,'gx'=4,'gy'=16] {'gx','gy'}, dimensions={0} | all-to-all | bytes 524288 | tf_op jit(solution)/shard_map/all_to_all | solution.py:472
  81.1 0.0 copy-done.1
  81.1 0.0 copy-done.9
  81.1 2.1 %shard_map.134 = (bf16[64,16,128]{2,1,0:T(8,128)(2,1)}, bf16[576,128]{1,0:T(8,128)(2,1)S(1)}) custom-call(bf16[64,16,128]{2,1,0:T(8,128)(2,1)S(1)} %all_to_all.21.recv_ref, bf16[20,360,128]{2,1,0:T(8,128)(2,1)S(1)} %copy-done.1, bf16[128,512]{1,0:T(8,128)(2,1)S(1)} %copy-done.9, bf16[512,256]{1,0:T(8,128)(2,1)S(1)} %copy-done.6, ...), custom_call_target="tpu_custom_call" | custom-call | tf_op jit(solution)/shard_map/pallas_call | solution.py:501
  83.2 6.0 %all-to-all-start.3 = ((bf16[64,16,128]{2,1,0:T(8,128)(2,1)}), bf16[64,16,128]{2,1,0:T(8,128)(2,1)S(1)}, u32[]{:S(2)}, u32[]{:S(2)}) async-start(bf16[64,16,128]{2,1,0:T(8,128)(2,1)} %get-tuple-element.22), calls=%async_computation.3 | async-start | bytes 524288 | tf_op jit(solution)/shard_map/all_to_all | solution.py:472
  89.2 2.8 %collective-permute-start.2 = (bf16[576,128]{1,0:T(8,128)(2,1)S(1)}, bf16[576,128]{1,0:T(8,128)(2,1)S(1)}, u32[]{:S(2)}, u32[]{:S(2)}) collective-permute-start(bf16[576,128]{1,0:T(8,128)(2,1)S(1)} %get-tuple-element.23.refs_0_), channel_id=1, source_target_pairs={{0,192},{64,0},{128,64},{192,128},{1,193},{65,1},{129,65},{193,129... | collective-permute-start | bytes 442376 | tf_op jit(solution)/shard_map/ppermute | solution.py:454
  92.0 0.3 collective-permute-start.1
  92.4 0.7 collective-permute-start
  93.1 4.8 %collective-permute-done.2.refs_3_ = bf16[576,128]{1,0:T(8,128)(2,1)S(1)} collective-permute-done((bf16[576,128]{1,0:T(8,128)(2,1)S(1)}, bf16[576,128]{1,0:T(8,128)(2,1)S(1)}, u32[]{:S(2)}, u32[]{:S(2)}) %collective-permute-start.2) | collective-permute-done | bytes 147488 | tf_op jit(solution)/shard_map/ppermute | solution.py:454
  97.9 0.4 collective-permute-done.1.refs_2_
  98.2 4.2 %collective-permute-done.refs_1_ = bf16[576,128]{1,0:T(8,128)(2,1)S(1)} collective-permute-done((bf16[576,128]{1,0:T(8,128)(2,1)S(1)}, bf16[576,128]{1,0:T(8,128)(2,1)S(1)}, u32[]{:S(2)}, u32[]{:S(2)}) %collective-permute-start) | collective-permute-done | bytes 147488 | tf_op jit(solution)/shard_map/ppermute | solution.py:454
  102.5 8.1 %shard_map.135 = f32[20,20,3,24,24]{4,3,2,1,0:T(8,128)} custom-call(bf16[576,128]{1,0:T(8,128)(2,1)S(1)} %get-tuple-element.23.refs_0_, bf16[576,128]{1,0:T(8,128)(2,1)S(1)} %collective-permute-done.refs_1_, bf16[576,128]{1,0:T(8,128)(2,1)S(1)} %collective-permute-done.1.refs_2_, bf16[576,128]{1,0:T(8,128)(2,1)S(1)} %collective-permute-done.2.refs_3_), custom_call_target="tpu_custom_call" | custom-call | flops 1000000000 | bytes 100000000 | tf_op jit(solution)/shard_map/pallas_call | solution.py:507
  110.6 0.0 all-to-all-done.3.recv_ref
  110.6 0.0 copy-start.4
  110.6 0.1 shard_map.137
  110.7 0.0 collective-permute-start.5
  110.7 1.5 %collective-permute-start.4 = (f32[24,128]{1,0:T(8,128)S(1)}, f32[24,128]{1,0:T(8,128)S(1)}, u32[]{:S(2)}, u32[]{:S(2)}) collective-permute-start(f32[24,128]{1,0:T(8,128)S(1)} %shard_map.137), channel_id=1, source_target_pairs={{0,64},{64,128},{128,192},{192,0},{1,65},{65,129},{129,193},{193,1... | collective-permute-start | bytes 36872 | tf_op jit(solution)/shard_map/ppermute | solution.py:454
  112.2 0.1 collective-permute-start.3
  112.3 0.0 copy-done.4
  112.3 7.2 %shard_map.136 = bf16[16,20,2,2048]{3,2,1,0:T(2,128)(2,1)} custom-call(bf16[64,16,128]{2,1,0:T(8,128)(2,1)} %copy-done.4, bf16[16,640,128]{2,1,0:T(8,128)(2,1)} %get-tuple-element.25.up_hbm, bf16[20,20]{1,0:T(8,128)(2,1)} %bypass_ref.3, bf16[320,20]{1,0:T(8,128)(2,1)} %constant.19.clone.channel_ref, bf16[320,384]{1,0:T(8,128)(2,1)} %constant.20.clone.same_ref, ...), custom_call_target="tpu_custom_call" | custom-call | tf_op jit(solution)/shard_map/pallas_call | solution.py:525
  119.5 0.0 collective-permute-done.5
  119.5 0.0 collective-permute-done.4
  119.6 0.0 collective-permute-done.3
  119.6 0.6 fusion
Async XLA Ops:
  5.7 25.0 %all-to-all-start = ((bf16[64,16,128]{2,1,0:T(8,128)(2,1)}), bf16[64,16,128]{2,1,0:T(8,128)(2,1)S(1)}, u32[]{:S(2)}, u32[]{:S(2)}) async-start(bf16[64,16,128]{2,1,0:T(8,128)(2,1)} %get-tuple-element.15), calls=%async_computation | async-start | bytes 524288 | tf_op jit(solution)/shard_map/all_to_all | solution.py:472
  18.7 12.0 %copy-start.5 = (bf16[360,512]{1,0:T(8,128)(2,1)S(1)}, bf16[360,512]{1,0:T(8,128)(2,1)}, u32[]{:S(2)}) copy-start(bf16[360,512]{1,0:T(8,128)(2,1)} %constant.17.clone.ya_ref) | copy-start | bytes 1105924
  18.7 12.0 %copy-start.6 = (bf16[512,256]{1,0:T(8,128)(2,1)S(1)}, bf16[512,256]{1,0:T(8,128)(2,1)}, u32[]{:S(2)}) copy-start(bf16[512,256]{1,0:T(8,128)(2,1)} %constant.16.clone.xa_ref) | copy-start | bytes 786436
  18.8 35.2 %copy-start.2 = (bf16[2048,256]{1,0:T(8,128)(2,1)S(1)}, bf16[2048,256]{1,0:T(8,128)(2,1)}, u32[]{:S(2)}) copy-start(bf16[2048,256]{1,0:T(8,128)(2,1)} %constant.14.clone.zt_hbm.ahead_ref) | copy-start | bytes 3145732
  18.8 35.2 %copy-start.3 = (bf16[192,2048]{1,0:T(8,128)(2,1)S(1)}, bf16[192,2048]{1,0:T(8,128)(2,1)}, u32[]{:S(2)}) copy-start(bf16[192,2048]{1,0:T(8,128)(2,1)} %constant.15.clone.back_ref.back_hbm) | copy-start | bytes 2359300
  18.8 35.2 %copy-start.7 = (bf16[320,384]{1,0:T(8,128)(2,1)S(1)}, bf16[320,384]{1,0:T(8,128)(2,1)}, u32[]{:S(2)}) copy-start(bf16[320,384]{1,0:T(8,128)(2,1)} %constant.20.clone.same_ref) | copy-start | bytes 737284
  18.8 35.2 %copy-start.8 = (bf16[320,20]{1,0:T(8,128)(2,1)S(1)}, bf16[320,20]{1,0:T(8,128)(2,1)}, u32[]{:S(2)}) copy-start(bf16[320,20]{1,0:T(8,128)(2,1)} %constant.19.clone.channel_ref) | copy-start | bytes 38404
  18.8 35.2 %copy-start.10 = (bf16[20,20]{1,0:T(8,128)(2,1)S(1)}, bf16[20,20]{1,0:T(8,128)(2,1)}, u32[]{:S(2)}) copy-start(bf16[20,20]{1,0:T(8,128)(2,1)} %bypass_ref.3) | copy-start | bytes 2404
  30.7 1.5 %copy-start = (bf16[20,360,128]{2,1,0:T(8,128)(2,1)S(1)}, bf16[20,360,128]{2,1,0:T(8,128)(2,1)}, u32[]{:S(2)}) copy-start(bf16[20,360,128]{2,1,0:T(8,128)(2,1)} %get-tuple-element.16.weight_ref) | copy-start | bytes 5529604
  54.0 27.1 %copy-start.1 = (bf16[20,360,128]{2,1,0:T(8,128)(2,1)S(1)}, bf16[20,360,128]{2,1,0:T(8,128)(2,1)}, u32[]{:S(2)}) copy-start(bf16[20,360,128]{2,1,0:T(8,128)(2,1)} %get-tuple-element.16.weight_ref) | copy-start | bytes 5529604
  54.0 27.1 %copy-start.9 = (bf16[128,512]{1,0:T(8,128)(2,1)S(1)}, bf16[128,512]{1,0:T(8,128)(2,1)}, u32[]{:S(2)}) copy-start(bf16[128,512]{1,0:T(8,128)(2,1)} %constant.18.clone.spread_ref) | copy-start | bytes 393220
  83.2 27.4 %all-to-all-start.3 = ((bf16[64,16,128]{2,1,0:T(8,128)(2,1)}), bf16[64,16,128]{2,1,0:T(8,128)(2,1)S(1)}, u32[]{:S(2)}, u32[]{:S(2)}) async-start(bf16[64,16,128]{2,1,0:T(8,128)(2,1)} %get-tuple-element.22), calls=%async_computation.3 | async-start | bytes 524288 | tf_op jit(solution)/shard_map/all_to_all | solution.py:472
  89.2 8.6 %collective-permute-start.2 = (bf16[576,128]{1,0:T(8,128)(2,1)S(1)}, bf16[576,128]{1,0:T(8,128)(2,1)S(1)}, u32[]{:S(2)}, u32[]{:S(2)}) collective-permute-start(bf16[576,128]{1,0:T(8,128)(2,1)S(1)} %get-tuple-element.23.refs_0_), channel_id=1, source_target_pairs={{0,192},{64,0},{128,64},{192,128},{1,193},{65,1},{129,65},{193,129... | collective-permute-start | bytes 442376 | tf_op jit(solution)/shard_map/ppermute | solution.py:454
  92.0 6.2 %collective-permute-start.1 = (bf16[576,128]{1,0:T(8,128)(2,1)S(1)}, bf16[576,128]{1,0:T(8,128)(2,1)S(1)}, u32[]{:S(2)}, u32[]{:S(2)}) collective-permute-start(bf16[576,128]{1,0:T(8,128)(2,1)S(1)} %get-tuple-element.23.refs_0_), channel_id=1, source_target_pairs={{0,128},{64,192},{128,0},{192,64},{1,129},{65,193},{129,1},{193,65... | collective-permute-start | bytes 442376 | tf_op jit(solution)/shard_map/ppermute | solution.py:454
  92.4 10.1 %collective-permute-start = (bf16[576,128]{1,0:T(8,128)(2,1)S(1)}, bf16[576,128]{1,0:T(8,128)(2,1)S(1)}, u32[]{:S(2)}, u32[]{:S(2)}) collective-permute-start(bf16[576,128]{1,0:T(8,128)(2,1)S(1)} %get-tuple-element.23.refs_0_), channel_id=1, source_target_pairs={{0,64},{64,128},{128,192},{192,0},{1,65},{65,129},{129,193},{193,1... | collective-permute-start | bytes 442376 | tf_op jit(solution)/shard_map/ppermute | solution.py:454
  110.6 1.7 %copy-start.4 = (bf16[64,16,128]{2,1,0:T(8,128)(2,1)}, bf16[64,16,128]{2,1,0:T(8,128)(2,1)S(1)}, u32[]{:S(2)}) copy-start(bf16[64,16,128]{2,1,0:T(8,128)(2,1)S(1)} %all-to-all-done.3.recv_ref) | copy-start | bytes 786436
  110.7 8.8 %collective-permute-start.5 = (f32[24,128]{1,0:T(8,128)S(1)}, f32[24,128]{1,0:T(8,128)S(1)}, u32[]{:S(2)}, u32[]{:S(2)}) collective-permute-start(f32[24,128]{1,0:T(8,128)S(1)} %shard_map.137), channel_id=1, source_target_pairs={{0,192},{64,0},{128,64},{192,128},{1,193},{65,1},{129,65},{193,129... | collective-permute-start | bytes 36872 | tf_op jit(solution)/shard_map/ppermute | solution.py:454
  110.7 8.8 %collective-permute-start.4 = (f32[24,128]{1,0:T(8,128)S(1)}, f32[24,128]{1,0:T(8,128)S(1)}, u32[]{:S(2)}, u32[]{:S(2)}) collective-permute-start(f32[24,128]{1,0:T(8,128)S(1)} %shard_map.137), channel_id=1, source_target_pairs={{0,64},{64,128},{128,192},{192,0},{1,65},{65,129},{129,193},{193,1... | collective-permute-start | bytes 36872 | tf_op jit(solution)/shard_map/ppermute | solution.py:454
  112.2 7.4 %collective-permute-start.3 = (f32[24,128]{1,0:T(8,128)S(1)}, f32[24,128]{1,0:T(8,128)S(1)}, u32[]{:S(2)}, u32[]{:S(2)}) collective-permute-start(f32[24,128]{1,0:T(8,128)S(1)} %shard_map.137), channel_id=1, source_target_pairs={{0,128},{64,192},{128,0},{192,64},{1,129},{65,193},{129,1},{193,65... | collective-permute-start | bytes 36872 | tf_op jit(solution)/shard_map/ppermute | solution.py:454

commit v5 on v4

--- a/solution.py
+++ b/solution.py
@@ -71,7 +71,6 @@
     y_ahead = np.einsum("gyl,rs->slygr", fy.reshape(PY, CY, KY), slots).reshape(
         SPEC, CY * PY * CHUNK
     )
-    spread = np.einsum("cd,kl,e->ckdel", eye4, np.eye(32), np.ones(4)).reshape(128, 512)
     channel = np.einsum("jk,x,cd,y->jxcykd", np.eye(GROUPS), np.ones(XB), eye4, np.ones(CY))
     channel = channel.reshape(BLOCK, C)
     cell = np.einsum("j,xw,c,yz->jxcywz", np.ones(GROUPS), np.eye(XB), np.ones(4), eye2)
@@ -81,7 +80,6 @@
         "zt_back": by_slot.T,
         "x_ahead": x_ahead,
         "y_ahead": y_ahead,
-        "spread": spread,
         "channel": channel,
         "same": np.concatenate([np.zeros((BLOCK, 64)), cell @ cell.T], axis=1),
     }
@@ -176,10 +174,7 @@
         copy.wait()
 
 
-def weights_kernel(weight_ref, cot_ref, out_ref, rows_ref, sems):
-    made = copies(cot_ref, rows_ref, sems)
-    for copy in made:
-        copy.start()
+def weights_kernel(weight_ref, out_ref):
     gap = jnp.zeros((8, KY), F32)
 
     def one(o, carry):
@@ -194,8 +189,6 @@
         return carry
 
     lax.fori_loop(0, C, one, 0)
-    for copy in made:
-        copy.wait()
 
 
 def to_modes(recv_ref, x_ref, y_ref):
@@ -267,12 +260,14 @@
 
 
 def mix_back_kernel(
-    recv_ref, weight_ref, spread_ref, xa_ref, ya_ref, own_ref, send_ref, spec_ref, stage,
+    recv_ref, weight_ref, xa_ref, ya_ref, send_ref, spec_ref, stage,
 ):
     spec = to_modes(recv_ref, xa_ref, ya_ref)
-    spec_ref[pl.ds(0, 3 * PACK), :] = own_ref[...]
-    spec_ref[pl.ds(3 * PACK, 3 * PACK), :] = pack_modes(spec.astype(F32))
-    copied = dot(spec, spread_ref[...])
+    spec_ref[...] = pack_modes(spec.astype(F32))
+    row = lax.broadcasted_iota(jnp.int32, (128, 512), 0)
+    column = lax.broadcasted_iota(jnp.int32, (128, 512), 1)
+    spread = (row // 32 == column // 128) & (row % 32 == column % 32)
+    copied = dot(spec, spread.astype(F32).astype(BF16))
     modes = [jnp.zeros((KY, 128), F32) for _ in range(Q3 * GROUPS)]
     for o in range(C):
         weight = weight_ref[o].astype(F32)
@@ -330,19 +325,18 @@
 
 def point_kernel(
     recv_ref, field_hbm, cot_hbm, bypass_ref, channel_ref, same_ref, back_ref, ahead_ref,
-    send_ref, up_hbm, field_ref, cot_ref, up_ref, stage, left, coeff, cross, sems,
+    send_ref, up_hbm, field_ref, cot_cells, up_ref, stage, left, coeff, cross, sems, cot_sems,
 ):
     field_hbm = field_hbm.reshape(TILES, ROWS, 128)
-    cot_hbm = cot_hbm.reshape(TILES, ROWS, 128)
+    cot_ref = cot_cells.reshape(TILES, ROWS, 128)
+    cot_made = copies(cot_hbm, cot_cells, cot_sems)
     made = []
     for n in range(STEPS):
         some = pl.ds(PER * n, PER)
-        made.append(
-            start_all(
-                (field_hbm.at[some], field_ref.at[some], sems.at[1, n]),
-                (cot_hbm.at[some], cot_ref.at[some], sems.at[2, n]),
-            )
-        )
+        made.append(start_all((field_hbm.at[some], field_ref.at[some], sems.at[1, n])))
+        made[n] += cot_made[PER * n * GROUPS : PER * (n + 1) * GROUPS]
+        for copy in made[n][1:]:
+            copy.start()
     bypass_matrix(bypass_ref, channel_ref, same_ref, ((1,), (1,)), left)
     unpack_chunks(recv_ref, stage, left)
     coeff[...] = jnp.zeros_like(coeff)
@@ -414,14 +408,13 @@
 
 
 def outer_kernel(*refs):
-    out_ref, first, second = refs[4:]
+    out_ref, first, second = refs[8:]
 
     @pl.when(pl.program_id(0) == 0)
     def _():
         for b in range(4):
-            both = refs[b][...].astype(F32)
-            turn(unpack_modes(both[: 3 * PACK]), b, first)
-            turn(unpack_modes(both[3 * PACK :]), b, second)
+            turn(unpack_modes(refs[b][...].astype(F32)), b, first)
+            turn(unpack_modes(refs[4 + b][...].astype(F32)), b, second)
 
     c = pl.program_id(0) * PAIR
     for s in range(Q3):
@@ -478,10 +471,9 @@
         out_specs=(VMEM, HBM), limit=62,
     )(field_t, table["zt_ahead"])
     recv = exchange(send)
-    weight, cot_rows = call(
-        weights_kernel, (shape((C, SPEC, 128), BF16), cells), [VMEM, HBM], [sems],
-        out_specs=(VMEM,) * 2, limit=60,
-    )(weight_t, cot_t)
+    weight = call(
+        weights_kernel, shape((C, SPEC, 128), BF16), [VMEM], [], out_specs=VMEM,
+    )(weight_t)
     send, own = call(
         mix_kernel, (chunks, shape((3 * PACK, 128), BF16)), [VMEM] * 4,
         [pltpu.VMEM((SPEC, 128), F32)], out_specs=(VMEM,) * 2, limit=12,
@@ -492,23 +484,25 @@
     back = pltpu.VMEM((NQ, NP), BF16)
     send, up = call(
         point_kernel, (chunks, rows), [VMEM, HBM, HBM] + [VMEM] * 5,
-        [held, held, held, stage, left, pltpu.VMEM((ROWS, 256), F32),
-         pltpu.VMEM((BLOCK, BLOCK), F32), dma(3, STEPS)],
+        [held, pltpu.VMEM(cells.shape, BF16), held, stage, left, pltpu.VMEM((ROWS, 256), F32),
+         pltpu.VMEM((BLOCK, BLOCK), F32), dma(2, STEPS), sems],
         out_specs=(VMEM, HBM), limit=51,
-    )(recv, field_rows, cot_rows, bypass_weight, table["channel"], table["same"],
+    )(recv, field_rows, cot_t, bypass_weight, table["channel"], table["same"],
       table["zt_back"], table["zt_ahead"])
     recv = exchange(send)
-    send, both = call(
-        mix_back_kernel, (chunks, shape((6 * PACK, 128), BF16)), [VMEM] * 6, [stage],
+    specs = around(own)
+    recv, *specs = lax.optimization_barrier((recv, *specs))
+    send, spec_up = call(
+        mix_back_kernel, (chunks, shape((3 * PACK, 128), BF16)), [VMEM] * 4, [stage],
         out_specs=(VMEM,) * 2,
-    )(recv, weight, table["spread"], table["x_ahead"], table["y_ahead"], own)
+    )(recv, weight, table["x_ahead"], table["y_ahead"])
     recv = exchange(send)
-    specs = around(both)
+    specs += around(spec_up)
     grad_spectral = pl.pallas_call(
         outer_kernel,
         grid=(C // PAIR,),
         out_shape=shape((C, C, Q3, KX, KY), F32),
-        in_specs=[VMEM] * 4,
+        in_specs=[VMEM] * 8,
         out_specs=pl.BlockSpec((PAIR, C, Q3, KX, KY), lambda c: (c, 0, 0, 0, 0)),
         scratch_shapes=[pltpu.VMEM((C, Q3, 4, KX, KY), F32)] * 2,
         compiler_params=pltpu.CompilerParams(vmem_limit_bytes=24 * MIB),

time: 121 us -> 119 us (0.983); the launches traced: 120 us -> 117 us
  blocking collectives: 38 us -> 17.8 us
  starting transfers between devices: 24.5 us -> 35.2 us
  waiting for transfers between devices: 11.4 us -> 19.2 us
  Pallas kernels: 43.3 us -> 38.3 us
  local copies, waits for them, and re-layouts: 1.57 us -> 4.78 us
    all_to_all x2 -> x1, blocking collectives: 38 us -> 17.8 us  [exchange(): return lax.all_to_all(value, ('gx', 'gy'), 0, 0, tiled=True)]
    all_to_all x2 -> x3, starting transfers between devices: 19 us -> 27.9 us  [exchange(): return lax.all_to_all(value, ('gx', 'gy'), 0, 0, tiled=True)]
    pallas_call x2, Pallas kernels: 12 us -> 5.56 us  [the longest x1 3.46 us: body(): call(weights_kernel, shape((C, SPEC, 128), BF16), [VMEM], [], out_specs=V...]
    all_to_all x2 -> x3, waiting for transfers between devices: 1.98 us -> 7.7 us  [exchange(): return lax.all_to_all(value, ('gx', 'gy'), 0, 0, tiled=True)]
    unnamed x22 -> x26, local copies, waits for them, and re-layouts: 1.57 us -> 4.78 us
    ppermute x6 -> x9, waiting for transfers between devices: 9.4 us -> 11.5 us  [around(): lax.ppermute(value, 'dp', [(i, (i + k) % 4) for i in range(4)])]
    ppermute x6 -> x9, starting transfers between devices: 5.43 us -> 7.33 us  [around(): lax.ppermute(value, 'dp', [(i, (i + k) % 4) for i in range(4)])]
    pallas_call x1, Pallas kernels: 9.24 us -> 10.7 us  [body(): call(point_kernel, (chunks, rows), [VMEM, HBM, HBM] + [VMEM] * 5, [held,...]
  transfers between devices with their start and end apart: 8 -> 12, of which waited for: 4 -> 8; matrix products, arithmetic and copies ran while one was open for 0% -> 0% of each run, Pallas kernels for 21% -> 16%
where the time goes in v5:
time: 119 us; the launch traced here: 117 us
  Pallas kernels  38.3 us (32%)
  starting transfers between devices  35.2 us (30%)
  waiting for transfers between devices  19.2 us (16%)
  blocking collectives  17.8 us (15%)
  local copies, waits for them, and re-layouts  4.78 us (4%)
    all_to_all x3, starting transfers between devices, exchange(): return lax.all_to_all(value, ('gx', 'gy'), 0, 0, tiled=True)  27.9 us
    all_to_all x1, blocking collectives, exchange(): return lax.all_to_all(value, ('gx', 'gy'), 0, 0, tiled=True)  17.8 us
    ppermute x9, waiting for transfers between devices, around(): lax.ppermute(value, 'dp', [(i, (i + k) % 4) for i in range(4)])  11.5 us
    pallas_call x1, Pallas kernels, body(): call(point_kernel, (chunks, rows), [VMEM, HBM, HBM] + [VMEM] * 5, [held,...  10.7 us
    pallas_call x1, Pallas kernels, body(): pl.pallas_call(outer_kernel, grid=(C // PAIR,), out_shape=shape((C, C, Q3...  8.13 us
    all_to_all x3, waiting for transfers between devices, exchange(): return lax.all_to_all(value, ('gx', 'gy'), 0, 0, tiled=True)  7.7 us
    ppermute x9, starting transfers between devices, around(): lax.ppermute(value, 'dp', [(i, (i + k) % 4) for i in range(4)])  7.33 us
    pallas_call x1, Pallas kernels, body(): call(final_kernel, shape((CX, C, CY, NP), BF16), [VMEM, HBM, VMEM, VMEM,...  7.24 us
  transfers between devices with their start and end apart: 12, of which 8 were waited for; matrix products, arithmetic and copies ran while one was open for 0% of the time, Pallas kernels for 16%

profile of v5, /device:TPU:1, one launch (start us, length us, event | category | flops | bytes accessed | tf_op | source)
XLA Modules:
  0.0 116.8 jit_solution(16822805306245861732)
XLA Ops:
  0.6 5.1 %shard_map.121 = (bf16[64,16,128]{2,1,0:T(8,128)(2,1)}, bf16[16,5,16,4,2,128]{5,4,3,2,1,0:T(2,128)(2,1)}) custom-call(bf16[16,20,2,2048]{3,2,1,0:T(2,128)(2,1)} %bitcast.13, bf16[2048,256]{1,0:T(8,128)(2,1)} %constant.12.clone.zt_hbm.ahead_ref), custom_call_target="tpu_custom_call" | custom-call | tf_op jit(solution)/shard_map/pallas_call | solution.py:467
  5.7 13.0 %all-to-all-start = ((bf16[64,16,128]{2,1,0:T(8,128)(2,1)}), bf16[64,16,128]{2,1,0:T(8,128)(2,1)S(1)}, u32[]{:S(2)}, u32[]{:S(2)}) async-start(bf16[64,16,128]{2,1,0:T(8,128)(2,1)} %get-tuple-element.18), calls=%async_computation | async-start | bytes 524288 | tf_op jit(solution)/shard_map/all_to_all | solution.py:465
  18.7 0.0 copy-start
  18.7 3.1 %copy-done = bf16[24,24,20,20,3]{1,0,4,3,2:T(8,128)(2,1)S(1)} copy-done((bf16[24,24,20,20,3]{1,0,4,3,2:T(8,128)(2,1)S(1)}, bf16[24,24,20,20,3]{1,0,4,3,2:T(8,128)(2,1)}, u32[]{:S(2)}) %copy-start) | copy-done | bytes 1382424
  21.8 0.0 copy-start.4
  21.8 3.5 %shard_map.122.weight_ref = bf16[20,360,128]{2,1,0:T(8,128)(2,1)S(1)} custom-call(bf16[20,20,3,24,24]{4,3,2,1,0:T(8,128)(2,1)S(1)} %bitcast.11), custom_call_target="tpu_custom_call" | custom-call | tf_op jit(solution)/shard_map/pallas_call | solution.py:474
  25.3 0.0 copy-start.1
  25.3 5.4 %all-to-all-done.recv_ref = bf16[64,16,128]{2,1,0:T(8,128)(2,1)S(1)} async-done(((bf16[64,16,128]{2,1,0:T(8,128)(2,1)}), bf16[64,16,128]{2,1,0:T(8,128)(2,1)S(1)}, u32[]{:S(2)}, u32[]{:S(2)}) %all-to-all-start) | async-done | bytes 262176 | tf_op jit(solution)/shard_map/all_to_all | solution.py:465
  30.7 0.0 copy-done.4
  30.7 0.0 copy-start.5
  30.7 0.9 copy-done.5
  31.7 0.0 copy-start.2
  31.7 0.0 copy-start.7
  31.7 0.0 copy-start.8
  31.7 0.0 copy-start.12
  31.7 1.5 %shard_map.123 = (bf16[64,16,128]{2,1,0:T(8,128)(2,1)S(1)}, bf16[288,128]{1,0:T(8,128)(2,1)S(1)}) custom-call(bf16[64,16,128]{2,1,0:T(8,128)(2,1)S(1)} %all-to-all-done.recv_ref, bf16[20,360,128]{2,1,0:T(8,128)(2,1)S(1)} %shard_map.122.weight_ref, bf16[512,256]{1,0:T(8,128)(2,1)S(1)} %copy-done.5, bf16[360,512]{1,0:T(8,128)(2,1)S(1)} %copy-done.4), custom_call_target="tpu_custom_call" | custom-call | tf_op jit(solution)/shard_map/pallas_call | solution.py:477
  33.2 0.0 copy-start.10
  33.2 17.8 %all_to_all.20.recv_ref = bf16[64,16,128]{2,1,0:T(8,128)(2,1)S(1)} all-to-all(bf16[64,16,128]{2,1,0:T(8,128)(2,1)S(1)} %get-tuple-element.19), channel_id=1, replica_groups=mesh['dp'=4,'gx'=4,'gy'=16] {'gx','gy'}, dimensions={0} | all-to-all | bytes 524288 | tf_op jit(solution)/shard_map/all_to_all | solution.py:465
  51.0 0.0 copy-done.10
  51.1 0.0 copy-done.1
  51.1 0.0 copy-done.2
  51.1 0.0 copy-done.7
  51.1 0.0 copy-done.8
  51.1 0.0 copy-done.12
  51.1 0.0 copy-start.6
  51.1 10.7 %shard_map.124 = (bf16[64,16,128]{2,1,0:T(8,128)(2,1)S(1)}, bf16[16,640,128]{2,1,0:T(8,128)(2,1)}) custom-call(bf16[64,16,128]{2,1,0:T(8,128)(2,1)S(1)} %all_to_all.20.recv_ref, bf16[16,5,16,4,2,128]{5,4,3,2,1,0:T(2,128)(2,1)} %get-tuple-element.20.field_hbm, bf16[16,20,2,2048]{3,2,1,0:T(2,128)(2,1)} %bitcast.14, bf16[20,20]{1,0:T(8,128)(2,1)S(1)} %copy-done.12, ...), custom_call_target="tpu_custom_call" | custom-call | tf_op jit(solution)/shard_map/pallas_call | solution.py:485
  61.8 0.0 copy-start.9
  61.9 0.7 copy-done.9
  62.6 0.0 copy-start.11
  62.6 6.2 %all-to-all-start.2 = ((bf16[64,16,128]{2,1,0:T(8,128)(2,1)}), bf16[64,16,128]{2,1,0:T(8,128)(2,1)S(1)}, u32[]{:S(2)}, u32[]{:S(2)}) async-start(bf16[64,16,128]{2,1,0:T(8,128)(2,1)} %copy-done.9), calls=%async_computation.2 | async-start | bytes 524288 | tf_op jit(solution)/shard_map/all_to_all | solution.py:465
  68.7 2.8 %collective-permute-start.2 = (bf16[288,128]{1,0:T(8,128)(2,1)}, bf16[288,128]{1,0:T(8,128)(2,1)S(1)}, u32[]{:S(2)}, u32[]{:S(2)}) collective-permute-start(bf16[288,128]{1,0:T(8,128)(2,1)} %copy-done.10), channel_id=1, source_target_pairs={{0,192},{64,0},{128,64},{192,128},{1,193},{65,1},{129,65},{193,129... | collective-permute-start | bytes 221192 | tf_op jit(solution)/shard_map/ppermute | solution.py:447
  71.5 0.4 collective-permute-start.1
  71.9 0.7 collective-permute-start
  72.6 0.7 collective-permute-done.2.refs_3_
  73.3 3.5 %collective-permute-done.1.refs_2_ = bf16[288,128]{1,0:T(8,128)(2,1)S(1)} collective-permute-done((bf16[288,128]{1,0:T(8,128)(2,1)}, bf16[288,128]{1,0:T(8,128)(2,1)S(1)}, u32[]{:S(2)}, u32[]{:S(2)}) %collective-permute-start.1) | collective-permute-done | bytes 73760 | tf_op jit(solution)/shard_map/ppermute | solution.py:447
  76.8 1.7 %collective-permute-done.refs_1_ = bf16[288,128]{1,0:T(8,128)(2,1)S(1)} collective-permute-done((bf16[288,128]{1,0:T(8,128)(2,1)}, bf16[288,128]{1,0:T(8,128)(2,1)S(1)}, u32[]{:S(2)}, u32[]{:S(2)}) %collective-permute-start) | collective-permute-done | bytes 73760 | tf_op jit(solution)/shard_map/ppermute | solution.py:447
  78.5 2.3 %all-to-all-done.2.recv_ref = bf16[64,16,128]{2,1,0:T(8,128)(2,1)S(1)} async-done(((bf16[64,16,128]{2,1,0:T(8,128)(2,1)}), bf16[64,16,128]{2,1,0:T(8,128)(2,1)S(1)}, u32[]{:S(2)}, u32[]{:S(2)}) %all-to-all-start.2) | async-done | bytes 262176 | tf_op jit(solution)/shard_map/all_to_all | solution.py:465
  80.7 0.0 copy-done.6
  80.7 2.1 %shard_map.125 = (bf16[64,16,128]{2,1,0:T(8,128)(2,1)}, bf16[288,128]{1,0:T(8,128)(2,1)S(1)}) custom-call(bf16[64,16,128]{2,1,0:T(8,128)(2,1)S(1)} %all-to-all-done.2.recv_ref, bf16[20,360,128]{2,1,0:T(8,128)(2,1)S(1)} %shard_map.122.weight_ref, bf16[512,256]{1,0:T(8,128)(2,1)S(1)} %copy-done.6, bf16[360,512]{1,0:T(8,128)(2,1)S(1)} %copy-done.4), custom_call_target="tpu_custom_call" | custom-call | tf_op jit(solution)/shard_map/pallas_call | solution.py:495
  82.8 8.7 %all-to-all-start.3 = ((bf16[64,16,128]{2,1,0:T(8,128)(2,1)}), bf16[64,16,128]{2,1,0:T(8,128)(2,1)S(1)}, u32[]{:S(2)}, u32[]{:S(2)}) async-start(bf16[64,16,128]{2,1,0:T(8,128)(2,1)} %get-tuple-element.24), calls=%async_computation.3 | async-start | bytes 524288 | tf_op jit(solution)/shard_map/all_to_all | solution.py:465
  91.6 0.4 collective-permute-start.5
  92.0 0.5 collective-permute-start.4
  92.4 0.8 collective-permute-start.3
  93.2 2.0 %collective-permute-done.5.refs_7_ = bf16[288,128]{1,0:T(8,128)(2,1)S(1)} collective-permute-done((bf16[288,128]{1,0:T(8,128)(2,1)S(1)}, bf16[288,128]{1,0:T(8,128)(2,1)S(1)}, u32[]{:S(2)}, u32[]{:S(2)}) %collective-permute-start.5) | collective-permute-done | bytes 73760 | tf_op jit(solution)/shard_map/ppermute | solution.py:447
  95.2 1.5 %collective-permute-done.4.refs_6_ = bf16[288,128]{1,0:T(8,128)(2,1)S(1)} collective-permute-done((bf16[288,128]{1,0:T(8,128)(2,1)S(1)}, bf16[288,128]{1,0:T(8,128)(2,1)S(1)}, u32[]{:S(2)}, u32[]{:S(2)}) %collective-permute-start.4) | collective-permute-done | bytes 73760 | tf_op jit(solution)/shard_map/ppermute | solution.py:447
  96.7 2.2 %collective-permute-done.3.refs_5_ = bf16[288,128]{1,0:T(8,128)(2,1)S(1)} collective-permute-done((bf16[288,128]{1,0:T(8,128)(2,1)S(1)}, bf16[288,128]{1,0:T(8,128)(2,1)S(1)}, u32[]{:S(2)}, u32[]{:S(2)}) %collective-permute-start.3) | collective-permute-done | bytes 73760 | tf_op jit(solution)/shard_map/ppermute | solution.py:447
  98.8 0.0 copy-done.11
  98.8 8.1 %shard_map.126 = f32[20,20,3,24,24]{4,3,2,1,0:T(8,128)} custom-call(bf16[288,128]{1,0:T(8,128)(2,1)S(1)} %copy-done.11, bf16[288,128]{1,0:T(8,128)(2,1)S(1)} %collective-permute-done.refs_1_, bf16[288,128]{1,0:T(8,128)(2,1)S(1)} %collective-permute-done.1.refs_2_, bf16[288,128]{1,0:T(8,128)(2,1)S(1)} %collective-permute-done.2.refs_3_, ...), custom_call_target="tpu_custom_call" | custom-call | flops 1000000000 | bytes 100000000 | tf_op jit(solution)/shard_map/pallas_call | solution.py:501
  107.0 0.0 all-to-all-done.3.recv_ref
  107.0 0.0 copy-start.3
  107.0 0.1 shard_map.128
  107.1 0.4 collective-permute-start.8
  107.5 1.1 collective-permute-start.7
  108.6 0.4 collective-permute-start.6
  108.9 0.0 copy-done.3
  108.9 7.2 %shard_map.127 = bf16[16,20,2,2048]{3,2,1,0:T(2,128)(2,1)} custom-call(bf16[64,16,128]{2,1,0:T(8,128)(2,1)} %copy-done.3, bf16[16,640,128]{2,1,0:T(8,128)(2,1)} %get-tuple-element.31.up_hbm, bf16[20,20]{1,0:T(8,128)(2,1)} %bypass_ref.3, bf16[320,20]{1,0:T(8,128)(2,1)} %constant.16.clone.channel_ref, bf16[320,384]{1,0:T(8,128)(2,1)} %constant.17.clone.same_ref, ...), custom_call_target="tpu_custom_call" | custom-call | tf_op jit(solution)/shard_map/pallas_call | solution.py:519
  116.2 0.0 collective-permute-done.8
  116.2 0.0 collective-permute-done.7
  116.2 0.0 collective-permute-done.6
  116.2 0.6 fusion
Async XLA Ops:
  5.7 25.0 %all-to-all-start = ((bf16[64,16,128]{2,1,0:T(8,128)(2,1)}), bf16[64,16,128]{2,1,0:T(8,128)(2,1)S(1)}, u32[]{:S(2)}, u32[]{:S(2)}) async-start(bf16[64,16,128]{2,1,0:T(8,128)(2,1)} %get-tuple-element.18), calls=%async_computation | async-start | bytes 524288 | tf_op jit(solution)/shard_map/all_to_all | solution.py:465
  18.7 3.1 %copy-start = (bf16[24,24,20,20,3]{1,0,4,3,2:T(8,128)(2,1)S(1)}, bf16[24,24,20,20,3]{1,0,4,3,2:T(8,128)(2,1)}, u32[]{:S(2)}) copy-start(bf16[24,24,20,20,3]{1,0,4,3,2:T(8,128)(2,1)} %param.12) | copy-start | bytes 4147204
  21.8 8.9 %copy-start.4 = (bf16[360,512]{1,0:T(8,128)(2,1)S(1)}, bf16[360,512]{1,0:T(8,128)(2,1)}, u32[]{:S(2)}) copy-start(bf16[360,512]{1,0:T(8,128)(2,1)} %constant.15.clone.ya_ref) | copy-start | bytes 1105924
  25.3 25.8 %copy-start.1 = (bf16[2048,256]{1,0:T(8,128)(2,1)S(1)}, bf16[2048,256]{1,0:T(8,128)(2,1)}, u32[]{:S(2)}) copy-start(bf16[2048,256]{1,0:T(8,128)(2,1)} %constant.12.clone.zt_hbm.ahead_ref) | copy-start | bytes 3145732
  30.7 1.0 copy-start.5
  31.7 19.4 %copy-start.2 = (bf16[192,2048]{1,0:T(8,128)(2,1)S(1)}, bf16[192,2048]{1,0:T(8,128)(2,1)}, u32[]{:S(2)}) copy-start(bf16[192,2048]{1,0:T(8,128)(2,1)} %constant.13.clone.back_ref.back_hbm) | copy-start | bytes 2359300
  31.7 19.4 %copy-start.7 = (bf16[320,384]{1,0:T(8,128)(2,1)S(1)}, bf16[320,384]{1,0:T(8,128)(2,1)}, u32[]{:S(2)}) copy-start(bf16[320,384]{1,0:T(8,128)(2,1)} %constant.17.clone.same_ref) | copy-start | bytes 737284
  31.7 19.4 %copy-start.8 = (bf16[320,20]{1,0:T(8,128)(2,1)S(1)}, bf16[320,20]{1,0:T(8,128)(2,1)}, u32[]{:S(2)}) copy-start(bf16[320,20]{1,0:T(8,128)(2,1)} %constant.16.clone.channel_ref) | copy-start | bytes 38404
  31.7 19.4 %copy-start.12 = (bf16[20,20]{1,0:T(8,128)(2,1)S(1)}, bf16[20,20]{1,0:T(8,128)(2,1)}, u32[]{:S(2)}) copy-start(bf16[20,20]{1,0:T(8,128)(2,1)} %bypass_ref.3) | copy-start | bytes 2404
  33.2 17.8 %copy-start.10 = (bf16[288,128]{1,0:T(8,128)(2,1)}, bf16[288,128]{1,0:T(8,128)(2,1)S(1)}, u32[]{:S(2)}) copy-start(bf16[288,128]{1,0:T(8,128)(2,1)S(1)} %get-tuple-element.25.refs_0_) | copy-start | bytes 221188
  51.1 29.6 %copy-start.6 = (bf16[512,256]{1,0:T(8,128)(2,1)S(1)}, bf16[512,256]{1,0:T(8,128)(2,1)}, u32[]{:S(2)}) copy-start(bf16[512,256]{1,0:T(8,128)(2,1)} %constant.14.clone.xa_ref) | copy-start | bytes 786436
  61.8 0.7 copy-start.9
  62.6 36.3 %copy-start.11 = (bf16[288,128]{1,0:T(8,128)(2,1)S(1)}, bf16[288,128]{1,0:T(8,128)(2,1)}, u32[]{:S(2)}) copy-start(bf16[288,128]{1,0:T(8,128)(2,1)} %copy-done.10) | copy-start | bytes 221188
  62.6 18.2 %all-to-all-start.2 = ((bf16[64,16,128]{2,1,0:T(8,128)(2,1)}), bf16[64,16,128]{2,1,0:T(8,128)(2,1)S(1)}, u32[]{:S(2)}, u32[]{:S(2)}) async-start(bf16[64,16,128]{2,1,0:T(8,128)(2,1)} %copy-done.9), calls=%async_computation.2 | async-start | bytes 524288 | tf_op jit(solution)/shard_map/all_to_all | solution.py:465
  68.7 4.5 %collective-permute-start.2 = (bf16[288,128]{1,0:T(8,128)(2,1)}, bf16[288,128]{1,0:T(8,128)(2,1)S(1)}, u32[]{:S(2)}, u32[]{:S(2)}) collective-permute-start(bf16[288,128]{1,0:T(8,128)(2,1)} %copy-done.10), channel_id=1, source_target_pairs={{0,192},{64,0},{128,64},{192,128},{1,193},{65,1},{129,65},{193,129... | collective-permute-start | bytes 221192 | tf_op jit(solution)/shard_map/ppermute | solution.py:447
  71.5 5.2 %collective-permute-start.1 = (bf16[288,128]{1,0:T(8,128)(2,1)}, bf16[288,128]{1,0:T(8,128)(2,1)S(1)}, u32[]{:S(2)}, u32[]{:S(2)}) collective-permute-start(bf16[288,128]{1,0:T(8,128)(2,1)} %copy-done.10), channel_id=1, source_target_pairs={{0,128},{64,192},{128,0},{192,64},{1,129},{65,193},{129,1},{193,65... | collective-permute-start | bytes 221192 | tf_op jit(solution)/shard_map/ppermute | solution.py:447
  71.9 6.6 %collective-permute-start = (bf16[288,128]{1,0:T(8,128)(2,1)}, bf16[288,128]{1,0:T(8,128)(2,1)S(1)}, u32[]{:S(2)}, u32[]{:S(2)}) collective-permute-start(bf16[288,128]{1,0:T(8,128)(2,1)} %copy-done.10), channel_id=1, source_target_pairs={{0,64},{64,128},{128,192},{192,0},{1,65},{65,129},{129,193},{193,1... | collective-permute-start | bytes 221192 | tf_op jit(solution)/shard_map/ppermute | solution.py:447
  82.8 24.1 %all-to-all-start.3 = ((bf16[64,16,128]{2,1,0:T(8,128)(2,1)}), bf16[64,16,128]{2,1,0:T(8,128)(2,1)S(1)}, u32[]{:S(2)}, u32[]{:S(2)}) async-start(bf16[64,16,128]{2,1,0:T(8,128)(2,1)} %get-tuple-element.24), calls=%async_computation.3 | async-start | bytes 524288 | tf_op jit(solution)/shard_map/all_to_all | solution.py:465
  91.6 3.6 %collective-permute-start.5 = (bf16[288,128]{1,0:T(8,128)(2,1)S(1)}, bf16[288,128]{1,0:T(8,128)(2,1)S(1)}, u32[]{:S(2)}, u32[]{:S(2)}) collective-permute-start(bf16[288,128]{1,0:T(8,128)(2,1)S(1)} %get-tuple-element.29.refs_4_), channel_id=1, source_target_pairs={{0,192},{64,0},{128,64},{192,128},{1,193},{65,1},{129,65},{193,129... | collective-permute-start | bytes 221192 | tf_op jit(solution)/shard_map/ppermute | solution.py:447
  92.0 4.7 %collective-permute-start.4 = (bf16[288,128]{1,0:T(8,128)(2,1)S(1)}, bf16[288,128]{1,0:T(8,128)(2,1)S(1)}, u32[]{:S(2)}, u32[]{:S(2)}) collective-permute-start(bf16[288,128]{1,0:T(8,128)(2,1)S(1)} %get-tuple-element.29.refs_4_), channel_id=1, source_target_pairs={{0,128},{64,192},{128,0},{192,64},{1,129},{65,193},{129,1},{193,65... | collective-permute-start | bytes 221192 | tf_op jit(solution)/shard_map/ppermute | solution.py:447
  92.4 6.4 %collective-permute-start.3 = (bf16[288,128]{1,0:T(8,128)(2,1)S(1)}, bf16[288,128]{1,0:T(8,128)(2,1)S(1)}, u32[]{:S(2)}, u32[]{:S(2)}) collective-permute-start(bf16[288,128]{1,0:T(8,128)(2,1)S(1)} %get-tuple-element.29.refs_4_), channel_id=1, source_target_pairs={{0,64},{64,128},{128,192},{192,0},{1,65},{65,129},{129,193},{193,1... | collective-permute-start | bytes 221192 | tf_op jit(solution)/shard_map/ppermute | solution.py:447
  107.0 2.0 %copy-start.3 = (bf16[64,16,128]{2,1,0:T(8,128)(2,1)}, bf16[64,16,128]{2,1,0:T(8,128)(2,1)S(1)}, u32[]{:S(2)}) copy-start(bf16[64,16,128]{2,1,0:T(8,128)(2,1)S(1)} %all-to-all-done.3.recv_ref) | copy-start | bytes 786436
  107.1 9.1 %collective-permute-start.8 = (f32[24,128]{1,0:T(8,128)S(1)}, f32[24,128]{1,0:T(8,128)S(1)}, u32[]{:S(2)}, u32[]{:S(2)}) collective-permute-start(f32[24,128]{1,0:T(8,128)S(1)} %shard_map.128), channel_id=1, source_target_pairs={{0,192},{64,0},{128,64},{192,128},{1,193},{65,1},{129,65},{193,129... | collective-permute-start | bytes 36872 | tf_op jit(solution)/shard_map/ppermute | solution.py:447
  107.5 8.7 %collective-permute-start.7 = (f32[24,128]{1,0:T(8,128)S(1)}, f32[24,128]{1,0:T(8,128)S(1)}, u32[]{:S(2)}, u32[]{:S(2)}) collective-permute-start(f32[24,128]{1,0:T(8,128)S(1)} %shard_map.128), channel_id=1, source_target_pairs={{0,64},{64,128},{128,192},{192,0},{1,65},{65,129},{129,193},{193,1... | collective-permute-start | bytes 36872 | tf_op jit(solution)/shard_map/ppermute | solution.py:447
  108.6 7.7 %collective-permute-start.6 = (f32[24,128]{1,0:T(8,128)S(1)}, f32[24,128]{1,0:T(8,128)S(1)}, u32[]{:S(2)}, u32[]{:S(2)}) collective-permute-start(f32[24,128]{1,0:T(8,128)S(1)} %shard_map.128), channel_id=1, source_target_pairs={{0,128},{64,192},{128,0},{192,64},{1,129},{65,193},{129,1},{193,65... | collective-permute-start | bytes 36872 | tf_op jit(solution)/shard_map/ppermute | solution.py:447

commit v6 on v5

--- a/solution.py
+++ b/solution.py
@@ -94,9 +94,9 @@
     )
 
 
-def copies(field_ref, rows_ref, sems, back=False):
+def copies(field_ref, rows_ref, sems, back=False, tiles=range(TILES)):
     made = []
-    for tile in range(TILES):
+    for tile in tiles:
         for j in range(GROUPS):
             outer = field_ref.at[:, pl.ds(4 * j, 4), :, pl.ds(128 * tile, 128)]
             inner = rows_ref.at[tile, j]
@@ -191,6 +191,19 @@
     lax.fori_loop(0, C, one, 0)
 
 
+HALF = TILES // 2
+
+
+def half_kernel(cot_ref, half_hbm, half_ref, sems, out_sem):
+    made = copies(cot_ref, half_ref, sems, tiles=range(HALF))
+    for copy in made:
+        copy.start()
+    for copy in made:
+        copy.wait()
+    for copy in start_all((half_ref, half_hbm, out_sem)):
+        copy.wait()
+
+
 def to_modes(recv_ref, x_ref, y_ref):
     pieces = recv_ref[...].reshape(PX, PY * CHUNK, 128)
     wide = jnp.concatenate([pieces[g] for g in range(PX)], axis=1)
@@ -324,19 +337,24 @@
 
 
 def point_kernel(
-    recv_ref, field_hbm, cot_hbm, bypass_ref, channel_ref, same_ref, back_ref, ahead_ref,
+    recv_ref, field_hbm, half_hbm, cot_hbm, bypass_ref, channel_ref, same_ref, back_ref, ahead_ref,
     send_ref, up_hbm, field_ref, cot_cells, up_ref, stage, left, coeff, cross, sems, cot_sems,
 ):
     field_hbm = field_hbm.reshape(TILES, ROWS, 128)
     cot_ref = cot_cells.reshape(TILES, ROWS, 128)
-    cot_made = copies(cot_hbm, cot_cells, cot_sems)
+    half_hbm = half_hbm.reshape(HALF, ROWS, 128)
+    cot_made = copies(cot_hbm, cot_cells, cot_sems, tiles=range(HALF, TILES))
     made = []
     for n in range(STEPS):
         some = pl.ds(PER * n, PER)
         made.append(start_all((field_hbm.at[some], field_ref.at[some], sems.at[1, n])))
-        made[n] += cot_made[PER * n * GROUPS : PER * (n + 1) * GROUPS]
-        for copy in made[n][1:]:
-            copy.start()
+        if PER * n < HALF:
+            made[n] += start_all((half_hbm.at[some], cot_ref.at[some], cot_sems.at[PER * n, 0]))
+        else:
+            at = (PER * n - HALF) * GROUPS
+            made[n] += cot_made[at : at + PER * GROUPS]
+            for copy in made[n][1:]:
+                copy.start()
     bypass_matrix(bypass_ref, channel_ref, same_ref, ((1,), (1,)), left)
     unpack_chunks(recv_ref, stage, left)
     coeff[...] = jnp.zeros_like(coeff)
@@ -474,6 +492,12 @@
     weight = call(
         weights_kernel, shape((C, SPEC, 128), BF16), [VMEM], [], out_specs=VMEM,
     )(weight_t)
+    some = shape((HALF, GROUPS, CX, 4, CY, 128), BF16)
+    half = call(
+        half_kernel, some, [HBM],
+        [pltpu.VMEM(some.shape, BF16), sems, pltpu.SemaphoreType.DMA], out_specs=HBM, limit=60,
+    )(cot_t)
+    weight, half = lax.optimization_barrier((weight, half))
     send, own = call(
         mix_kernel, (chunks, shape((3 * PACK, 128), BF16)), [VMEM] * 4,
         [pltpu.VMEM((SPEC, 128), F32)], out_specs=(VMEM,) * 2, limit=12,
@@ -483,11 +507,11 @@
     held = pltpu.VMEM(rows.shape, BF16)
     back = pltpu.VMEM((NQ, NP), BF16)
     send, up = call(
-        point_kernel, (chunks, rows), [VMEM, HBM, HBM] + [VMEM] * 5,
+        point_kernel, (chunks, rows), [VMEM] + [HBM] * 3 + [VMEM] * 5,
         [held, pltpu.VMEM(cells.shape, BF16), held, stage, left, pltpu.VMEM((ROWS, 256), F32),
          pltpu.VMEM((BLOCK, BLOCK), F32), dma(2, STEPS), sems],
         out_specs=(VMEM, HBM), limit=51,
-    )(recv, field_rows, cot_t, bypass_weight, table["channel"], table["same"],
+    )(recv, field_rows, half, cot_t, bypass_weight, table["channel"], table["same"],
       table["zt_back"], table["zt_ahead"])
     recv = exchange(send)
     specs = around(own)

time: 119 us -> 122 us (1.025)
  Pallas kernels: 38.3 us -> 41.6 us
  waiting for transfers between devices: 19.2 us -> 16 us
  blocking collectives: 17.8 us -> 20 us
    all_to_all x3, waiting for transfers between devices: 7.7 us -> 4.47 us  [exchange(): return lax.all_to_all(value, ('gx', 'gy'), 0, 0, tiled=True)]
    pallas_call x1 -> x2, Pallas kernels: 10.7 us -> 14 us  [the longest x1 10.8 us: body(): call(point_kernel, (chunks, rows), [VMEM] + [HBM] * 3 + [VMEM] * 5, [held...]
    all_to_all x1, blocking collectives: 17.8 us -> 20 us  [exchange(): return lax.all_to_all(value, ('gx', 'gy'), 0, 0, tiled=True)]
  transfers between devices with their start and end apart: 12 -> 12, of which waited for: 8 -> 8; matrix products, arithmetic and copies ran while one was open for 0% -> 0% of each run, Pallas kernels for 16% -> 18%
where the time goes in v6:
time: 122 us; the launch traced here: 119 us
  Pallas kernels  41.6 us (34%)
  starting transfers between devices  35.5 us (29%)
  blocking collectives  20 us (16%)
  waiting for transfers between devices  16 us (13%)
  local copies, waits for them, and re-layouts  4.78 us (4%)
    all_to_all x3, starting transfers between devices, exchange(): return lax.all_to_all(value, ('gx', 'gy'), 0, 0, tiled=True)  28.1 us
    all_to_all x1, blocking collectives, exchange(): return lax.all_to_all(value, ('gx', 'gy'), 0, 0, tiled=True)  20 us
    ppermute x9, waiting for transfers between devices, around(): lax.ppermute(value, 'dp', [(i, (i + k) % 4) for i in range(4)])  11.5 us
    pallas_call x1, Pallas kernels, body(): call(point_kernel, (chunks, rows), [VMEM] + [HBM] * 3 + [VMEM] * 5, [held...  10.8 us
    pallas_call x1, Pallas kernels, body(): pl.pallas_call(outer_kernel, grid=(C // PAIR,), out_shape=shape((C, C, Q3...  8.13 us
    ppermute x9, starting transfers between devices, around(): lax.ppermute(value, 'dp', [(i, (i + k) % 4) for i in range(4)])  7.34 us
    pallas_call x1, Pallas kernels, body(): call(final_kernel, shape((CX, C, CY, NP), BF16), [VMEM, HBM, VMEM, VMEM,...  7.24 us
    pallas_call x1, Pallas kernels, body(): call(analyze_kernel, (chunks, cells), [HBM, HBM], [pltpu.VMEM(cells.shape...  5.09 us
  transfers between devices with their start and end apart: 12, of which 8 were waited for; matrix products, arithmetic and copies ran while one was open for 0% of the time, Pallas kernels for 18%

profile of v6, /device:TPU:1, one launch (start us, length us, event | category | flops | bytes accessed | tf_op | source)
XLA Modules:
  0.0 119.3 jit_solution(5430540464466479394)
XLA Ops:
  0.6 5.1 %shard_map.121 = (bf16[64,16,128]{2,1,0:T(8,128)(2,1)}, bf16[16,5,16,4,2,128]{5,4,3,2,1,0:T(2,128)(2,1)}) custom-call(bf16[16,20,2,2048]{3,2,1,0:T(2,128)(2,1)} %bitcast.15, bf16[2048,256]{1,0:T(8,128)(2,1)} %constant.12.clone.zt_hbm.ahead_ref), custom_call_target="tpu_custom_call" | custom-call | tf_op jit(solution)/shard_map/pallas_call | solution.py:485
  5.7 13.0 %all-to-all-start = ((bf16[64,16,128]{2,1,0:T(8,128)(2,1)}), bf16[64,16,128]{2,1,0:T(8,128)(2,1)S(1)}, u32[]{:S(2)}, u32[]{:S(2)}) async-start(bf16[64,16,128]{2,1,0:T(8,128)(2,1)} %get-tuple-element.20), calls=%async_computation | async-start | bytes 524288 | tf_op jit(solution)/shard_map/all_to_all | solution.py:483
  18.7 3.2 %shard_map.123.half_hbm = bf16[8,5,16,4,2,128]{5,4,3,2,1,0:T(2,128)(2,1)} custom-call(bf16[16,20,2,2048]{3,2,1,0:T(2,128)(2,1)} %bitcast.13), custom_call_target="tpu_custom_call" | custom-call | tf_op jit(solution)/shard_map/pallas_call | solution.py:496
  21.9 0.0 copy-start
  22.0 3.1 %copy-done = bf16[24,24,20,20,3]{1,0,4,3,2:T(8,128)(2,1)S(1)} copy-done((bf16[24,24,20,20,3]{1,0,4,3,2:T(8,128)(2,1)S(1)}, bf16[24,24,20,20,3]{1,0,4,3,2:T(8,128)(2,1)}, u32[]{:S(2)}) %copy-start) | copy-done | bytes 1382424
  25.0 0.0 copy-start.4
  25.0 3.5 %shard_map.122.weight_ref = bf16[20,360,128]{2,1,0:T(8,128)(2,1)S(1)} custom-call(bf16[20,20,3,24,24]{4,3,2,1,0:T(8,128)(2,1)S(1)} %bitcast.11), custom_call_target="tpu_custom_call" | custom-call | tf_op jit(solution)/shard_map/pallas_call | solution.py:492
  28.5 0.0 copy-start.1
  28.5 2.2 %all-to-all-done.recv_ref = bf16[64,16,128]{2,1,0:T(8,128)(2,1)S(1)} async-done(((bf16[64,16,128]{2,1,0:T(8,128)(2,1)}), bf16[64,16,128]{2,1,0:T(8,128)(2,1)S(1)}, u32[]{:S(2)}, u32[]{:S(2)}) %all-to-all-start) | async-done | bytes 262176 | tf_op jit(solution)/shard_map/all_to_all | solution.py:483
  30.7 0.0 copy-done.4
  30.7 0.0 copy-start.5
  30.7 0.9 copy-done.5
  31.7 0.0 copy-start.2
  31.7 0.0 copy-start.7
  31.7 0.0 copy-start.8
  31.7 0.0 copy-start.12
  31.7 1.5 %shard_map.124 = (bf16[64,16,128]{2,1,0:T(8,128)(2,1)S(1)}, bf16[288,128]{1,0:T(8,128)(2,1)S(1)}) custom-call(bf16[64,16,128]{2,1,0:T(8,128)(2,1)S(1)} %all-to-all-done.recv_ref, bf16[20,360,128]{2,1,0:T(8,128)(2,1)S(1)} %shard_map.122.weight_ref, bf16[512,256]{1,0:T(8,128)(2,1)S(1)} %copy-done.5, bf16[360,512]{1,0:T(8,128)(2,1)S(1)} %copy-done.4), custom_call_target="tpu_custom_call" | custom-call | tf_op jit(solution)/shard_map/pallas_call | solution.py:501
  33.2 0.0 copy-start.10
  33.2 20.0 %all_to_all.20.recv_ref = bf16[64,16,128]{2,1,0:T(8,128)(2,1)S(1)} all-to-all(bf16[64,16,128]{2,1,0:T(8,128)(2,1)S(1)} %get-tuple-element.22), channel_id=1, replica_groups=mesh['dp'=4,'gx'=4,'gy'=16] {'gx','gy'}, dimensions={0} | all-to-all | bytes 524288 | tf_op jit(solution)/shard_map/all_to_all | solution.py:483
  53.2 0.0 copy-done.10
  53.2 0.0 copy-done.1
  53.2 0.0 copy-done.2
  53.2 0.0 copy-done.7
  53.2 0.0 copy-done.8
  53.3 0.0 copy-done.12
  53.3 0.0 copy-start.6
  53.3 10.8 %shard_map.125 = (bf16[64,16,128]{2,1,0:T(8,128)(2,1)S(1)}, bf16[16,640,128]{2,1,0:T(8,128)(2,1)}) custom-call(bf16[64,16,128]{2,1,0:T(8,128)(2,1)S(1)} %all_to_all.20.recv_ref, bf16[16,5,16,4,2,128]{5,4,3,2,1,0:T(2,128)(2,1)} %get-tuple-element.23.field_hbm, bf16[8,5,16,4,2,128]{5,4,3,2,1,0:T(2,128)(2,1)} %shard_map.123.half_hbm, ...), custom_call_target="tpu_custom_call" | custom-call | tf_op jit(solution)/shard_map/pallas_call | solution.py:509
  64.0 0.0 copy-start.9
  64.1 0.7 copy-done.9
  64.8 0.0 copy-start.11
  64.8 6.2 %all-to-all-start.2 = ((bf16[64,16,128]{2,1,0:T(8,128)(2,1)}), bf16[64,16,128]{2,1,0:T(8,128)(2,1)S(1)}, u32[]{:S(2)}, u32[]{:S(2)}) async-start(bf16[64,16,128]{2,1,0:T(8,128)(2,1)} %copy-done.9), calls=%async_computation.2 | async-start | bytes 524288 | tf_op jit(solution)/shard_map/all_to_all | solution.py:483
  70.9 2.8 %collective-permute-start.2 = (bf16[288,128]{1,0:T(8,128)(2,1)}, bf16[288,128]{1,0:T(8,128)(2,1)S(1)}, u32[]{:S(2)}, u32[]{:S(2)}) collective-permute-start(bf16[288,128]{1,0:T(8,128)(2,1)} %copy-done.10), channel_id=1, source_target_pairs={{0,192},{64,0},{128,64},{192,128},{1,193},{65,1},{129,65},{193,129... | collective-permute-start | bytes 221192 | tf_op jit(solution)/shard_map/ppermute | solution.py:465
  73.7 0.3 collective-permute-start.1
  74.1 0.7 collective-permute-start
  74.8 0.7 collective-permute-done.2.refs_3_
  75.5 3.5 %collective-permute-done.1.refs_2_ = bf16[288,128]{1,0:T(8,128)(2,1)S(1)} collective-permute-done((bf16[288,128]{1,0:T(8,128)(2,1)}, bf16[288,128]{1,0:T(8,128)(2,1)S(1)}, u32[]{:S(2)}, u32[]{:S(2)}) %collective-permute-start.1) | collective-permute-done | bytes 73760 | tf_op jit(solution)/shard_map/ppermute | solution.py:465
  79.0 1.7 %collective-permute-done.refs_1_ = bf16[288,128]{1,0:T(8,128)(2,1)S(1)} collective-permute-done((bf16[288,128]{1,0:T(8,128)(2,1)}, bf16[288,128]{1,0:T(8,128)(2,1)S(1)}, u32[]{:S(2)}, u32[]{:S(2)}) %collective-permute-start) | collective-permute-done | bytes 73760 | tf_op jit(solution)/shard_map/ppermute | solution.py:465
  80.7 2.2 %all-to-all-done.2.recv_ref = bf16[64,16,128]{2,1,0:T(8,128)(2,1)S(1)} async-done(((bf16[64,16,128]{2,1,0:T(8,128)(2,1)}), bf16[64,16,128]{2,1,0:T(8,128)(2,1)S(1)}, u32[]{:S(2)}, u32[]{:S(2)}) %all-to-all-start.2) | async-done | bytes 262176 | tf_op jit(solution)/shard_map/all_to_all | solution.py:483
  82.9 0.0 copy-done.6
  82.9 2.1 %shard_map.126 = (bf16[64,16,128]{2,1,0:T(8,128)(2,1)}, bf16[288,128]{1,0:T(8,128)(2,1)S(1)}) custom-call(bf16[64,16,128]{2,1,0:T(8,128)(2,1)S(1)} %all-to-all-done.2.recv_ref, bf16[20,360,128]{2,1,0:T(8,128)(2,1)S(1)} %shard_map.122.weight_ref, bf16[512,256]{1,0:T(8,128)(2,1)S(1)} %copy-done.6, bf16[360,512]{1,0:T(8,128)(2,1)S(1)} %copy-done.4), custom_call_target="tpu_custom_call" | custom-call | tf_op jit(solution)/shard_map/pallas_call | solution.py:519
  85.0 9.0 %all-to-all-start.3 = ((bf16[64,16,128]{2,1,0:T(8,128)(2,1)}), bf16[64,16,128]{2,1,0:T(8,128)(2,1)S(1)}, u32[]{:S(2)}, u32[]{:S(2)}) async-start(bf16[64,16,128]{2,1,0:T(8,128)(2,1)} %get-tuple-element.28), calls=%async_computation.3 | async-start | bytes 524288 | tf_op jit(solution)/shard_map/all_to_all | solution.py:483
  94.0 0.4 collective-permute-start.5
  94.4 0.5 collective-permute-start.4
  94.9 0.8 collective-permute-start.3
  95.6 2.0 %collective-permute-done.5.refs_7_ = bf16[288,128]{1,0:T(8,128)(2,1)S(1)} collective-permute-done((bf16[288,128]{1,0:T(8,128)(2,1)S(1)}, bf16[288,128]{1,0:T(8,128)(2,1)S(1)}, u32[]{:S(2)}, u32[]{:S(2)}) %collective-permute-start.5) | collective-permute-done | bytes 73760 | tf_op jit(solution)/shard_map/ppermute | solution.py:465
  97.6 1.5 %collective-permute-done.4.refs_6_ = bf16[288,128]{1,0:T(8,128)(2,1)S(1)} collective-permute-done((bf16[288,128]{1,0:T(8,128)(2,1)S(1)}, bf16[288,128]{1,0:T(8,128)(2,1)S(1)}, u32[]{:S(2)}, u32[]{:S(2)}) %collective-permute-start.4) | collective-permute-done | bytes 73760 | tf_op jit(solution)/shard_map/ppermute | solution.py:465
  99.1 2.2 %collective-permute-done.3.refs_5_ = bf16[288,128]{1,0:T(8,128)(2,1)S(1)} collective-permute-done((bf16[288,128]{1,0:T(8,128)(2,1)S(1)}, bf16[288,128]{1,0:T(8,128)(2,1)S(1)}, u32[]{:S(2)}, u32[]{:S(2)}) %collective-permute-start.3) | collective-permute-done | bytes 73760 | tf_op jit(solution)/shard_map/ppermute | solution.py:465
  101.3 0.0 copy-done.11
  101.3 8.1 %shard_map.127 = f32[20,20,3,24,24]{4,3,2,1,0:T(8,128)} custom-call(bf16[288,128]{1,0:T(8,128)(2,1)S(1)} %copy-done.11, bf16[288,128]{1,0:T(8,128)(2,1)S(1)} %collective-permute-done.refs_1_, bf16[288,128]{1,0:T(8,128)(2,1)S(1)} %collective-permute-done.1.refs_2_, bf16[288,128]{1,0:T(8,128)(2,1)S(1)} %collective-permute-done.2.refs_3_, ...), custom_call_target="tpu_custom_call" | custom-call | flops 1000000000 | bytes 100000000 | tf_op jit(solution)/shard_map/pallas_call | solution.py:525
  109.4 0.0 all-to-all-done.3.recv_ref
  109.4 0.0 copy-start.3
  109.4 0.1 shard_map.129
  109.5 0.4 collective-permute-start.8
  109.9 1.1 collective-permute-start.7
  111.0 0.4 collective-permute-start.6
  111.4 0.0 copy-done.3
  111.4 7.2 %shard_map.128 = bf16[16,20,2,2048]{3,2,1,0:T(2,128)(2,1)} custom-call(bf16[64,16,128]{2,1,0:T(8,128)(2,1)} %copy-done.3, bf16[16,640,128]{2,1,0:T(8,128)(2,1)} %get-tuple-element.35.up_hbm, bf16[20,20]{1,0:T(8,128)(2,1)} %bypass_ref.3, bf16[320,20]{1,0:T(8,128)(2,1)} %constant.16.clone.channel_ref, bf16[320,384]{1,0:T(8,128)(2,1)} %constant.17.clone.same_ref, ...), custom_call_target="tpu_custom_call" | custom-call | tf_op jit(solution)/shard_map/pallas_call | solution.py:543
  118.6 0.0 collective-permute-done.8
  118.6 0.0 collective-permute-done.7
  118.6 0.0 collective-permute-done.6
  118.7 0.6 fusion
Async XLA Ops:
  5.7 25.0 %all-to-all-start = ((bf16[64,16,128]{2,1,0:T(8,128)(2,1)}), bf16[64,16,128]{2,1,0:T(8,128)(2,1)S(1)}, u32[]{:S(2)}, u32[]{:S(2)}) async-start(bf16[64,16,128]{2,1,0:T(8,128)(2,1)} %get-tuple-element.20), calls=%async_computation | async-start | bytes 524288 | tf_op jit(solution)/shard_map/all_to_all | solution.py:483
  21.9 3.1 %copy-start = (bf16[24,24,20,20,3]{1,0,4,3,2:T(8,128)(2,1)S(1)}, bf16[24,24,20,20,3]{1,0,4,3,2:T(8,128)(2,1)}, u32[]{:S(2)}) copy-start(bf16[24,24,20,20,3]{1,0,4,3,2:T(8,128)(2,1)} %param.12) | copy-start | bytes 4147204
  25.0 5.7 %copy-start.4 = (bf16[360,512]{1,0:T(8,128)(2,1)S(1)}, bf16[360,512]{1,0:T(8,128)(2,1)}, u32[]{:S(2)}) copy-start(bf16[360,512]{1,0:T(8,128)(2,1)} %constant.15.clone.ya_ref) | copy-start | bytes 1105924
  28.5 24.7 %copy-start.1 = (bf16[2048,256]{1,0:T(8,128)(2,1)S(1)}, bf16[2048,256]{1,0:T(8,128)(2,1)}, u32[]{:S(2)}) copy-start(bf16[2048,256]{1,0:T(8,128)(2,1)} %constant.12.clone.zt_hbm.ahead_ref) | copy-start | bytes 3145732
  30.7 1.0 copy-start.5
  31.7 21.6 %copy-start.2 = (bf16[192,2048]{1,0:T(8,128)(2,1)S(1)}, bf16[192,2048]{1,0:T(8,128)(2,1)}, u32[]{:S(2)}) copy-start(bf16[192,2048]{1,0:T(8,128)(2,1)} %constant.13.clone.back_ref.back_hbm) | copy-start | bytes 2359300
  31.7 21.6 %copy-start.7 = (bf16[320,384]{1,0:T(8,128)(2,1)S(1)}, bf16[320,384]{1,0:T(8,128)(2,1)}, u32[]{:S(2)}) copy-start(bf16[320,384]{1,0:T(8,128)(2,1)} %constant.17.clone.same_ref) | copy-start | bytes 737284
  31.7 21.6 %copy-start.8 = (bf16[320,20]{1,0:T(8,128)(2,1)S(1)}, bf16[320,20]{1,0:T(8,128)(2,1)}, u32[]{:S(2)}) copy-start(bf16[320,20]{1,0:T(8,128)(2,1)} %constant.16.clone.channel_ref) | copy-start | bytes 38404
  31.7 21.6 %copy-start.12 = (bf16[20,20]{1,0:T(8,128)(2,1)S(1)}, bf16[20,20]{1,0:T(8,128)(2,1)}, u32[]{:S(2)}) copy-start(bf16[20,20]{1,0:T(8,128)(2,1)} %bypass_ref.3) | copy-start | bytes 2404
  33.2 20.0 %copy-start.10 = (bf16[288,128]{1,0:T(8,128)(2,1)}, bf16[288,128]{1,0:T(8,128)(2,1)S(1)}, u32[]{:S(2)}) copy-start(bf16[288,128]{1,0:T(8,128)(2,1)S(1)} %get-tuple-element.29.refs_0_) | copy-start | bytes 221188
  53.3 29.7 %copy-start.6 = (bf16[512,256]{1,0:T(8,128)(2,1)S(1)}, bf16[512,256]{1,0:T(8,128)(2,1)}, u32[]{:S(2)}) copy-start(bf16[512,256]{1,0:T(8,128)(2,1)} %constant.14.clone.xa_ref) | copy-start | bytes 786436
  64.0 0.7 copy-start.9
  64.8 36.5 %copy-start.11 = (bf16[288,128]{1,0:T(8,128)(2,1)S(1)}, bf16[288,128]{1,0:T(8,128)(2,1)}, u32[]{:S(2)}) copy-start(bf16[288,128]{1,0:T(8,128)(2,1)} %copy-done.10) | copy-start | bytes 221188
  64.8 18.2 %all-to-all-start.2 = ((bf16[64,16,128]{2,1,0:T(8,128)(2,1)}), bf16[64,16,128]{2,1,0:T(8,128)(2,1)S(1)}, u32[]{:S(2)}, u32[]{:S(2)}) async-start(bf16[64,16,128]{2,1,0:T(8,128)(2,1)} %copy-done.9), calls=%async_computation.2 | async-start | bytes 524288 | tf_op jit(solution)/shard_map/all_to_all | solution.py:483
  70.9 4.5 %collective-permute-start.2 = (bf16[288,128]{1,0:T(8,128)(2,1)}, bf16[288,128]{1,0:T(8,128)(2,1)S(1)}, u32[]{:S(2)}, u32[]{:S(2)}) collective-permute-start(bf16[288,128]{1,0:T(8,128)(2,1)} %copy-done.10), channel_id=1, source_target_pairs={{0,192},{64,0},{128,64},{192,128},{1,193},{65,1},{129,65},{193,129... | collective-permute-start | bytes 221192 | tf_op jit(solution)/shard_map/ppermute | solution.py:465
  73.7 5.2 %collective-permute-start.1 = (bf16[288,128]{1,0:T(8,128)(2,1)}, bf16[288,128]{1,0:T(8,128)(2,1)S(1)}, u32[]{:S(2)}, u32[]{:S(2)}) collective-permute-start(bf16[288,128]{1,0:T(8,128)(2,1)} %copy-done.10), channel_id=1, source_target_pairs={{0,128},{64,192},{128,0},{192,64},{1,129},{65,193},{129,1},{193,65... | collective-permute-start | bytes 221192 | tf_op jit(solution)/shard_map/ppermute | solution.py:465
  74.1 6.6 %collective-permute-start = (bf16[288,128]{1,0:T(8,128)(2,1)}, bf16[288,128]{1,0:T(8,128)(2,1)S(1)}, u32[]{:S(2)}, u32[]{:S(2)}) collective-permute-start(bf16[288,128]{1,0:T(8,128)(2,1)} %copy-done.10), channel_id=1, source_target_pairs={{0,64},{64,128},{128,192},{192,0},{1,65},{65,129},{129,193},{193,1... | collective-permute-start | bytes 221192 | tf_op jit(solution)/shard_map/ppermute | solution.py:465
  85.0 24.4 %all-to-all-start.3 = ((bf16[64,16,128]{2,1,0:T(8,128)(2,1)}), bf16[64,16,128]{2,1,0:T(8,128)(2,1)S(1)}, u32[]{:S(2)}, u32[]{:S(2)}) async-start(bf16[64,16,128]{2,1,0:T(8,128)(2,1)} %get-tuple-element.28), calls=%async_computation.3 | async-start | bytes 524288 | tf_op jit(solution)/shard_map/all_to_all | solution.py:483
  94.0 3.6 %collective-permute-start.5 = (bf16[288,128]{1,0:T(8,128)(2,1)S(1)}, bf16[288,128]{1,0:T(8,128)(2,1)S(1)}, u32[]{:S(2)}, u32[]{:S(2)}) collective-permute-start(bf16[288,128]{1,0:T(8,128)(2,1)S(1)} %get-tuple-element.33.refs_4_), channel_id=1, source_target_pairs={{0,192},{64,0},{128,64},{192,128},{1,193},{65,1},{129,65},{193,129... | collective-permute-start | bytes 221192 | tf_op jit(solution)/shard_map/ppermute | solution.py:465
  94.4 4.7 %collective-permute-start.4 = (bf16[288,128]{1,0:T(8,128)(2,1)S(1)}, bf16[288,128]{1,0:T(8,128)(2,1)S(1)}, u32[]{:S(2)}, u32[]{:S(2)}) collective-permute-start(bf16[288,128]{1,0:T(8,128)(2,1)S(1)} %get-tuple-element.33.refs_4_), channel_id=1, source_target_pairs={{0,128},{64,192},{128,0},{192,64},{1,129},{65,193},{129,1},{193,65... | collective-permute-start | bytes 221192 | tf_op jit(solution)/shard_map/ppermute | solution.py:465
  94.9 6.4 %collective-permute-start.3 = (bf16[288,128]{1,0:T(8,128)(2,1)S(1)}, bf16[288,128]{1,0:T(8,128)(2,1)S(1)}, u32[]{:S(2)}, u32[]{:S(2)}) collective-permute-start(bf16[288,128]{1,0:T(8,128)(2,1)S(1)} %get-tuple-element.33.refs_4_), channel_id=1, source_target_pairs={{0,64},{64,128},{128,192},{192,0},{1,65},{65,129},{129,193},{193,1... | collective-permute-start | bytes 221192 | tf_op jit(solution)/shard_map/ppermute | solution.py:465
  109.4 2.0 %copy-start.3 = (bf16[64,16,128]{2,1,0:T(8,128)(2,1)}, bf16[64,16,128]{2,1,0:T(8,128)(2,1)S(1)}, u32[]{:S(2)}) copy-start(bf16[64,16,128]{2,1,0:T(8,128)(2,1)S(1)} %all-to-all-done.3.recv_ref) | copy-start | bytes 786436
  109.5 9.1 %collective-permute-start.8 = (f32[24,128]{1,0:T(8,128)S(1)}, f32[24,128]{1,0:T(8,128)S(1)}, u32[]{:S(2)}, u32[]{:S(2)}) collective-permute-start(f32[24,128]{1,0:T(8,128)S(1)} %shard_map.129), channel_id=1, source_target_pairs={{0,192},{64,0},{128,64},{192,128},{1,193},{65,1},{129,65},{193,129... | collective-permute-start | bytes 36872 | tf_op jit(solution)/shard_map/ppermute | solution.py:465
  109.9 8.7 %collective-permute-start.7 = (f32[24,128]{1,0:T(8,128)S(1)}, f32[24,128]{1,0:T(8,128)S(1)}, u32[]{:S(2)}, u32[]{:S(2)}) collective-permute-start(f32[24,128]{1,0:T(8,128)S(1)} %shard_map.129), channel_id=1, source_target_pairs={{0,64},{64,128},{128,192},{192,0},{1,65},{65,129},{129,193},{193,1... | collective-permute-start | bytes 36872 | tf_op jit(solution)/shard_map/ppermute | solution.py:465
  111.0 7.7 %collective-permute-start.6 = (f32[24,128]{1,0:T(8,128)S(1)}, f32[24,128]{1,0:T(8,128)S(1)}, u32[]{:S(2)}, u32[]{:S(2)}) collective-permute-start(f32[24,128]{1,0:T(8,128)S(1)} %shard_map.129), channel_id=1, source_target_pairs={{0,128},{64,192},{128,0},{192,64},{1,129},{65,193},{129,1},{193,65... | collective-permute-start | bytes 36872 | tf_op jit(solution)/shard_map/ppermute | solution.py:465

commit v7 on v5

--- a/solution.py
+++ b/solution.py
@@ -404,7 +404,7 @@
                 tiles[4 * j + c, s, b] = turned[32 * c : 32 * c + KX]
 
 
-PAIR = 4
+PAIR = 5
 
 
 def outer_kernel(*refs):

time: 119 us -> 119 us (level)
  no operation moved by 1% of the time
where the time goes in v7:
time: 119 us; the launch traced here: 117 us
  Pallas kernels  38.2 us (32%)
  starting transfers between devices  35.2 us (30%)
  waiting for transfers between devices  19.2 us (16%)
  blocking collectives  17.8 us (15%)
  local copies, waits for them, and re-layouts  4.78 us (4%)
    all_to_all x3, starting transfers between devices, exchange(): return lax.all_to_all(value, ('gx', 'gy'), 0, 0, tiled=True)  27.9 us
    all_to_all x1, blocking collectives, exchange(): return lax.all_to_all(value, ('gx', 'gy'), 0, 0, tiled=True)  17.8 us
    ppermute x9, waiting for transfers between devices, around(): lax.ppermute(value, 'dp', [(i, (i + k) % 4) for i in range(4)])  11.5 us
    pallas_call x1, Pallas kernels, body(): call(point_kernel, (chunks, rows), [VMEM, HBM, HBM] + [VMEM] * 5, [held,...  10.7 us
    pallas_call x1, Pallas kernels, body(): pl.pallas_call(outer_kernel, grid=(C // PAIR,), out_shape=shape((C, C, Q3...  8.01 us
    all_to_all x3, waiting for transfers between devices, exchange(): return lax.all_to_all(value, ('gx', 'gy'), 0, 0, tiled=True)  7.7 us
    ppermute x9, starting transfers between devices, around(): lax.ppermute(value, 'dp', [(i, (i + k) % 4) for i in range(4)])  7.33 us
    pallas_call x1, Pallas kernels, body(): call(final_kernel, shape((CX, C, CY, NP), BF16), [VMEM, HBM, VMEM, VMEM,...  7.24 us
  transfers between devices with their start and end apart: 12, of which 8 were waited for; matrix products, arithmetic and copies ran while one was open for 0% of the time, Pallas kernels for 16%

profile of v7, /device:TPU:1, one launch (start us, length us, event | category | flops | bytes accessed | tf_op | source)
XLA Modules:
  0.0 116.7 jit_solution(3959167472648868872)
XLA Ops:
  0.6 5.1 %shard_map.121 = (bf16[64,16,128]{2,1,0:T(8,128)(2,1)}, bf16[16,5,16,4,2,128]{5,4,3,2,1,0:T(2,128)(2,1)}) custom-call(bf16[16,20,2,2048]{3,2,1,0:T(2,128)(2,1)} %bitcast.13, bf16[2048,256]{1,0:T(8,128)(2,1)} %constant.12.clone.zt_hbm.ahead_ref), custom_call_target="tpu_custom_call" | custom-call | tf_op jit(solution)/shard_map/pallas_call | solution.py:467
  5.7 13.0 %all-to-all-start = ((bf16[64,16,128]{2,1,0:T(8,128)(2,1)}), bf16[64,16,128]{2,1,0:T(8,128)(2,1)S(1)}, u32[]{:S(2)}, u32[]{:S(2)}) async-start(bf16[64,16,128]{2,1,0:T(8,128)(2,1)} %get-tuple-element.18), calls=%async_computation | async-start | bytes 524288 | tf_op jit(solution)/shard_map/all_to_all | solution.py:465
  18.7 0.0 copy-start
  18.7 3.1 %copy-done = bf16[24,24,20,20,3]{1,0,4,3,2:T(8,128)(2,1)S(1)} copy-done((bf16[24,24,20,20,3]{1,0,4,3,2:T(8,128)(2,1)S(1)}, bf16[24,24,20,20,3]{1,0,4,3,2:T(8,128)(2,1)}, u32[]{:S(2)}) %copy-start) | copy-done | bytes 1382424
  21.8 0.0 copy-start.4
  21.8 3.5 %shard_map.122.weight_ref = bf16[20,360,128]{2,1,0:T(8,128)(2,1)S(1)} custom-call(bf16[20,20,3,24,24]{4,3,2,1,0:T(8,128)(2,1)S(1)} %bitcast.11), custom_call_target="tpu_custom_call" | custom-call | tf_op jit(solution)/shard_map/pallas_call | solution.py:474
  25.3 0.0 copy-start.1
  25.3 5.4 %all-to-all-done.recv_ref = bf16[64,16,128]{2,1,0:T(8,128)(2,1)S(1)} async-done(((bf16[64,16,128]{2,1,0:T(8,128)(2,1)}), bf16[64,16,128]{2,1,0:T(8,128)(2,1)S(1)}, u32[]{:S(2)}, u32[]{:S(2)}) %all-to-all-start) | async-done | bytes 262176 | tf_op jit(solution)/shard_map/all_to_all | solution.py:465
  30.7 0.0 copy-done.4
  30.7 0.0 copy-start.5
  30.7 0.9 copy-done.5
  31.7 0.0 copy-start.2
  31.7 0.0 copy-start.7
  31.7 0.0 copy-start.8
  31.7 0.0 copy-start.12
  31.7 1.5 %shard_map.123 = (bf16[64,16,128]{2,1,0:T(8,128)(2,1)S(1)}, bf16[288,128]{1,0:T(8,128)(2,1)S(1)}) custom-call(bf16[64,16,128]{2,1,0:T(8,128)(2,1)S(1)} %all-to-all-done.recv_ref, bf16[20,360,128]{2,1,0:T(8,128)(2,1)S(1)} %shard_map.122.weight_ref, bf16[512,256]{1,0:T(8,128)(2,1)S(1)} %copy-done.5, bf16[360,512]{1,0:T(8,128)(2,1)S(1)} %copy-done.4), custom_call_target="tpu_custom_call" | custom-call | tf_op jit(solution)/shard_map/pallas_call | solution.py:477
  33.2 0.0 copy-start.10
  33.2 17.8 %all_to_all.20.recv_ref = bf16[64,16,128]{2,1,0:T(8,128)(2,1)S(1)} all-to-all(bf16[64,16,128]{2,1,0:T(8,128)(2,1)S(1)} %get-tuple-element.19), channel_id=1, replica_groups=mesh['dp'=4,'gx'=4,'gy'=16] {'gx','gy'}, dimensions={0} | all-to-all | bytes 524288 | tf_op jit(solution)/shard_map/all_to_all | solution.py:465
  51.0 0.0 copy-done.10
  51.1 0.0 copy-done.1
  51.1 0.0 copy-done.2
  51.1 0.0 copy-done.7
  51.1 0.0 copy-done.8
  51.1 0.0 copy-done.12
  51.1 0.0 copy-start.6
  51.1 10.7 %shard_map.124 = (bf16[64,16,128]{2,1,0:T(8,128)(2,1)S(1)}, bf16[16,640,128]{2,1,0:T(8,128)(2,1)}) custom-call(bf16[64,16,128]{2,1,0:T(8,128)(2,1)S(1)} %all_to_all.20.recv_ref, bf16[16,5,16,4,2,128]{5,4,3,2,1,0:T(2,128)(2,1)} %get-tuple-element.20.field_hbm, bf16[16,20,2,2048]{3,2,1,0:T(2,128)(2,1)} %bitcast.14, bf16[20,20]{1,0:T(8,128)(2,1)S(1)} %copy-done.12, ...), custom_call_target="tpu_custom_call" | custom-call | tf_op jit(solution)/shard_map/pallas_call | solution.py:485
  61.8 0.0 copy-start.9
  61.9 0.7 copy-done.9
  62.6 0.0 copy-start.11
  62.6 6.2 %all-to-all-start.2 = ((bf16[64,16,128]{2,1,0:T(8,128)(2,1)}), bf16[64,16,128]{2,1,0:T(8,128)(2,1)S(1)}, u32[]{:S(2)}, u32[]{:S(2)}) async-start(bf16[64,16,128]{2,1,0:T(8,128)(2,1)} %copy-done.9), calls=%async_computation.2 | async-start | bytes 524288 | tf_op jit(solution)/shard_map/all_to_all | solution.py:465
  68.7 2.8 %collective-permute-start.2 = (bf16[288,128]{1,0:T(8,128)(2,1)}, bf16[288,128]{1,0:T(8,128)(2,1)S(1)}, u32[]{:S(2)}, u32[]{:S(2)}) collective-permute-start(bf16[288,128]{1,0:T(8,128)(2,1)} %copy-done.10), channel_id=1, source_target_pairs={{0,192},{64,0},{128,64},{192,128},{1,193},{65,1},{129,65},{193,129... | collective-permute-start | bytes 221192 | tf_op jit(solution)/shard_map/ppermute | solution.py:447
  71.5 0.4 collective-permute-start.1
  71.9 0.7 collective-permute-start
  72.6 0.7 collective-permute-done.2.refs_3_
  73.3 3.5 %collective-permute-done.1.refs_2_ = bf16[288,128]{1,0:T(8,128)(2,1)S(1)} collective-permute-done((bf16[288,128]{1,0:T(8,128)(2,1)}, bf16[288,128]{1,0:T(8,128)(2,1)S(1)}, u32[]{:S(2)}, u32[]{:S(2)}) %collective-permute-start.1) | collective-permute-done | bytes 73760 | tf_op jit(solution)/shard_map/ppermute | solution.py:447
  76.8 1.7 %collective-permute-done.refs_1_ = bf16[288,128]{1,0:T(8,128)(2,1)S(1)} collective-permute-done((bf16[288,128]{1,0:T(8,128)(2,1)}, bf16[288,128]{1,0:T(8,128)(2,1)S(1)}, u32[]{:S(2)}, u32[]{:S(2)}) %collective-permute-start) | collective-permute-done | bytes 73760 | tf_op jit(solution)/shard_map/ppermute | solution.py:447
  78.5 2.3 %all-to-all-done.2.recv_ref = bf16[64,16,128]{2,1,0:T(8,128)(2,1)S(1)} async-done(((bf16[64,16,128]{2,1,0:T(8,128)(2,1)}), bf16[64,16,128]{2,1,0:T(8,128)(2,1)S(1)}, u32[]{:S(2)}, u32[]{:S(2)}) %all-to-all-start.2) | async-done | bytes 262176 | tf_op jit(solution)/shard_map/all_to_all | solution.py:465
  80.7 0.0 copy-done.6
  80.7 2.1 %shard_map.125 = (bf16[64,16,128]{2,1,0:T(8,128)(2,1)}, bf16[288,128]{1,0:T(8,128)(2,1)S(1)}) custom-call(bf16[64,16,128]{2,1,0:T(8,128)(2,1)S(1)} %all-to-all-done.2.recv_ref, bf16[20,360,128]{2,1,0:T(8,128)(2,1)S(1)} %shard_map.122.weight_ref, bf16[512,256]{1,0:T(8,128)(2,1)S(1)} %copy-done.6, bf16[360,512]{1,0:T(8,128)(2,1)S(1)} %copy-done.4), custom_call_target="tpu_custom_call" | custom-call | tf_op jit(solution)/shard_map/pallas_call | solution.py:495
  82.8 8.7 %all-to-all-start.3 = ((bf16[64,16,128]{2,1,0:T(8,128)(2,1)}), bf16[64,16,128]{2,1,0:T(8,128)(2,1)S(1)}, u32[]{:S(2)}, u32[]{:S(2)}) async-start(bf16[64,16,128]{2,1,0:T(8,128)(2,1)} %get-tuple-element.24), calls=%async_computation.3 | async-start | bytes 524288 | tf_op jit(solution)/shard_map/all_to_all | solution.py:465
  91.6 0.4 collective-permute-start.5
  92.0 0.5 collective-permute-start.4
  92.4 0.8 collective-permute-start.3
  93.2 2.0 %collective-permute-done.5.refs_7_ = bf16[288,128]{1,0:T(8,128)(2,1)S(1)} collective-permute-done((bf16[288,128]{1,0:T(8,128)(2,1)S(1)}, bf16[288,128]{1,0:T(8,128)(2,1)S(1)}, u32[]{:S(2)}, u32[]{:S(2)}) %collective-permute-start.5) | collective-permute-done | bytes 73760 | tf_op jit(solution)/shard_map/ppermute | solution.py:447
  95.2 1.5 %collective-permute-done.4.refs_6_ = bf16[288,128]{1,0:T(8,128)(2,1)S(1)} collective-permute-done((bf16[288,128]{1,0:T(8,128)(2,1)S(1)}, bf16[288,128]{1,0:T(8,128)(2,1)S(1)}, u32[]{:S(2)}, u32[]{:S(2)}) %collective-permute-start.4) | collective-permute-done | bytes 73760 | tf_op jit(solution)/shard_map/ppermute | solution.py:447
  96.7 2.2 %collective-permute-done.3.refs_5_ = bf16[288,128]{1,0:T(8,128)(2,1)S(1)} collective-permute-done((bf16[288,128]{1,0:T(8,128)(2,1)S(1)}, bf16[288,128]{1,0:T(8,128)(2,1)S(1)}, u32[]{:S(2)}, u32[]{:S(2)}) %collective-permute-start.3) | collective-permute-done | bytes 73760 | tf_op jit(solution)/shard_map/ppermute | solution.py:447
  98.8 0.0 copy-done.11
  98.8 8.0 %shard_map.126 = f32[20,20,3,24,24]{4,3,2,1,0:T(8,128)} custom-call(bf16[288,128]{1,0:T(8,128)(2,1)S(1)} %copy-done.11, bf16[288,128]{1,0:T(8,128)(2,1)S(1)} %collective-permute-done.refs_1_, bf16[288,128]{1,0:T(8,128)(2,1)S(1)} %collective-permute-done.1.refs_2_, bf16[288,128]{1,0:T(8,128)(2,1)S(1)} %collective-permute-done.2.refs_3_, ...), custom_call_target="tpu_custom_call" | custom-call | flops 1000000000 | bytes 100000000 | tf_op jit(solution)/shard_map/pallas_call | solution.py:501
  106.9 0.0 all-to-all-done.3.recv_ref
  106.9 0.0 copy-start.3
  106.9 0.1 shard_map.128
  107.0 0.4 collective-permute-start.8
  107.4 1.1 collective-permute-start.7
  108.4 0.4 collective-permute-start.6
  108.8 0.0 copy-done.3
  108.8 7.2 %shard_map.127 = bf16[16,20,2,2048]{3,2,1,0:T(2,128)(2,1)} custom-call(bf16[64,16,128]{2,1,0:T(8,128)(2,1)} %copy-done.3, bf16[16,640,128]{2,1,0:T(8,128)(2,1)} %get-tuple-element.31.up_hbm, bf16[20,20]{1,0:T(8,128)(2,1)} %bypass_ref.3, bf16[320,20]{1,0:T(8,128)(2,1)} %constant.16.clone.channel_ref, bf16[320,384]{1,0:T(8,128)(2,1)} %constant.17.clone.same_ref, ...), custom_call_target="tpu_custom_call" | custom-call | tf_op jit(solution)/shard_map/pallas_call | solution.py:519
  116.1 0.0 collective-permute-done.8
  116.1 0.0 collective-permute-done.7
  116.1 0.0 collective-permute-done.6
  116.1 0.6 fusion
Async XLA Ops:
  5.7 25.0 %all-to-all-start = ((bf16[64,16,128]{2,1,0:T(8,128)(2,1)}), bf16[64,16,128]{2,1,0:T(8,128)(2,1)S(1)}, u32[]{:S(2)}, u32[]{:S(2)}) async-start(bf16[64,16,128]{2,1,0:T(8,128)(2,1)} %get-tuple-element.18), calls=%async_computation | async-start | bytes 524288 | tf_op jit(solution)/shard_map/all_to_all | solution.py:465
  18.7 3.1 %copy-start = (bf16[24,24,20,20,3]{1,0,4,3,2:T(8,128)(2,1)S(1)}, bf16[24,24,20,20,3]{1,0,4,3,2:T(8,128)(2,1)}, u32[]{:S(2)}) copy-start(bf16[24,24,20,20,3]{1,0,4,3,2:T(8,128)(2,1)} %param.12) | copy-start | bytes 4147204
  21.8 8.9 %copy-start.4 = (bf16[360,512]{1,0:T(8,128)(2,1)S(1)}, bf16[360,512]{1,0:T(8,128)(2,1)}, u32[]{:S(2)}) copy-start(bf16[360,512]{1,0:T(8,128)(2,1)} %constant.15.clone.ya_ref) | copy-start | bytes 1105924
  25.3 25.8 %copy-start.1 = (bf16[2048,256]{1,0:T(8,128)(2,1)S(1)}, bf16[2048,256]{1,0:T(8,128)(2,1)}, u32[]{:S(2)}) copy-start(bf16[2048,256]{1,0:T(8,128)(2,1)} %constant.12.clone.zt_hbm.ahead_ref) | copy-start | bytes 3145732
  30.7 1.0 copy-start.5
  31.7 19.4 %copy-start.2 = (bf16[192,2048]{1,0:T(8,128)(2,1)S(1)}, bf16[192,2048]{1,0:T(8,128)(2,1)}, u32[]{:S(2)}) copy-start(bf16[192,2048]{1,0:T(8,128)(2,1)} %constant.13.clone.back_ref.back_hbm) | copy-start | bytes 2359300
  31.7 19.4 %copy-start.7 = (bf16[320,384]{1,0:T(8,128)(2,1)S(1)}, bf16[320,384]{1,0:T(8,128)(2,1)}, u32[]{:S(2)}) copy-start(bf16[320,384]{1,0:T(8,128)(2,1)} %constant.17.clone.same_ref) | copy-start | bytes 737284
  31.7 19.4 %copy-start.8 = (bf16[320,20]{1,0:T(8,128)(2,1)S(1)}, bf16[320,20]{1,0:T(8,128)(2,1)}, u32[]{:S(2)}) copy-start(bf16[320,20]{1,0:T(8,128)(2,1)} %constant.16.clone.channel_ref) | copy-start | bytes 38404
  31.7 19.4 %copy-start.12 = (bf16[20,20]{1,0:T(8,128)(2,1)S(1)}, bf16[20,20]{1,0:T(8,128)(2,1)}, u32[]{:S(2)}) copy-start(bf16[20,20]{1,0:T(8,128)(2,1)} %bypass_ref.3) | copy-start | bytes 2404
  33.2 17.8 %copy-start.10 = (bf16[288,128]{1,0:T(8,128)(2,1)}, bf16[288,128]{1,0:T(8,128)(2,1)S(1)}, u32[]{:S(2)}) copy-start(bf16[288,128]{1,0:T(8,128)(2,1)S(1)} %get-tuple-element.25.refs_0_) | copy-start | bytes 221188
  51.1 29.6 %copy-start.6 = (bf16[512,256]{1,0:T(8,128)(2,1)S(1)}, bf16[512,256]{1,0:T(8,128)(2,1)}, u32[]{:S(2)}) copy-start(bf16[512,256]{1,0:T(8,128)(2,1)} %constant.14.clone.xa_ref) | copy-start | bytes 786436
  61.8 0.7 copy-start.9
  62.6 36.3 %copy-start.11 = (bf16[288,128]{1,0:T(8,128)(2,1)S(1)}, bf16[288,128]{1,0:T(8,128)(2,1)}, u32[]{:S(2)}) copy-start(bf16[288,128]{1,0:T(8,128)(2,1)} %copy-done.10) | copy-start | bytes 221188
  62.6 18.2 %all-to-all-start.2 = ((bf16[64,16,128]{2,1,0:T(8,128)(2,1)}), bf16[64,16,128]{2,1,0:T(8,128)(2,1)S(1)}, u32[]{:S(2)}, u32[]{:S(2)}) async-start(bf16[64,16,128]{2,1,0:T(8,128)(2,1)} %copy-done.9), calls=%async_computation.2 | async-start | bytes 524288 | tf_op jit(solution)/shard_map/all_to_all | solution.py:465
  68.7 4.5 %collective-permute-start.2 = (bf16[288,128]{1,0:T(8,128)(2,1)}, bf16[288,128]{1,0:T(8,128)(2,1)S(1)}, u32[]{:S(2)}, u32[]{:S(2)}) collective-permute-start(bf16[288,128]{1,0:T(8,128)(2,1)} %copy-done.10), channel_id=1, source_target_pairs={{0,192},{64,0},{128,64},{192,128},{1,193},{65,1},{129,65},{193,129... | collective-permute-start | bytes 221192 | tf_op jit(solution)/shard_map/ppermute | solution.py:447
  71.5 5.2 %collective-permute-start.1 = (bf16[288,128]{1,0:T(8,128)(2,1)}, bf16[288,128]{1,0:T(8,128)(2,1)S(1)}, u32[]{:S(2)}, u32[]{:S(2)}) collective-permute-start(bf16[288,128]{1,0:T(8,128)(2,1)} %copy-done.10), channel_id=1, source_target_pairs={{0,128},{64,192},{128,0},{192,64},{1,129},{65,193},{129,1},{193,65... | collective-permute-start | bytes 221192 | tf_op jit(solution)/shard_map/ppermute | solution.py:447
  71.9 6.6 %collective-permute-start = (bf16[288,128]{1,0:T(8,128)(2,1)}, bf16[288,128]{1,0:T(8,128)(2,1)S(1)}, u32[]{:S(2)}, u32[]{:S(2)}) collective-permute-start(bf16[288,128]{1,0:T(8,128)(2,1)} %copy-done.10), channel_id=1, source_target_pairs={{0,64},{64,128},{128,192},{192,0},{1,65},{65,129},{129,193},{193,1... | collective-permute-start | bytes 221192 | tf_op jit(solution)/shard_map/ppermute | solution.py:447
  82.8 24.0 %all-to-all-start.3 = ((bf16[64,16,128]{2,1,0:T(8,128)(2,1)}), bf16[64,16,128]{2,1,0:T(8,128)(2,1)S(1)}, u32[]{:S(2)}, u32[]{:S(2)}) async-start(bf16[64,16,128]{2,1,0:T(8,128)(2,1)} %get-tuple-element.24), calls=%async_computation.3 | async-start | bytes 524288 | tf_op jit(solution)/shard_map/all_to_all | solution.py:465
  91.6 3.6 %collective-permute-start.5 = (bf16[288,128]{1,0:T(8,128)(2,1)S(1)}, bf16[288,128]{1,0:T(8,128)(2,1)S(1)}, u32[]{:S(2)}, u32[]{:S(2)}) collective-permute-start(bf16[288,128]{1,0:T(8,128)(2,1)S(1)} %get-tuple-element.29.refs_4_), channel_id=1, source_target_pairs={{0,192},{64,0},{128,64},{192,128},{1,193},{65,1},{129,65},{193,129... | collective-permute-start | bytes 221192 | tf_op jit(solution)/shard_map/ppermute | solution.py:447
  92.0 4.7 %collective-permute-start.4 = (bf16[288,128]{1,0:T(8,128)(2,1)S(1)}, bf16[288,128]{1,0:T(8,128)(2,1)S(1)}, u32[]{:S(2)}, u32[]{:S(2)}) collective-permute-start(bf16[288,128]{1,0:T(8,128)(2,1)S(1)} %get-tuple-element.29.refs_4_), channel_id=1, source_target_pairs={{0,128},{64,192},{128,0},{192,64},{1,129},{65,193},{129,1},{193,65... | collective-permute-start | bytes 221192 | tf_op jit(solution)/shard_map/ppermute | solution.py:447
  92.4 6.4 %collective-permute-start.3 = (bf16[288,128]{1,0:T(8,128)(2,1)S(1)}, bf16[288,128]{1,0:T(8,128)(2,1)S(1)}, u32[]{:S(2)}, u32[]{:S(2)}) collective-permute-start(bf16[288,128]{1,0:T(8,128)(2,1)S(1)} %get-tuple-element.29.refs_4_), channel_id=1, source_target_pairs={{0,64},{64,128},{128,192},{192,0},{1,65},{65,129},{129,193},{193,1... | collective-permute-start | bytes 221192 | tf_op jit(solution)/shard_map/ppermute | solution.py:447
  106.9 2.0 %copy-start.3 = (bf16[64,16,128]{2,1,0:T(8,128)(2,1)}, bf16[64,16,128]{2,1,0:T(8,128)(2,1)S(1)}, u32[]{:S(2)}) copy-start(bf16[64,16,128]{2,1,0:T(8,128)(2,1)S(1)} %all-to-all-done.3.recv_ref) | copy-start | bytes 786436
  107.0 9.1 %collective-permute-start.8 = (f32[24,128]{1,0:T(8,128)S(1)}, f32[24,128]{1,0:T(8,128)S(1)}, u32[]{:S(2)}, u32[]{:S(2)}) collective-permute-start(f32[24,128]{1,0:T(8,128)S(1)} %shard_map.128), channel_id=1, source_target_pairs={{0,192},{64,0},{128,64},{192,128},{1,193},{65,1},{129,65},{193,129... | collective-permute-start | bytes 36872 | tf_op jit(solution)/shard_map/ppermute | solution.py:447
  107.4 8.7 %collective-permute-start.7 = (f32[24,128]{1,0:T(8,128)S(1)}, f32[24,128]{1,0:T(8,128)S(1)}, u32[]{:S(2)}, u32[]{:S(2)}) collective-permute-start(f32[24,128]{1,0:T(8,128)S(1)} %shard_map.128), channel_id=1, source_target_pairs={{0,64},{64,128},{128,192},{192,0},{1,65},{65,129},{129,193},{193,1... | collective-permute-start | bytes 36872 | tf_op jit(solution)/shard_map/ppermute | solution.py:447
  108.4 7.7 %collective-permute-start.6 = (f32[24,128]{1,0:T(8,128)S(1)}, f32[24,128]{1,0:T(8,128)S(1)}, u32[]{:S(2)}, u32[]{:S(2)}) collective-permute-start(f32[24,128]{1,0:T(8,128)S(1)} %shard_map.128), channel_id=1, source_target_pairs={{0,128},{64,192},{128,0},{192,64},{1,129},{65,193},{129,1},{193,65... | collective-permute-start | bytes 36872 | tf_op jit(solution)/shard_map/ppermute | solution.py:447
